TPU v7x, 256 devices: a whole 4x4x8 slice. The times are simulated.
256 devices in a mesh: ctx: 16 (over z, core), tp: 4 (over y), dec: 4 (over x).
Axes of the slice: x: 4, y: 4, z: 8, core: 2. Of those that a mesh axis runs over, the one named last changes fastest.
Arguments:
- x_input: bfloat16 [4, 4096, 16384], P('dec', 'ctx', 'tp'), may hold values from -3 to 3
- b_input: bfloat16 [4, 4096, 2048], P('dec', 'ctx', 'tp'), may hold values from -6 to 6
- output_projection_input: bfloat16 [4, 4096, 2048], P('dec', 'ctx', 'tp'), may hold values from -6 to 6
- step_input: bfloat16 [4, 4096, 256], P('dec', 'ctx', 'tp'), may hold values from -3 to 13
- gate_input: bfloat16 [4, 4096, 16384], P('dec', 'ctx', 'tp'), may hold values from -6 to 6
- kernel_x: bfloat16 [4, 16384], P(None, 'tp'), may hold values from -3 to 3
- kernel_b: bfloat16 [4, 2048], P(None, 'tp'), may hold values from -3 to 3
- kernel_c: bfloat16 [4, 2048], P(None, 'tp'), may hold values from -3 to 3
- step_bias: float32 [256], P('tp'), may hold values from -2 to 1
- fading_logarithm: float32 [256], P('tp'), may hold values from -13 to -2
- norm_gain: float32 [16384], P('tp'), may hold values from 0.25 to 1.75
- owner_map: int32 [4, 256, 1], P('dec', 'tp'), may hold values from 0 to 3; in each aligned block of 4 rows (0 to 3, 4 to 7, ..., all dimensions but the last counted through in order) at most 2 rows name the same one
Outputs:
- mixer_output: bfloat16 [4, 4096, 16384], P('dec', 'ctx', 'tp')
- decode_state: float32 [4, 4, 64, 2, 64, 256], P('dec', None, ('tp', 'ctx'))
Inputs may be any that keep to these rules, and one draw needn't show every extreme that they name: `owner_map`: in every block of 4 heads of one prompt starting at a multiple of 4, at most 2 heads name the same decode device.
All inputs are finite; a program needn't handle non-finite values.
Results may differ from a plain program's by a relative error of at most 0.009.
Values may be sent and summed in bfloat16 or wider, within the bound.
No kernel may reach another device: no remote copies, remote signals or barrier semaphores. Data moves between devices by JAX's collectives and lax.ppermute only.
A program may use at most 192 MiB of HBM per device.

v0:
```python
import jax
import jax.numpy as jnp
from jax import lax
from jax.sharding import PartitionSpec as P

HEAD_DIM = 64
STATE = 256
STRETCH = 256


epsilon = 1e-05


def passed_along(value, axis, steps):
    count = lax.axis_size(axis)
    first, last = (max(0, -steps), min(count, count - steps))
    return lax.ppermute(value, axis, [(source, source + steps) for source in range(first, last)])


def causal_filter(sequence_lines, prior_rows, kernel):
    taps_count = kernel.shape[0]
    length_now = sequence_lines.shape[0]
    padded = jnp.concatenate([prior_rows, sequence_lines], axis=0).astype(jnp.float32)
    running = jnp.zeros(sequence_lines.shape, jnp.float32)
    for offset in range(taps_count):
        running = (
            running + kernel[offset].astype(jnp.float32) * padded[offset : offset + length_now]
        )
    return jax.nn.silu(running).astype(jnp.bfloat16)


def state_blocks(x_conv, b_conv, c_conv, step_size, decay_rate, initial, block_len):
    head_count, head_width, state_width = initial.shape
    count_of_groups = b_conv.shape[1] // state_width
    per_group = head_count // count_of_groups
    block_count = x_conv.shape[0] // block_len
    x_blocks = x_conv.reshape(block_count, block_len, count_of_groups, per_group, head_width)
    b_blocks = b_conv.reshape(block_count, block_len, count_of_groups, state_width)
    c_blocks = c_conv.reshape(block_count, block_len, count_of_groups, state_width)
    s_blocks = step_size.reshape(block_count, block_len, count_of_groups, per_group)
    rate_grid = decay_rate.reshape(count_of_groups, per_group)
    causal = jnp.arange(block_len)[:, None] >= jnp.arange(block_len)[None, :]
    highest = lax.Precision.HIGHEST

    def advance(carried, pieces):
        signal_tile, b_block, c_block, s_block = pieces
        cumulative = jnp.cumsum(s_block * rate_grid, axis=0)
        closing = cumulative[-1]
        scores = jnp.einsum("qgn,sgn->gqs", c_block, b_block, preferred_element_type=jnp.float32)
        gaps = cumulative[:, None] - cumulative[None, :]
        decays = jnp.exp(jnp.where(causal[:, :, None, None], gaps, -jnp.inf))
        decays = jnp.transpose(decays, (2, 3, 0, 1))
        steps_t = jnp.transpose(s_block, (1, 2, 0))[:, :, None, :]
        block_weights = (scores[:, None] * decays * steps_t).astype(jnp.bfloat16)
        intra = jnp.einsum(
            "ghqs,sghp->qghp", block_weights, signal_tile, preferred_element_type=jnp.float32
        )
        inter = (
            jnp.einsum("qgn,ghpn->qghp", c_block.astype(jnp.float32), carried, precision=highest)
            * jnp.exp(cumulative)[:, :, :, None]
        )
        outputs = intra + inter
        block_inputs = (
            signal_tile.astype(jnp.float32)
            * (s_block * jnp.exp(closing[None] - cumulative))[:, :, :, None]
        ).astype(jnp.bfloat16)
        update = jnp.einsum(
            "sghp,sgn->ghpn", block_inputs, b_block, preferred_element_type=jnp.float32
        )
        carried = jnp.exp(closing)[:, :, None, None] * carried + update
        return (carried, outputs)

    start_state = initial.reshape(count_of_groups, per_group, head_width, state_width)
    carried, outputs = lax.scan(advance, start_state, (x_blocks, b_blocks, c_blocks, s_blocks))
    scan_out = outputs.reshape(block_count * block_len, head_count * head_width)
    return (scan_out, carried.reshape(head_count, head_width, state_width))


def gated_norm(scan_out, gate_rows, norm_gain, count_of_groups):
    row_count = scan_out.shape[0]
    gated_rows = scan_out.astype(jnp.float32) * jax.nn.silu(gate_rows.astype(jnp.float32))
    grouped = gated_rows.reshape(row_count, count_of_groups, -1)
    inverse_rms = 1.0 / jnp.sqrt(jnp.mean(grouped * grouped, axis=2, keepdims=True) + epsilon)
    return ((grouped * inverse_rms).reshape(row_count, -1) * norm_gain).astype(jnp.bfloat16)


def slot_table(owners, dest_count, capacity):
    onehot = (owners[:, None] == jnp.arange(dest_count)[None, :]).astype(jnp.int32)
    earlier = jnp.cumsum(onehot, axis=0) - onehot
    slot_rank = jnp.sum(earlier * onehot, axis=1)
    slot_hit = (slot_rank[:, None] == jnp.arange(capacity)[None, :]).astype(jnp.float32)
    return onehot.astype(jnp.float32)[:, :, None] * slot_hit[:, None, :]


def local(
    x_input,
    b_input,
    output_projection_input,
    step_input,
    gate_input,
    kernel_x,
    kernel_b,
    kernel_c,
    step_bias,
    fading_logarithm,
    norm_gain,
    owner_map,
):
    ctx_count = lax.axis_size("ctx")
    ctx_rank = lax.axis_index("ctx")
    dec_count = lax.axis_size("dec")
    x_rows = x_input[0]
    b_rows = b_input[0]
    c_rows = output_projection_input[0]
    token_count = x_rows.shape[0]
    first_tail = token_count - kernel_x.shape[0] + 1
    prior_x, prior_b, preceding_output_projection = passed_along(
        (x_rows[first_tail:], b_rows[first_tail:], c_rows[first_tail:]), "ctx", 1
    )
    x_conv = causal_filter(x_rows, prior_x, kernel_x)
    b_conv = causal_filter(b_rows, prior_b, kernel_b)
    c_conv = causal_filter(c_rows, preceding_output_projection, kernel_c)
    decay_rate = -jnp.exp(fading_logarithm)
    heads_local = fading_logarithm.shape[0]
    group_local = b_rows.shape[1] // STATE
    per_device = heads_local // ctx_count
    capacity = max(2, per_device // 2)
    repeats = ctx_count // group_local
    b_dest = jnp.repeat(b_conv.reshape(token_count, group_local, STATE), repeats, axis=1).reshape(
        token_count, ctx_count * STATE
    )
    c_dest = jnp.repeat(c_conv.reshape(token_count, group_local, STATE), repeats, axis=1).reshape(
        token_count, ctx_count * STATE
    )
    x_heads, b_heads, c_heads, step_heads = (
        lax.all_to_all(x_conv, "ctx", split_axis=1, concat_axis=0, tiled=True),
        lax.all_to_all(b_dest, "ctx", split_axis=1, concat_axis=0, tiled=True),
        lax.all_to_all(c_dest, "ctx", split_axis=1, concat_axis=0, tiled=True),
        lax.all_to_all(step_input[0], "ctx", split_axis=1, concat_axis=0, tiled=True),
    )
    head_start = ctx_rank * per_device
    step_size = jax.nn.softplus(
        step_heads.astype(jnp.float32) + lax.dynamic_slice_in_dim(step_bias, head_start, per_device)
    )
    initial = jnp.zeros((per_device, HEAD_DIM, STATE), jnp.float32)
    rate_heads = lax.dynamic_slice_in_dim(decay_rate, head_start, per_device)
    scan_out, closing_state = state_blocks(
        x_heads, b_heads, c_heads, step_size, rate_heads, initial, STRETCH
    )
    scan_rows = lax.all_to_all(
        scan_out.astype(jnp.bfloat16), "ctx", split_axis=0, concat_axis=1, tiled=True
    )
    mixer_rows = gated_norm(scan_rows, gate_input[0], norm_gain, group_local)
    owners = lax.dynamic_slice_in_dim(owner_map[0, :, 0], ctx_rank * per_device, per_device)
    table = slot_table(owners, dec_count, capacity)
    outgoing = jnp.einsum("jer,jpn->erpn", table, closing_state, precision=lax.Precision.HIGHEST)
    arrived = lax.all_to_all(outgoing, "dec", split_axis=0, concat_axis=0, tiled=True)
    return (mixer_rows[None], arrived[None, :, None])


def solution(mesh):
    return jax.shard_map(
        local,
        mesh=mesh,
        in_specs=(
            P("dec", "ctx", "tp"),
            P("dec", "ctx", "tp"),
            P("dec", "ctx", "tp"),
            P("dec", "ctx", "tp"),
            P("dec", "ctx", "tp"),
            P(None, "tp"),
            P(None, "tp"),
            P(None, "tp"),
            P("tp"),
            P("tp"),
            P("tp"),
            P("dec", "tp", None),
        ),
        out_specs=(P("dec", "ctx", "tp"), P("dec", None, ("tp", "ctx"), None, None, None)),
        check_vma=False,
    )
```

profile of v0, /device:TPU:1, one launch (start us, length us, event | category | flops | bytes accessed | tf_op | source)
XLA Modules:
  0.0 399.4 jit_solution(3460179320594119131)
XLA Ops:
  1.4 4.9 %collective-permute-start.1 = (bf16[3,512]{1,0:T(4,128)(2,1)S(1)}, bf16[3,512]{1,0:T(4,128)(2,1)S(1)}, u32[]{:S(2)}, u32[]{:S(2)}) collective-permute-start(bf16[3,512]{1,0:T(4,128)(2,1)S(1)} %slice_bitcast_fusion.4), channel_id=1, source_target_pairs={{0,16},{16,32},{32,48},{48,64},{64,80},{80,96},{96,112},{112,128},... | collective-permute-start | bytes 9224 | tf_op jit(solution)/shard_map/ppermute | solution.py:17
  6.3 1.4 all_to_all.57
  7.7 7.7 %all-to-all-start = ((bf16[256,16,4]{0,2,1:T(4,128)(2,1)}), bf16[256,16,4]{0,2,1:T(4,128)(2,1)S(1)}, u32[]{:S(2)}, u32[]{:S(2)}) async-start(bf16[256,16,4]{0,2,1:T(4,128)(2,1)} %all_to_all.57), calls=%async_computation | async-start | bytes 65536 | tf_op jit(solution)/shard_map/all_to_all | solution.py:139
  17.6 5.1 %all-to-all-done = bf16[256,16,4]{0,2,1:T(4,128)(2,1)S(1)} async-done(((bf16[256,16,4]{0,2,1:T(4,128)(2,1)}), bf16[256,16,4]{0,2,1:T(4,128)(2,1)S(1)}, u32[]{:S(2)}, u32[]{:S(2)}) %all-to-all-start) | async-done | bytes 32800 | tf_op jit(solution)/shard_map/all_to_all | solution.py:139
  22.8 1.5 broadcast_in_dim.20
  24.3 3.9 all-to-all-start.2
  28.2 3.5 collective-permute-start.2
  31.8 41.5 %collective-permute-done.2 = bf16[3,512]{1,0:T(4,128)(2,1)S(1)} collective-permute-done((bf16[3,512]{1,0:T(4,128)(2,1)S(1)}, bf16[3,512]{1,0:T(4,128)(2,1)S(1)}, u32[]{:S(2)}, u32[]{:S(2)}) %collective-permute-start.2) | collective-permute-done | bytes 3104 | tf_op jit(solution)/shard_map/ppermute | solution.py:17
  73.8 3.4 all-to-all-done.2
  77.2 1.7 broadcast_in_dim.21
  78.8 5.5 %all-to-all-start.3 = ((bf16[256,16,256]{2,0,1:T(8,128)(2,1)}), bf16[256,16,256]{2,0,1:T(8,128)(2,1)}, u32[]{:S(2)}, u32[]{:S(2)}) async-start(bf16[256,16,256]{2,0,1:T(8,128)(2,1)} %bitcast.26), calls=%async_computation.3 | async-start | bytes 4194304 | tf_op jit(solution)/shard_map/all_to_all | solution.py:138
  85.2 3.5 collective-permute-start
  88.8 41.5 %collective-permute-done = bf16[3,4096]{1,0:T(4,128)(2,1)S(1)} collective-permute-done((bf16[3,4096]{1,0:T(4,128)(2,1)S(1)}, bf16[3,4096]{1,0:T(4,128)(2,1)S(1)}, u32[]{:S(2)}, u32[]{:S(2)}) %collective-permute-start) | collective-permute-done | bytes 24608 | tf_op jit(solution)/shard_map/ppermute | solution.py:17
  130.3 2.2 maximum_convert_fusion
  132.5 2.6 multiply_convert_fusion.1
  135.1 2.5 copy.85
  137.6 8.3 %all-to-all-start.1 = ((bf16[256,16,256]{0,2,1:T(8,128)(2,1)}), bf16[256,16,256]{0,2,1:T(8,128)(2,1)S(1)}, u32[]{:S(2)}, u32[]{:S(2)}) async-start(bf16[256,16,256]{0,2,1:T(8,128)(2,1)} %bitcast.254), calls=%async_computation.1 | async-start | bytes 4194304 | tf_op jit(solution)/shard_map/all_to_all | solution.py:136
  146.6 48.3 %all-to-all-done.1 = bf16[256,16,256]{0,2,1:T(8,128)(2,1)S(1)} async-done(((bf16[256,16,256]{0,2,1:T(8,128)(2,1)}), bf16[256,16,256]{0,2,1:T(8,128)(2,1)S(1)}, u32[]{:S(2)}, u32[]{:S(2)}) %all-to-all-start.1) | async-done | bytes 2097184 | tf_op jit(solution)/shard_map/all_to_all | solution.py:136
  194.9 119.3 %while.13 = (s32[]{:T(128)}, f32[1,4,64,256]{3,2,1,0:T(8,128)S(1)}, bf16[16,256,1,4,64]{1,4,3,2,0:T(8,128)(2,1)}, f32[16,256,1,4]{1,3,0,2:T(4,128)S(1)}, f32[4]{...) while((s32[]{:T(128)}, f32[1,4,64,256]{3,2,1,0:T(8,128)S(1)}, ...), condition=%wide.region_3.4_spmd.clone, body=%wide.region_0.3_spmd.clone.sunk | while | flops 304090112 | bytes 3153944 | solution.py:74
  195.2 1.2 reduce-window.14
  199.0 1.9 fusion.93
  202.6 1.2 reduce-window.14
  206.4 1.9 fusion.93
  210.1 1.2 reduce-window.14
  213.9 1.9 fusion.93
  217.6 1.2 reduce-window.14
  221.4 1.9 fusion.93
  225.0 1.2 reduce-window.14
  228.8 1.9 fusion.93
  232.5 1.2 reduce-window.14
  236.3 1.9 fusion.93
  239.9 1.2 reduce-window.14
  243.7 1.9 fusion.93
  247.4 1.2 reduce-window.14
  251.2 1.9 fusion.93
  254.9 1.2 reduce-window.14
  258.6 1.9 fusion.93
  262.3 1.2 reduce-window.14
  266.1 1.9 fusion.93
  269.8 1.2 reduce-window.14
  271.7 1.2 fusion.92
  273.6 1.9 fusion.93
  277.2 1.2 reduce-window.14
  279.1 1.2 fusion.92
  281.0 1.9 fusion.93
  284.7 1.2 reduce-window.14
  288.5 1.9 fusion.93
  292.1 1.2 reduce-window.14
  295.9 1.9 fusion.93
  299.6 1.2 reduce-window.14
  303.4 1.9 fusion.93
  307.1 1.2 reduce-window.14
  310.9 1.9 fusion.93
  315.9 4.0 %all-to-all-start.5 = ((f32[4,2,64,256]{3,2,1,0:T(8,128)}), f32[4,2,64,256]{3,2,1,0:T(8,128)S(1)}, u32[]{:S(2)}, u32[]{:S(2)}) async-start(f32[4,2,64,256]{3,2,1,0:T(8,128)} %copy.81), calls=%async_computation.5 | async-start | bytes 1048576 | tf_op jit(solution)/shard_map/all_to_all | solution.py:157
  320.0 2.4 copy.75
  322.3 6.6 %all-to-all-done.5 = f32[4,2,64,256]{3,2,1,0:T(8,128)S(1)} async-done(((f32[4,2,64,256]{3,2,1,0:T(8,128)}), f32[4,2,64,256]{3,2,1,0:T(8,128)S(1)}, u32[]{:S(2)}, u32[]{:S(2)}) %all-to-all-start.5) | async-done | bytes 524320 | tf_op jit(solution)/shard_map/all_to_all | solution.py:157
  328.9 6.0 %all-to-all-start.4 = ((bf16[16,256,256]{2,1,0:T(8,128)(2,1)}), bf16[16,256,256]{2,1,0:T(8,128)(2,1)}, u32[]{:S(2)}, u32[]{:S(2)}) async-start(bf16[16,256,256]{2,1,0:T(8,128)(2,1)} %copy.75), calls=%async_computation.4 | async-start | bytes 4194304 | tf_op jit(solution)/shard_map/all_to_all | solution.py:150
  335.0 3.3 copy.77
  338.2 45.8 %all-to-all-done.4 = bf16[16,256,256]{2,1,0:T(8,128)(2,1)} async-done(((bf16[16,256,256]{2,1,0:T(8,128)(2,1)}), bf16[16,256,256]{2,1,0:T(8,128)(2,1)}, u32[]{:S(2)}, u32[]{:S(2)}) %all-to-all-start.4) | async-done | bytes 2097184 | tf_op jit(solution)/shard_map/all_to_all | solution.py:150
  384.0 3.9 copy.76
  387.9 2.2 convert_element_type.157
  390.1 1.9 fusion.49
  392.1 2.5 fusion.47
  394.6 4.1 %copy.82 = bf16[1,256,4096]{2,1,0:T(8,128)(2,1)} copy(bf16[1,256,4096]{1,2,0:T(8,128)(2,1)} %fusion.47) | data formatting | bytes 4194304
  (400 shorter events, 72.7 us)
Async XLA Ops:
  0.6 145.5 %copy-start = (s32[1,64,1]{1,2,0:T(1,128)S(1)}, s32[1,64,1]{1,2,0:T(1,128)}, u32[]{:S(2)}) copy-start(s32[1,64,1]{1,2,0:T(1,128)} %param.25) | copy-start | bytes 772
  1.4 14.9 %collective-permute-start.1 = (bf16[3,512]{1,0:T(4,128)(2,1)S(1)}, bf16[3,512]{1,0:T(4,128)(2,1)S(1)}, u32[]{:S(2)}, u32[]{:S(2)}) collective-permute-start(bf16[3,512]{1,0:T(4,128)(2,1)S(1)} %slice_bitcast_fusion.4), channel_id=1, source_target_pairs={{0,16},{16,32},{32,48},{48,64},{64,80},{80,96},{96,112},{112,128},... | collective-permute-start | bytes 9224 | tf_op jit(solution)/shard_map/ppermute | solution.py:17
  7.7 15.1 %all-to-all-start = ((bf16[256,16,4]{0,2,1:T(4,128)(2,1)}), bf16[256,16,4]{0,2,1:T(4,128)(2,1)S(1)}, u32[]{:S(2)}, u32[]{:S(2)}) async-start(bf16[256,16,4]{0,2,1:T(4,128)(2,1)} %all_to_all.57), calls=%async_computation | async-start | bytes 65536 | tf_op jit(solution)/shard_map/all_to_all | solution.py:139
  17.3 10.9 %copy-start.4 = (bf16[1,256,512]{2,1,0:T(8,128)(2,1)S(1)}, bf16[1,256,512]{2,1,0:T(8,128)(2,1)}, u32[]{:S(2)}) copy-start(bf16[1,256,512]{2,1,0:T(8,128)(2,1)} %param.16) | copy-start | bytes 786436
  17.3 14.5 %copy-start.7 = (bf16[4,512]{1,0:T(4,128)(2,1)S(1)}, bf16[4,512]{1,0:T(4,128)(2,1)}, u32[]{:S(2)}) copy-start(bf16[4,512]{1,0:T(4,128)(2,1)} %param.21) | copy-start | bytes 12292
  24.3 52.9 %all-to-all-start.2 = ((bf16[256,16,256]{2,0,1:T(8,128)(2,1)}), bf16[256,16,256]{2,0,1:T(8,128)(2,1)S(1)}, u32[]{:S(2)}, u32[]{:S(2)}) async-start(bf16[256,16,256]{2,0,1:T(8,128)(2,1)} %bitcast.17), calls=%async_computation.2 | async-start | bytes 4194304 | tf_op jit(solution)/shard_map/all_to_all | solution.py:137
  28.2 45.1 %collective-permute-start.2 = (bf16[3,512]{1,0:T(4,128)(2,1)S(1)}, bf16[3,512]{1,0:T(4,128)(2,1)S(1)}, u32[]{:S(2)}, u32[]{:S(2)}) collective-permute-start(bf16[3,512]{1,0:T(4,128)(2,1)S(1)} %slice_bitcast_fusion.3), channel_id=1, source_target_pairs={{0,16},{16,32},{32,48},{48,64},{64,80},{80,96},{96,112},{112,128},... | collective-permute-start | bytes 9224 | tf_op jit(solution)/shard_map/ppermute | solution.py:17
  73.4 15.4 %copy-start.5 = (bf16[4,4096]{1,0:T(4,128)(2,1)S(1)}, bf16[4,4096]{1,0:T(4,128)(2,1)}, u32[]{:S(2)}) copy-start(bf16[4,4096]{1,0:T(4,128)(2,1)} %param.19) | copy-start | bytes 98308
  77.2 55.3 %copy-start.2 = (bf16[256,16,256]{2,0,1:T(8,128)(2,1)}, bf16[256,16,256]{2,0,1:T(8,128)(2,1)S(1)}, u32[]{:S(2)}) copy-start(bf16[256,16,256]{2,0,1:T(8,128)(2,1)S(1)} %all-to-all-done.2) | copy-start | bytes 6291460
  78.8 58.7 %all-to-all-start.3 = ((bf16[256,16,256]{2,0,1:T(8,128)(2,1)}), bf16[256,16,256]{2,0,1:T(8,128)(2,1)}, u32[]{:S(2)}, u32[]{:S(2)}) async-start(bf16[256,16,256]{2,0,1:T(8,128)(2,1)} %bitcast.26), calls=%async_computation.3 | async-start | bytes 4194304 | tf_op jit(solution)/shard_map/all_to_all | solution.py:138
  85.2 45.1 %collective-permute-start = (bf16[3,4096]{1,0:T(4,128)(2,1)S(1)}, bf16[3,4096]{1,0:T(4,128)(2,1)S(1)}, u32[]{:S(2)}, u32[]{:S(2)}) collective-permute-start(bf16[3,4096]{1,0:T(4,128)(2,1)S(1)} %slice_bitcast_fusion.2), channel_id=1, source_target_pairs={{0,16},{16,32},{32,48},{48,64},{64,80},{80,96},{96,112},{112,128},... | collective-permute-start | bytes 73736 | tf_op jit(solution)/shard_map/ppermute | solution.py:17
  135.1 10.8 %copy-start.8 = (f32[64]{0:T(128)S(1)}, f32[64]{0:T(128)}, u32[]{:S(2)}) copy-start(f32[64]{0:T(128)} %param.22) | copy-start | bytes 772
  135.1 10.9 %copy-start.9 = (f32[64]{0:T(128)S(1)}, f32[64]{0:T(128)}, u32[]{:S(2)}) copy-start(f32[64]{0:T(128)} %param.23) | copy-start | bytes 772
  137.6 57.3 %all-to-all-start.1 = ((bf16[256,16,256]{0,2,1:T(8,128)(2,1)}), bf16[256,16,256]{0,2,1:T(8,128)(2,1)S(1)}, u32[]{:S(2)}, u32[]{:S(2)}) async-start(bf16[256,16,256]{0,2,1:T(8,128)(2,1)} %bitcast.254), calls=%async_computation.1 | async-start | bytes 4194304 | tf_op jit(solution)/shard_map/all_to_all | solution.py:136
  314.2 5.8 %copy-start.3 = (bf16[16,256,1,4,64]{1,4,3,2,0:T(8,128)(2,1)S(1)}, bf16[16,256,1,4,64]{1,4,3,2,0:T(8,128)(2,1)}, u32[]{:S(2)}) copy-start(bf16[16,256,1,4,64]{1,4,3,2,0:T(8,128)(2,1)} %get-tuple-element.50) | copy-start | bytes 6291460
  315.9 13.0 %all-to-all-start.5 = ((f32[4,2,64,256]{3,2,1,0:T(8,128)}), f32[4,2,64,256]{3,2,1,0:T(8,128)S(1)}, u32[]{:S(2)}, u32[]{:S(2)}) async-start(f32[4,2,64,256]{3,2,1,0:T(8,128)} %copy.81), calls=%async_computation.5 | async-start | bytes 1048576 | tf_op jit(solution)/shard_map/all_to_all | solution.py:157
  328.9 55.1 %all-to-all-start.4 = ((bf16[16,256,256]{2,1,0:T(8,128)(2,1)}), bf16[16,256,256]{2,1,0:T(8,128)(2,1)}, u32[]{:S(2)}, u32[]{:S(2)}) async-start(bf16[16,256,256]{2,1,0:T(8,128)(2,1)} %copy.75), calls=%async_computation.4 | async-start | bytes 4194304 | tf_op jit(solution)/shard_map/all_to_all | solution.py:150
  387.9 2.2 copy-start.1
  387.9 4.1 %copy-start.6 = (f32[4096]{0:T(1024)S(1)}, f32[4096]{0:T(1024)}, u32[]{:S(2)}) copy-start(f32[4096]{0:T(1024)} %param.24) | copy-start | bytes 49156
where the time goes:
time: 401 us; the launch traced here: 399 us
  waiting for transfers between devices  192 us (48%)
  matrix products  76.2 us (19%)
  starting transfers between devices  47.5 us (12%)
  other arithmetic  43.2 us (11%)
  local copies, waits for them, and re-layouts  37.8 us (9%)
    ppermute x3, waiting for transfers between devices, passed_along(): lax.ppermute(value, axis, [(source, source + steps) for source in range(f...  83 us
    all_to_all x1, waiting for transfers between devices, local(): lax.all_to_all(x_conv, 'ctx', split_axis=1, concat_axis=0, tiled=True)  48.3 us
    all_to_all x1, waiting for transfers between devices, local(): lax.all_to_all(scan_out.astype(jnp.bfloat16), 'ctx', split_axis=0, concat...  45.8 us
    dot_general x16, matrix products, advance(): jnp.einsum('qgn,ghpn->qghp', c_block.astype(jnp.float32), carried, precis...  30.7 us
    another operation x32, other arithmetic  20 us
    dot_general x16, matrix products, advance(): jnp.einsum('qgn,sgn->gqs', c_block, b_block, preferred_element_type=jnp.f...  19.1 us
    dot_general x16, matrix products, advance(): jnp.einsum('sghp,sgn->ghpn', block_inputs, b_block, preferred_element_typ...  17.9 us
    ppermute x3, starting transfers between devices, passed_along(): lax.ppermute(value, axis, [(source, source + steps) for source in range(f...  12 us
  transfers between devices with their start and end apart: 9, of which 7 were waited for; matrix products, arithmetic and copies ran while one was open for 4% of the time, Pallas kernels for 0%

commit v1 on v0

v1 whole, which is shorter than its diff:
```python
import functools

import jax
import jax.numpy as jnp
from jax import lax
from jax.experimental import pallas as pl
from jax.experimental.pallas import tpu as pltpu
from jax.sharding import PartitionSpec as P

HEAD_DIM = 64
STATE = 256
BLOCK = 256
HB = 4
WIDE = HB * HEAD_DIM
LOG2E = 1.4426950408889634
VMEM = 56 * 1024 * 1024

epsilon = 1e-05
F32 = jnp.float32
BF16 = jnp.bfloat16
HIGHEST = lax.Precision.HIGHEST


def split3(value):
    high = value.astype(BF16)
    rest = value - high.astype(F32)
    middle = rest.astype(BF16)
    low = (rest - middle.astype(F32)).astype(BF16)
    return high, middle, low


def softplus(value):
    return jnp.maximum(value, 0.0) + jnp.log1p(jnp.exp(-jnp.abs(value)))


def silu_of_twice(half):
    return half + half * jnp.tanh(half)


def spread(rows, width, first_head, heads):
    row = lax.broadcasted_iota(jnp.int32, (rows, width), 0)
    channel = lax.broadcasted_iota(jnp.int32, (rows, width), 1)
    head = row % heads
    return (head == first_head + channel // HEAD_DIM).astype(BF16)


def conv(pad_ref, prior, rows, taps):
    count = rows.shape[0]
    pad_ref[0:8, :] = prior
    pad_ref[8 : 8 + count, :] = rows
    taps = taps.astype(F32) * 0.5
    running = taps[0:1] * pad_ref[5 : 5 + count, :]
    for j in range(1, 4):
        running = running + taps[j : j + 1] * pad_ref[5 + j : 5 + j + count, :]
    return silu_of_twice(running).astype(BF16)


def steps_of(step, bias, fading):
    size = softplus(step.astype(F32) + bias)
    decay = -size * jnp.exp(fading)
    count = step.shape[0]
    row = lax.broadcasted_iota(jnp.int32, (count, count), 0)
    col = lax.broadcasted_iota(jnp.int32, (count, count), 1)
    lower = (row >= col).astype(BF16)
    pieces = jnp.concatenate(split3(decay), axis=1)
    sums = jnp.dot(lower, pieces, preferred_element_type=F32)
    heads = step.shape[1]
    cumulative = sums[:, :heads] + sums[:, heads : 2 * heads] + sums[:, 2 * heads :]
    return size, cumulative


def tail_kernel(x_ref, b_ref, c_ref, out_ref):
    at = 0
    for ref in (x_ref, b_ref, c_ref):
        out_ref[:, at : at + ref.shape[1]] = ref[...]
        at += ref.shape[1]


def tail_rows(x, b, c):
    end = x.shape[0] // 16 - 1
    width = x.shape[1] + b.shape[1] + c.shape[1]
    return pl.pallas_call(
        tail_kernel,
        grid=(1,),
        in_specs=[pl.BlockSpec((16, v.shape[1]), lambda i: (end, 0)) for v in (x, b, c)],
        out_specs=pl.BlockSpec((16, width), lambda i: (0, 0)),
        out_shape=jax.ShapeDtypeStruct((16, width), BF16),
        compiler_params=pltpu.CompilerParams(vmem_limit_bytes=VMEM),
        name="tail_rows",
    )(x, b, c)


def update_kernel(
    core_ref, xo_ref, xr_ref, bo_ref, br_ref, so_ref, sr_ref, hx_ref, hb_ref, kx_ref, kb_ref,
    bias_ref, fading_ref, u_ref, first_ref, decay_ref, pad, bo_t, br_t, w_own, w_recv, closing,
):
    i = pl.program_id(0)
    core = core_ref[0]
    heads = so_ref.shape[1]
    even = core == 0

    @pl.when(i == 0)
    def _():
        for step_ref, w_ref, at in ((so_ref, w_own, 0), (sr_ref, w_recv, 1)):
            size, cumulative = steps_of(step_ref[...], bias_ref[...], fading_ref[...])
            last = cumulative[BLOCK - 1 : BLOCK]
            weight = size * jnp.exp(last - cumulative)
            high, middle, _ = split3(weight)
            w_ref[...] = jnp.concatenate([high, middle], axis=1)
            closing[at : at + 1, :] = last

    def pair(own_ref, recv_ref, halo_ref):
        own = own_ref[...].astype(F32)
        recv = recv_ref[...].astype(F32)
        halo = halo_ref[...].astype(F32)[8:]
        prior_own = jnp.where(even, halo, recv[BLOCK - 8 :])
        prior_recv = jnp.where(even, own[BLOCK - 8 :], halo)
        return own, prior_own, recv, prior_recv

    @pl.when(i % 4 == 0)
    def _():
        own, prior_own, recv, prior_recv = pair(bo_ref, br_ref, hb_ref)
        bo_t[...] = conv(pad, prior_own, own, kb_ref[...]).astype(F32).T.astype(BF16)
        br_t[...] = conv(pad, prior_recv, recv, kb_ref[...]).astype(F32).T.astype(BF16)

    first_head = (2 * i + core) * HB
    select = spread(2 * heads, WIDE, first_head, heads)
    own, prior_own, recv, prior_recv = pair(xo_ref, xr_ref, hx_ref)

    def update(rows, prior, w_ref, b_t):
        x_conv = conv(pad, prior, rows, kx_ref[...]).astype(F32)
        weight = jnp.dot(w_ref[...], select, preferred_element_type=F32)
        return jnp.dot(b_t[...], (x_conv * weight).astype(BF16), preferred_element_type=F32)

    u_own = update(own, prior_own, w_own, bo_t)
    u_recv = update(recv, prior_recv, w_recv, br_t)
    last_own = closing[0:1, :]
    last_recv = closing[1:2, :]
    row = lax.broadcasted_iota(jnp.int32, (8, heads), 0)
    logs = jnp.where(row == 0, last_own, jnp.where(row == 1, last_recv, last_own + last_recv))
    pieces = jnp.concatenate(split3(jnp.exp(logs)), axis=1)
    decays = jnp.dot(pieces, spread(3 * heads, WIDE, first_head, heads), preferred_element_type=F32)
    own_factor = jnp.where(even, decays[1:2], 1.0)
    recv_factor = jnp.where(even, 1.0, decays[0:1])
    u_ref[0, 0:STATE, :] = (u_own * own_factor + u_recv * recv_factor).astype(BF16)
    high, middle, low = split3(decays[2:3])
    row = lax.broadcasted_iota(jnp.int32, (16, WIDE), 0)
    u_ref[0, STATE : STATE + 16, :] = jnp.where(
        row == 0,
        high.astype(F32),
        jnp.where(row == 1, middle.astype(F32), jnp.where(row == 2, low.astype(F32), 0.0)),
    ).astype(BF16)
    first_ref[0] = jnp.where(even, u_own, u_recv).astype(BF16)
    decay_ref[0] = jnp.broadcast_to(jnp.where(even, decays[0:1], decays[1:2]), (8, WIDE))


def block_updates(core, x, x_recv, b, b_recv, step, step_recv, halo, kernel_x, kernel_b, bias, fading):
    heads = step.shape[1]
    blocks = x_recv.shape[1] // WIDE // 2
    group_at = x.shape[1] // WIDE
    full = lambda i, c: (0, 0)
    own = lambda i, c: (0, 2 * i + c[0])
    group = lambda i, c: (0, i // 4)
    return pl.pallas_call(
        update_kernel,
        grid_spec=pltpu.PrefetchScalarGridSpec(
            num_scalar_prefetch=1,
            grid=(blocks,),
            in_specs=[
                pl.BlockSpec((BLOCK, WIDE), own),
                pl.BlockSpec((BLOCK, WIDE), own),
                pl.BlockSpec((BLOCK, STATE), group),
                pl.BlockSpec((BLOCK, STATE), group),
                pl.BlockSpec((BLOCK, heads), full),
                pl.BlockSpec((BLOCK, heads), full),
                pl.BlockSpec((16, WIDE), own),
                pl.BlockSpec((16, STATE), lambda i, c: (0, group_at + i // 4)),
                pl.BlockSpec((4, WIDE), own),
                pl.BlockSpec((4, STATE), group),
                pl.BlockSpec((1, heads), full),
                pl.BlockSpec((1, heads), full),
            ],
            out_specs=[
                pl.BlockSpec((1, STATE + 16, WIDE), lambda i, c: (i, 0, 0)),
                pl.BlockSpec((1, STATE, WIDE), lambda i, c: (i, 0, 0)),
                pl.BlockSpec((1, 8, WIDE), lambda i, c: (i, 0, 0)),
            ],
            scratch_shapes=[
                pltpu.VMEM((BLOCK + 8, WIDE), F32),
                pltpu.VMEM((STATE, BLOCK), BF16),
                pltpu.VMEM((STATE, BLOCK), BF16),
                pltpu.VMEM((BLOCK, 2 * heads), BF16),
                pltpu.VMEM((BLOCK, 2 * heads), BF16),
                pltpu.VMEM((8, heads), F32),
            ],
        ),
        out_shape=[
            jax.ShapeDtypeStruct((blocks, STATE + 16, WIDE), BF16),
            jax.ShapeDtypeStruct((blocks, STATE, WIDE), BF16),
            jax.ShapeDtypeStruct((blocks, 8, WIDE), F32),
        ],
        compiler_params=pltpu.CompilerParams(vmem_limit_bytes=VMEM),
        cost_estimate=pl.CostEstimate(flops=600_000_000, bytes_accessed=6_000_000, transcendentals=1_200_000),
        name="block_updates",
    )(core, x, x_recv, b, b_recv, step, step_recv, halo, halo, kernel_x, kernel_b, bias, fading)


def within_kernel(
    core_ref, x_ref, gate_ref, b_ref, c_ref, step_ref, hx_ref, hb_ref, hc_ref, tx_ref, tb_ref, tc_ref,
    kx_ref, kb_ref, kc_ref, bias_ref, fading_ref, a_ref, g_ref, cc_ref, pad, pieces, cum_t, scores, cross, x_step,
):
    k = pl.program_id(0)
    even = core_ref[0] == 0

    def filtered(rows_ref, halo_ref, tail_ref, taps_ref):
        prior = jnp.where(even, halo_ref[...].astype(F32), tail_ref[...].astype(F32))[8:]
        return conv(pad, prior, rows_ref[...].astype(F32), taps_ref[...])

    heads = step_ref.shape[1]
    half = BLOCK // 2

    @pl.when(k == 0)
    def _():
        size, cumulative = steps_of(step_ref[...], bias_ref[...], fading_ref[...])
        cumulative = cumulative * LOG2E
        pieces[0] = jnp.concatenate(split3(cumulative), axis=1)
        pieces[1] = jnp.concatenate(split3(size), axis=1)
        turned = cumulative.T
        for n in range(heads // HB):
            cum_t[n, 0:HB, :] = turned[n * HB : (n + 1) * HB]

    @pl.when(k % 8 == 0)
    def _():
        b_conv = filtered(b_ref, hb_ref, tb_ref, kb_ref)
        c_conv = filtered(c_ref, hc_ref, tc_ref, kc_ref)
        cc_ref[...] = c_conv
        products = lax.dot_general(
            c_conv, b_conv, (((1,), (1,)), ((), ())), preferred_element_type=F32
        )
        row = lax.broadcasted_iota(jnp.int32, (half, half), 0)
        col = lax.broadcasted_iota(jnp.int32, (half, half), 1)
        for a in range(2):
            at = slice(a * half, (a + 1) * half)
            scores[at, :] = jnp.where(row >= col, products[at, at], 0.0)
        cross[...] = products[half:, :half].astype(BF16)

    select = spread(3 * heads, WIDE, k * HB, heads)
    cum_wide = jnp.dot(pieces[0], select, preferred_element_type=F32)
    step_wide = jnp.dot(pieces[1], select, preferred_element_type=F32)
    x_conv = filtered(x_ref, hx_ref, tx_ref, kx_ref).astype(F32)
    stepped = x_conv * step_wide
    x_step[...] = stepped.astype(BF16)
    lines = cum_t[k]
    middle = cum_wide[half - 1 : half]
    scaled = (stepped[:half] * jnp.exp2(middle - cum_wide[:half])).astype(BF16)
    late = jnp.dot(cross[...], scaled, preferred_element_type=F32)
    late = late * jnp.exp2(cum_wide[half:] - middle)
    gate = silu_of_twice(gate_ref[...].astype(F32) * 0.5)
    g_ref[...] = (jnp.exp2(cum_wide) * gate).astype(BF16)
    for a in range(2):
        at = slice(a * half, (a + 1) * half)
        parts = []
        for j in range(HB):
            column = cum_wide[at, j * HEAD_DIM : j * HEAD_DIM + 1]
            line = lines[j : j + 1, at]
            weights = scores[at, :] * jnp.exp2(jnp.minimum(column - line, 0.0))
            parts.append(
                jnp.dot(
                    weights.astype(BF16),
                    x_step[at, j * HEAD_DIM : (j + 1) * HEAD_DIM],
                    preferred_element_type=F32,
                )
            )
        inside = jnp.concatenate(parts, axis=1)
        if a == 1:
            inside = inside + late
        a_ref[at, :] = (inside * gate[at]).astype(BF16)


def within_block(core, x, gate, b, c, step, halo, x_recv, b_recv, c_recv, kernel_x, kernel_b, kernel_c, bias, fading):
    heads = step.shape[1]
    blocks = x.shape[1] // WIDE
    groups = b.shape[1] // STATE
    per_group = blocks // groups
    end = BLOCK // 16 - 1
    full = lambda k, s: (0, 0)
    group = lambda k, s: (0, k // per_group)
    one = lambda k, s: (0, k)
    return pl.pallas_call(
        within_kernel,
        grid_spec=pltpu.PrefetchScalarGridSpec(
            num_scalar_prefetch=1,
            grid=(blocks,),
            in_specs=[
                pl.BlockSpec((BLOCK, WIDE), one),
                pl.BlockSpec((BLOCK, WIDE), one),
                pl.BlockSpec((BLOCK, STATE), group),
                pl.BlockSpec((BLOCK, STATE), group),
                pl.BlockSpec((BLOCK, heads), full),
                pl.BlockSpec((16, WIDE), one),
                pl.BlockSpec((16, STATE), lambda k, s: (0, blocks + k // per_group)),
                pl.BlockSpec((16, STATE), lambda k, s: (0, blocks + groups + k // per_group)),
                pl.BlockSpec((16, WIDE), lambda k, s: (end, k)),
                pl.BlockSpec((16, STATE), lambda k, s: (end, k // per_group)),
                pl.BlockSpec((16, STATE), lambda k, s: (end, k // per_group)),
                pl.BlockSpec((4, WIDE), one),
                pl.BlockSpec((4, STATE), group),
                pl.BlockSpec((4, STATE), group),
                pl.BlockSpec((1, heads), full),
                pl.BlockSpec((1, heads), full),
            ],
            out_specs=[
                pl.BlockSpec((BLOCK, WIDE), one),
                pl.BlockSpec((BLOCK, WIDE), one),
                pl.BlockSpec((BLOCK, STATE), group),
            ],
            scratch_shapes=[
                pltpu.VMEM((BLOCK + 8, WIDE), F32),
                pltpu.VMEM((2, BLOCK, 3 * heads), BF16),
                pltpu.VMEM((heads // HB, 8, BLOCK), F32),
                pltpu.VMEM((BLOCK, BLOCK // 2), F32),
                pltpu.VMEM((BLOCK // 2, BLOCK // 2), BF16),
                pltpu.VMEM((BLOCK, WIDE), BF16),
            ],
        ),
        out_shape=[
            jax.ShapeDtypeStruct(x.shape, BF16),
            jax.ShapeDtypeStruct(x.shape, BF16),
            jax.ShapeDtypeStruct(c.shape, BF16),
        ],
        compiler_params=pltpu.CompilerParams(vmem_limit_bytes=VMEM),
        cost_estimate=pl.CostEstimate(flops=8_000_000_000, bytes_accessed=12_000_000, transcendentals=6_000_000),
        name="within_block",
    )(
        core, x, gate, b, c, step, halo, halo, halo, x_recv, b_recv, c_recv, kernel_x, kernel_b, kernel_c,
        bias, fading,
    )


def scan_kernel(gathered_ref, decay_ref, _, starts_ref, final_ref):
    state = jnp.zeros(final_ref.shape, F32)
    for n in range(gathered_ref.shape[0]):
        starts_ref[n] = state.astype(BF16)
        decay = jnp.sum(decay_ref[n].astype(F32), axis=0, keepdims=True)
        state = state * decay + gathered_ref[n].astype(F32)
    final_ref[...] = state


def scan_states(gathered, after):
    chips = gathered.shape[0]
    rows = STATE // 4
    return pl.pallas_call(
        scan_kernel,
        grid=(4,),
        in_specs=[
            pl.BlockSpec((chips, rows, WIDE), lambda r: (0, r, 0)),
            pl.BlockSpec((chips, 16, WIDE), lambda r: (0, STATE // 16, 0)),
            pl.BlockSpec(memory_space=pl.ANY),
        ],
        out_specs=[
            pl.BlockSpec((chips, rows, WIDE), lambda r: (0, r, 0)),
            pl.BlockSpec((rows, WIDE), lambda r: (r, 0)),
        ],
        out_shape=[
            jax.ShapeDtypeStruct((chips, STATE, WIDE), BF16),
            jax.ShapeDtypeStruct((STATE, WIDE), F32),
        ],
        compiler_params=pltpu.CompilerParams(vmem_limit_bytes=VMEM),
        cost_estimate=pl.CostEstimate(flops=2_000_000, bytes_accessed=2_500_000, transcendentals=0),
        name="scan_states",
    )(gathered, gathered, after)


def start_kernel(core_ref, start_ref, first_ref, decay_ref, _, keep_ref, send_ref):
    even = core_ref[0] == 0
    start = start_ref[...].astype(F32)
    later = start * decay_ref[:, 0:1, :] + first_ref[...].astype(F32)
    keep_ref[...] = jnp.where(even, start, later).astype(BF16)
    send_ref[...] = jnp.where(even, later, start).astype(BF16)


def block_starts(core, chip_start, first_update, first_decay, after):
    blocks = chip_start.shape[0]
    part = blocks // 2
    one = lambda i, c: (i, 0, 0)
    shape = jax.ShapeDtypeStruct(chip_start.shape, BF16)
    return pl.pallas_call(
        start_kernel,
        grid_spec=pltpu.PrefetchScalarGridSpec(
            num_scalar_prefetch=1,
            grid=(blocks // part,),
            in_specs=[
                pl.BlockSpec((part, STATE, WIDE), one),
                pl.BlockSpec((part, STATE, WIDE), one),
                pl.BlockSpec((part, 8, WIDE), one),
                pl.BlockSpec(memory_space=pl.ANY),
            ],
            out_specs=[pl.BlockSpec((part, STATE, WIDE), one)] * 2,
        ),
        out_shape=[shape, shape],
        compiler_params=pltpu.CompilerParams(vmem_limit_bytes=VMEM),
        cost_estimate=pl.CostEstimate(flops=2_000_000, bytes_accessed=4_500_000, transcendentals=0),
        name="block_starts",
    )(core, chip_start, first_update, first_decay, after)


def finish_kernel(core_ref, a_ref, g_ref, cc_ref, keep_ref, recv_ref, gain_ref, out_ref, y_ref):
    core = core_ref[0]
    rows, width = a_ref.shape
    total = jnp.zeros((rows, 1), F32)
    c_conv = cc_ref[...]
    for j in range(keep_ref.shape[0]):
        for state_ref, parity in ((keep_ref, core), (recv_ref, 1 - core)):
            at = pl.ds(pl.multiple_of((2 * j + parity) * WIDE, WIDE), WIDE)
            carried = jnp.dot(c_conv, state_ref[j], preferred_element_type=F32)
            y = a_ref[:, at].astype(F32) + carried * g_ref[:, at].astype(F32)
            y_ref[:, at] = y
            total = total + jnp.sum(y * y, axis=1, keepdims=True)
    inverse = 1.0 / jnp.sqrt(total / width + epsilon)
    out_ref[...] = (y_ref[...] * inverse * gain_ref[...]).astype(BF16)


def finish(core, a, g, cc, keep, recv, gain):
    tokens, channels = a.shape
    groups = cc.shape[1] // STATE
    width = channels // groups
    per_group = keep.shape[0] // groups
    rows = tokens // 2
    return pl.pallas_call(
        finish_kernel,
        grid_spec=pltpu.PrefetchScalarGridSpec(
            num_scalar_prefetch=1,
            grid=(groups, 2),
            in_specs=[
                pl.BlockSpec((rows, width), lambda n, r, c: (r, n)),
                pl.BlockSpec((rows, width), lambda n, r, c: (r, n)),
                pl.BlockSpec((rows, STATE), lambda n, r, c: (r, n)),
                pl.BlockSpec((per_group, STATE, WIDE), lambda n, r, c: (n, 0, 0)),
                pl.BlockSpec((per_group, STATE, WIDE), lambda n, r, c: (n, 0, 0)),
                pl.BlockSpec((1, width), lambda n, r, c: (0, n)),
            ],
            out_specs=pl.BlockSpec((rows, width), lambda n, r, c: (r, n)),
            scratch_shapes=[pltpu.VMEM((rows, width), F32)],
        ),
        out_shape=jax.ShapeDtypeStruct((tokens, channels), BF16),
        compiler_params=pltpu.CompilerParams(vmem_limit_bytes=VMEM),
        cost_estimate=pl.CostEstimate(flops=600_000_000, bytes_accessed=9_000_000, transcendentals=1000),
        name="finish",
    )(core, a, g, cc, keep, recv, gain)


def slot_table(owners, dest_count, capacity):
    onehot = (owners[:, None] == jnp.arange(dest_count)[None, :]).astype(jnp.int32)
    earlier = jnp.cumsum(onehot, axis=0) - onehot
    slot_rank = jnp.sum(earlier * onehot, axis=1)
    slot_hit = (slot_rank[:, None] == jnp.arange(capacity)[None, :]).astype(F32)
    return onehot.astype(F32)[:, :, None] * slot_hit[:, None, :]


def local(
    x_input, b_input, output_projection_input, step_input, gate_input, kernel_x, kernel_b, kernel_c,
    step_bias, fading_logarithm, norm_gain, owner_map,
):
    ctx_count = lax.axis_size("ctx")
    ctx_rank = lax.axis_index("ctx")
    dec_count = lax.axis_size("dec")
    dec_rank = lax.axis_index("dec")
    core = ctx_rank % 2
    core_arg = core.astype(jnp.int32).reshape(1)
    x = x_input[0]
    b = b_input[0]
    c = output_projection_input[0]
    step = step_input[0]
    bias = step_bias.reshape(1, -1)
    fading = fading_logarithm.reshape(1, -1)

    swap = [(i, i ^ 1) for i in range(ctx_count)]
    tail = tail_rows(x, b, c)
    x_recv, b_recv, step_recv, c_recv = (
        lax.ppermute(x, "ctx", swap),
        lax.ppermute(b, "ctx", swap),
        lax.ppermute(step, "ctx", swap),
        lax.ppermute(c, "ctx", swap),
    )
    from_even = lax.ppermute(tail, "ctx", [(i, i + 1) for i in range(1, ctx_count - 1, 2)])
    from_odd = lax.ppermute(tail, "ctx", [(i, i + 2) for i in range(1, ctx_count - 2, 2)])
    halo_chip = jnp.where(core == 0, from_even, from_odd)

    updates, first_update, first_decay = block_updates(
        core_arg, x, x_recv, b, b_recv, step, step_recv, halo_chip, kernel_x, kernel_b, bias, fading
    )
    same_core = [[2 * i + j for i in range(ctx_count // 2)] for j in range(2)]
    gathered = lax.all_to_all(updates, "ctx", 0, 0, axis_index_groups=same_core, tiled=True)
    a, g, cc = within_block(
        core_arg, x, gate_input[0], b, c, step, from_even, x_recv, b_recv, c_recv,
        kernel_x, kernel_b, kernel_c, bias, fading,
    )
    starts, state = scan_states(gathered, cc)
    chip_start = lax.all_to_all(starts, "ctx", 0, 0, axis_index_groups=same_core, tiled=True)

    owners = lax.dynamic_slice_in_dim(owner_map[0, :, 0], ctx_rank * HB, HB)
    table = slot_table(owners, dec_count, 2)
    finals = state.T.reshape(HB, HEAD_DIM, STATE)
    outgoing = jnp.sum(table[:, :, :, None, None] * finals[:, None, None], axis=0)
    arrived = jnp.zeros(outgoing.shape, F32)
    for d in range(dec_count):
        piece = lax.dynamic_index_in_dim(outgoing, dec_rank ^ d, 0, keepdims=False)
        if d:
            piece = lax.ppermute(piece, "dec", [(i, i ^ d) for i in range(dec_count)])
        arrived = lax.dynamic_update_index_in_dim(arrived, piece, dec_rank ^ d, 0)

    keep, send = block_starts(core_arg, chip_start, first_update, first_decay, arrived)
    recv = lax.ppermute(send, "ctx", swap)
    mixer_rows = finish(core_arg, a, g, cc, keep, recv, norm_gain.reshape(1, -1))
    return (mixer_rows[None], arrived[None, :, None])


def solution(mesh):
    return jax.shard_map(
        local,
        mesh=mesh,
        in_specs=(
            P("dec", "ctx", "tp"),
            P("dec", "ctx", "tp"),
            P("dec", "ctx", "tp"),
            P("dec", "ctx", "tp"),
            P("dec", "ctx", "tp"),
            P(None, "tp"),
            P(None, "tp"),
            P(None, "tp"),
            P("tp"),
            P("tp"),
            P("tp"),
            P("dec", "tp", None),
        ),
        out_specs=(P("dec", "ctx", "tp"), P("dec", None, ("tp", "ctx"), None, None, None)),
        check_vma=False,
    )
```

time: 401 us -> 117 us (0.29)
  waiting for transfers between devices: 192 us -> 38.9 us
  matrix products: 76.2 us -> 0 us
  Pallas kernels: 0 us -> 42.9 us
  other arithmetic: 43.2 us -> 1.35 us
  local copies, waits for them, and re-layouts: 37.8 us -> 5.52 us
  starting transfers between devices: 47.5 us -> 26.3 us
    all_to_all x6 -> x2, waiting for transfers between devices: 109 us -> 24.9 us  [the longest x1 16 us: local(): lax.all_to_all(starts, 'ctx', 0, 0, axis_index_groups=same_core, tiled=True)]
    dot_general x65 -> x0, matrix products: 76.2 us -> none  [the longest x16 30.7 us: advance(): jnp.einsum('qgn,ghpn->qghp', c_block.astype(jnp.float32), carried, precis...]
    ppermute x3 -> x10, waiting for transfers between devices: 83 us -> 14 us  [the longest x3 8.32 us: local(): piece = lax.ppermute(piece, 'dec', [(i, i ^ d) for i in range(dec_count)])]
    pallas_call x0 -> x6, Pallas kernels: none -> 42.9 us  [the longest x1 18.2 us: within_block(): pl.pallas_call(within_kernel, grid_spec=pltpu.PrefetchScalarGridSpec(num_...]
    all_to_all x6 -> x2, starting transfers between devices: 35.5 us -> 12.5 us  [the longest x1 8.8 us: local(): lax.all_to_all(updates, 'ctx', 0, 0, axis_index_groups=same_core, tiled=T...]
    another operation x32 -> x0, other arithmetic: 20 us -> none
    convert_element_type x10 -> x2, other arithmetic: 11.2 us -> 0.15 us  [the longest x1 0.07 us: slot_table(): slot_hit = (slot_rank[:, None] == jnp.arange(capacity)[None, :]).astype(F32)]
    all_to_all x3 -> x0, local copies, waits for them, and re-layouts: 7.75 us -> none  [the longest x1 3.9 us: local(): lax.all_to_all(scan_out.astype(jnp.bfloat16), 'ctx', split_axis=0, concat...]
  transfers between devices with their start and end apart: 9 -> 12, of which waited for: 7 -> 8; matrix products, arithmetic and copies ran while one was open for 4% -> 2% of each run, Pallas kernels for 0% -> 17%
where the time goes in v1:
time: 117 us; the launch traced here: 116 us
  Pallas kernels  42.9 us (37%)
  waiting for transfers between devices  38.9 us (33%)
  starting transfers between devices  26.3 us (22%)
  local copies, waits for them, and re-layouts  5.52 us (5%)
  other arithmetic  1.35 us (1%)
    pallas_call x1, Pallas kernels, within_block(): pl.pallas_call(within_kernel, grid_spec=pltpu.PrefetchScalarGridSpec(num_...  18.2 us
    all_to_all x1, waiting for transfers between devices, local(): lax.all_to_all(starts, 'ctx', 0, 0, axis_index_groups=same_core, tiled=True)  16 us
    pallas_call x1, Pallas kernels, block_updates(): pl.pallas_call(update_kernel, grid_spec=pltpu.PrefetchScalarGridSpec(num_...  10.8 us
    all_to_all x1, waiting for transfers between devices, local(): lax.all_to_all(updates, 'ctx', 0, 0, axis_index_groups=same_core, tiled=T...  8.92 us
    all_to_all x1, starting transfers between devices, local(): lax.all_to_all(updates, 'ctx', 0, 0, axis_index_groups=same_core, tiled=T...  8.8 us
    ppermute x3, waiting for transfers between devices, local(): piece = lax.ppermute(piece, 'dec', [(i, i ^ d) for i in range(dec_count)])  8.32 us
    pallas_call x1, Pallas kernels, finish(): pl.pallas_call(finish_kernel, grid_spec=pltpu.PrefetchScalarGridSpec(num_...  6.09 us
    unnamed x31, local copies, waits for them, and re-layouts  5.19 us
  transfers between devices with their start and end apart: 12, of which 8 were waited for; matrix products, arithmetic and copies ran while one was open for 2% of the time, Pallas kernels for 17%

profile of v1, /device:TPU:1, one launch (start us, length us, event | category | flops | bytes accessed | tf_op | source)
XLA Modules:
  0.0 115.8 jit_solution(15470631817014152906)
XLA Ops:
  0.6 0.0 copy-start
  0.6 0.0 copy-start.6
  0.7 0.0 copy-start.13
  0.7 3.3 %collective-permute-start.1 = (bf16[256,4096]{1,0:T(8,128)(2,1)}, bf16[256,4096]{1,0:T(8,128)(2,1)S(1)}, u32[]{:S(2)}, u32[]{:S(2)}) collective-permute-start(bf16[256,4096]{1,0:T(8,128)(2,1)} %bitcast.29), channel_id=1, source_target_pairs={{0,16},{16,0},{32,48},{48,32},{64,80},{80,64},{96,112},{112,96},{1... | collective-permute-start | bytes 6291464 | tf_op jit(solution)/shard_map/ppermute | solution.py:480
  4.0 1.6 %tail_rows.1 = bf16[16,5120]{1,0:T(8,128)(2,1)} custom-call(bf16[256,4096]{1,0:T(8,128)(2,1)} %bitcast.30, bf16[256,512]{1,0:T(8,128)(2,1)} %bitcast.36, bf16[256,512]{1,0:T(8,128)(2,1)} %bitcast.41), custom_call_target="tpu_custom_call" | custom-call | tf_op jit(solution)/shard_map/tail_rows/pallas_call | solution.py:82
  5.6 1.7 %collective-permute-start = (bf16[16,5120]{1,0:T(8,128)(2,1)}, bf16[16,5120]{1,0:T(8,128)(2,1)S(1)}, u32[]{:S(2)}, u32[]{:S(2)}) collective-permute-start(bf16[16,5120]{1,0:T(8,128)(2,1)} %tail_rows.1), channel_id=1, source_target_pairs={{16,32},{48,64},{80,96},{112,128},{144,160},{176,192},{208,224},{1... | collective-permute-start | bytes 491528 | tf_op jit(solution)/shard_map/ppermute | solution.py:485
  7.3 3.6 %collective-permute-start.5 = (bf16[16,5120]{1,0:T(8,128)(2,1)}, bf16[16,5120]{1,0:T(8,128)(2,1)S(1)}, u32[]{:S(2)}, u32[]{:S(2)}) collective-permute-start(bf16[16,5120]{1,0:T(8,128)(2,1)} %tail_rows.1), channel_id=1, source_target_pairs={{16,48},{48,80},{80,112},{112,144},{144,176},{176,208},{208,240},{... | collective-permute-start | bytes 491528 | tf_op jit(solution)/shard_map/ppermute | solution.py:486
  10.9 0.0 copy-done.6
  10.9 0.1 collective-permute-start.2
  11.0 0.0 copy-done.13
  11.0 0.1 copy.20
  11.1 0.0 copy-start.10
  11.1 0.6 collective-permute-start.4
  11.7 0.0 collective-permute-done.hx_ref.hb_ref.hc_ref
  11.7 0.0 copy-start.11
  11.7 1.7 %collective-permute-done.5 = bf16[16,5120]{1,0:T(8,128)(2,1)S(1)} collective-permute-done((bf16[16,5120]{1,0:T(8,128)(2,1)}, bf16[16,5120]{1,0:T(8,128)(2,1)S(1)}, u32[]{:S(2)}, u32[]{:S(2)}) %collective-permute-start.5) | collective-permute-done | bytes 163872 | tf_op jit(solution)/shard_map/ppermute | solution.py:486
  13.4 0.7 broadcast_select_fusion.hx_ref.hb_ref
  14.1 0.0 collective-permute-done.4.sr_ref
  14.1 0.0 copy-start.12
  14.1 0.0 collective-permute-done.2.tb_ref.br_ref
  14.1 0.0 copy-start.9
  14.1 0.0 collective-permute-done.1.tx_ref.xr_ref
  14.1 0.0 copy-start.4
  14.1 0.0 copy-done.10
  14.2 0.6 copy-done.12
  14.7 0.1 copy-done.9
  14.8 0.7 copy-done.4
  15.5 10.8 %block_updates.1 = (bf16[8,272,256]{2,1,0:T(8,128)(2,1)}, bf16[8,256,256]{2,1,0:T(8,128)(2,1)}, f32[8,8,256]{2,1,0:T(8,128)}) custom-call(s32[1]{0:T(128)} %bitcast.core_ref, bf16[256,4096]{1,0:T(8,128)(2,1)} %bitcast.31, bf16[256,4096]{1,0:T(8,128)(2,1)} %copy-done.4, bf16[256,512]{1,0:T(8,128)(2,1)} %bitcast.37, bf16[256,512]{1,0:T(8,128)(2,1)} %copy-done.9, ...), custom_call_target="tpu_custom_call" | custom-call | flops 600000000 | bytes 6000000 | tf_op jit(solution)/shard_map/block_updates/pallas_call | solution.py:164
  26.3 0.0 copy-done.11
  26.3 0.0 copy-start.8
  26.4 8.8 %all-to-all-start = ((bf16[8,272,256]{2,1,0:T(8,128)(2,1)}), bf16[8,272,256]{2,1,0:T(8,128)(2,1)S(1)}, u32[]{:S(2)}, u32[]{:S(2)}) async-start(bf16[8,272,256]{2,1,0:T(8,128)(2,1)} %get-tuple-element.15), calls=%async_computation | async-start | bytes 2228224 | tf_op jit(solution)/shard_map/all_to_all | solution.py:493
  35.2 0.0 copy-done.8
  35.2 0.1 collective-permute-start.3
  35.3 0.0 copy-done
  35.3 0.1 fusion.3
  35.4 1.4 %collective-permute-done.3.tc_ref = bf16[256,512]{1,0:T(8,128)(2,1)S(1)} collective-permute-done((bf16[256,512]{1,0:T(8,128)(2,1)S(1)}, bf16[256,512]{1,0:T(8,128)(2,1)S(1)}, u32[]{:S(2)}, u32[]{:S(2)}) %collective-permute-start.3) | collective-permute-done | bytes 262176 | tf_op jit(solution)/shard_map/ppermute | solution.py:483
  36.8 0.7 copy-done.14
  37.5 18.2 %within_block.1 = (bf16[256,4096]{1,0:T(8,128)(2,1)}, bf16[256,4096]{1,0:T(8,128)(2,1)}, bf16[256,512]{1,0:T(8,128)(2,1)}) custom-call(s32[1]{0:T(128)} %bitcast.core_ref, bf16[256,4096]{1,0:T(8,128)(2,1)} %bitcast.32, bf16[256,4096]{1,0:T(8,128)(2,1)} %bitcast.52, bf16[256,512]{1,0:T(8,128)(2,1)} %bitcast.38, bf16[256,512]{1,0:T(8,128)(2,1)} %bitcast.42, ...), custom_call_target="tpu_custom_call" | custom-call | flops 8000000000 | bytes 12000000 | tf_op jit(solution)/shard_map/within_block/pallas_call | solution.py:289
  55.7 8.9 %all-to-all-done.gathered_ref.decay_ref = bf16[8,272,256]{2,1,0:T(8,128)(2,1)S(1)} async-done(((bf16[8,272,256]{2,1,0:T(8,128)(2,1)}), bf16[8,272,256]{2,1,0:T(8,128)(2,1)S(1)}, u32[]{:S(2)}, u32[]{:S(2)}) %all-to-all-start) | async-done | bytes 1114144 | tf_op jit(solution)/shard_map/all_to_all | solution.py:493
  64.6 1.0 copy-done.1
  65.6 3.5 %scan_states.1 = (bf16[8,256,256]{2,1,0:T(8,128)(2,1)}, f32[256,256]{1,0:T(8,128)}) custom-call(bf16[8,272,256]{2,1,0:T(8,128)(2,1)} %copy-done.1, bf16[8,272,256]{2,1,0:T(8,128)(2,1)} %copy-done.1, bf16[256,512]{1,0:T(8,128)(2,1)} %get-tuple-element.14._.cc_ref), custom_call_target="tpu_custom_call" | custom-call | flops 2000000 | bytes 2500000 | tf_op jit(solution)/shard_map/scan_states/pallas_call | solution.py:352
  69.1 3.7 %all-to-all-start.1 = ((bf16[8,256,256]{2,1,0:T(8,128)(2,1)}), bf16[8,256,256]{2,1,0:T(8,128)(2,1)S(1)}, u32[]{:S(2)}, u32[]{:S(2)}) async-start(bf16[8,256,256]{2,1,0:T(8,128)(2,1)} %get-tuple-element.16), calls=%async_computation.1 | async-start | bytes 2097152 | tf_op jit(solution)/shard_map/all_to_all | solution.py:499
  72.8 0.1 fusion.2
  72.9 0.2 select_reduce_fusion
  73.1 0.1 fusion.1
  73.2 0.1 broadcast_multiply_fusion
  73.2 0.0 copy-done.7
  73.2 0.1 copy.21
  73.4 0.2 multiply_reduce_fusion
  73.7 1.3 %collective-permute-start.6 = (f32[2,64,256]{2,1,0:T(8,128)S(1)}, f32[2,64,256]{2,1,0:T(8,128)S(1)}, u32[]{:S(2)}, u32[]{:S(2)}) collective-permute-start(f32[2,64,256]{2,1,0:T(8,128)S(1)} %get-tuple-element.30), channel_id=1, source_target_pairs={{0,1},{1,0},{2,3},{3,2},{4,5},{5,4},{6,7},{7,6},{8,9},{9,8},{10,11... | collective-permute-start | bytes 393224 | tf_op jit(solution)/shard_map/ppermute | solution.py:509
  75.0 2.5 %collective-permute-start.7 = (f32[2,64,256]{2,1,0:T(8,128)S(1)}, f32[2,64,256]{2,1,0:T(8,128)S(1)}, u32[]{:S(2)}, u32[]{:S(2)}) collective-permute-start(f32[2,64,256]{2,1,0:T(8,128)S(1)} %get-tuple-element.29), channel_id=1, source_target_pairs={{0,2},{1,3},{2,0},{3,1},{4,6},{5,7},{6,4},{7,5},{8,10},{9,11},{10,... | collective-permute-start | bytes 393224 | tf_op jit(solution)/shard_map/ppermute | solution.py:509
  77.5 0.2 collective-permute-start.8
  77.7 0.8 collective-permute-done.6
  78.5 5.0 %collective-permute-done.7 = f32[2,64,256]{2,1,0:T(8,128)S(1)} collective-permute-done((f32[2,64,256]{2,1,0:T(8,128)S(1)}, f32[2,64,256]{2,1,0:T(8,128)S(1)}, u32[]{:S(2)}, u32[]{:S(2)}) %collective-permute-start.7) | collective-permute-done | bytes 131104 | tf_op jit(solution)/shard_map/ppermute | solution.py:509
  83.6 2.5 %collective-permute-done.8 = f32[2,64,256]{2,1,0:T(8,128)S(1)} collective-permute-done((f32[2,64,256]{2,1,0:T(8,128)S(1)}, f32[2,64,256]{2,1,0:T(8,128)S(1)}, u32[]{:S(2)}, u32[]{:S(2)}) %collective-permute-start.8) | collective-permute-done | bytes 131104 | tf_op jit(solution)/shard_map/ppermute | solution.py:509
  86.0 0.0 copy-start.3
  86.0 16.0 %all-to-all-done.1.start_ref = bf16[8,256,256]{2,1,0:T(8,128)(2,1)S(1)} async-done(((bf16[8,256,256]{2,1,0:T(8,128)(2,1)}), bf16[8,256,256]{2,1,0:T(8,128)(2,1)S(1)}, u32[]{:S(2)}, u32[]{:S(2)}) %all-to-all-start.1) | async-done | bytes 1048608 | tf_op jit(solution)/shard_map/all_to_all | solution.py:499
  102.0 0.0 copy-done.3
  102.0 1.0 copy-done.2
  103.0 2.7 %block_starts.1 = (bf16[8,256,256]{2,1,0:T(8,128)(2,1)}, bf16[8,256,256]{2,1,0:T(8,128)(2,1)}) custom-call(s32[1]{0:T(128)} %bitcast.core_ref, bf16[8,256,256]{2,1,0:T(8,128)(2,1)} %copy-done.2, bf16[8,256,256]{2,1,0:T(8,128)(2,1)} %get-tuple-element.17.first_ref, f32[8,8,256]{2,1,0:T(8,128)} %get-tuple-element.18.decay_ref, f32[4,2,64,256]{3,2,1,0:T(8,128)} %copy-done.3), custom_call_target="tpu_custom_call" | custom-call | flops 2000000 | bytes 4500000 | tf_op jit(solution)/shard_map/block_starts/pallas_call | solution.py:387
  105.7 0.5 collective-permute-start.9
  106.2 2.5 %collective-permute-done.9.recv_ref = bf16[8,256,256]{2,1,0:T(8,128)(2,1)S(1)} collective-permute-done((bf16[8,256,256]{2,1,0:T(8,128)(2,1)}, bf16[8,256,256]{2,1,0:T(8,128)(2,1)S(1)}, u32[]{:S(2)}, u32[]{:S(2)}) %collective-permute-start.9) | collective-permute-done | bytes 1048608 | tf_op jit(solution)/shard_map/ppermute | solution.py:513
  108.7 1.0 copy-done.5
  109.7 6.1 %finish.1 = bf16[256,4096]{1,0:T(8,128)(2,1)} custom-call(s32[1]{0:T(128)} %bitcast.core_ref, bf16[256,4096]{1,0:T(8,128)(2,1)} %get-tuple-element.12.a_ref, bf16[256,4096]{1,0:T(8,128)(2,1)} %get-tuple-element.13.g_ref, bf16[256,512]{1,0:T(8,128)(2,1)} %get-tuple-element.14._.cc_ref, bf16[8,256,256]{2,1,0:T(8,128)(2,1)} %get-tuple-element.20.keep_ref, ...), custom_call_target="tpu_custom_call" | custom-call | flops 600000000 | bytes 9000000 | tf_op jit(solution)/shard_map/finish/pallas_call | solution.py:429
  (11 shorter events, 0.2 us)
Async XLA Ops:
  0.6 34.7 %copy-start = (s32[1,64,1]{1,2,0:T(1,128)S(1)}, s32[1,64,1]{1,2,0:T(1,128)}, u32[]{:S(2)}) copy-start(s32[1,64,1]{1,2,0:T(1,128)} %param.23) | copy-start | bytes 772
  0.6 10.2 %copy-start.6 = (bf16[1,256,512]{2,1,0:T(8,128)(2,1)S(1)}, bf16[1,256,512]{2,1,0:T(8,128)(2,1)}, u32[]{:S(2)}) copy-start(bf16[1,256,512]{2,1,0:T(8,128)(2,1)} %param.13) | copy-start | bytes 786436
  0.7 10.3 %copy-start.13 = (bf16[1,256,64]{1,2,0:T(8,128)(2,1)S(1)}, bf16[1,256,64]{1,2,0:T(8,128)(2,1)}, u32[]{:S(2)}) copy-start(bf16[1,256,64]{1,2,0:T(8,128)(2,1)} %param.15) | copy-start | bytes 98308
  0.7 13.5 %collective-permute-start.1 = (bf16[256,4096]{1,0:T(8,128)(2,1)}, bf16[256,4096]{1,0:T(8,128)(2,1)S(1)}, u32[]{:S(2)}, u32[]{:S(2)}) collective-permute-start(bf16[256,4096]{1,0:T(8,128)(2,1)} %bitcast.29), channel_id=1, source_target_pairs={{0,16},{16,0},{32,48},{48,32},{64,80},{80,64},{96,112},{112,96},{1... | collective-permute-start | bytes 6291464 | tf_op jit(solution)/shard_map/ppermute | solution.py:480
  5.6 6.1 %collective-permute-start = (bf16[16,5120]{1,0:T(8,128)(2,1)}, bf16[16,5120]{1,0:T(8,128)(2,1)S(1)}, u32[]{:S(2)}, u32[]{:S(2)}) collective-permute-start(bf16[16,5120]{1,0:T(8,128)(2,1)} %tail_rows.1), channel_id=1, source_target_pairs={{16,32},{48,64},{80,96},{112,128},{144,160},{176,192},{208,224},{1... | collective-permute-start | bytes 491528 | tf_op jit(solution)/shard_map/ppermute | solution.py:485
  7.3 6.1 %collective-permute-start.5 = (bf16[16,5120]{1,0:T(8,128)(2,1)}, bf16[16,5120]{1,0:T(8,128)(2,1)S(1)}, u32[]{:S(2)}, u32[]{:S(2)}) collective-permute-start(bf16[16,5120]{1,0:T(8,128)(2,1)} %tail_rows.1), channel_id=1, source_target_pairs={{16,48},{48,80},{80,112},{112,144},{144,176},{176,208},{208,240},{... | collective-permute-start | bytes 491528 | tf_op jit(solution)/shard_map/ppermute | solution.py:486
  10.9 3.2 %collective-permute-start.2 = (bf16[256,512]{1,0:T(8,128)(2,1)S(1)}, bf16[256,512]{1,0:T(8,128)(2,1)S(1)}, u32[]{:S(2)}, u32[]{:S(2)}) collective-permute-start(bf16[256,512]{1,0:T(8,128)(2,1)S(1)} %bitcast.39), channel_id=1, source_target_pairs={{0,16},{16,0},{32,48},{48,32},{64,80},{80,64},{96,112},{112,96},{1... | collective-permute-start | bytes 786440 | tf_op jit(solution)/shard_map/ppermute | solution.py:481
  11.1 3.0 %copy-start.10 = (bf16[1,256,64]{2,1,0:T(8,128)(2,1)}, bf16[1,256,64]{2,1,0:T(8,128)(2,1)S(1)}, u32[]{:S(2)}) copy-start(bf16[1,256,64]{2,1,0:T(8,128)(2,1)S(1)} %copy.20) | copy-start | bytes 98308
  11.1 3.0 %collective-permute-start.4 = (bf16[256,64]{1,0:T(8,128)(2,1)S(1)}, bf16[256,64]{1,0:T(8,128)(2,1)S(1)}, u32[]{:S(2)}, u32[]{:S(2)}) collective-permute-start(bf16[256,64]{1,0:T(8,128)(2,1)S(1)} %bitcast.44), channel_id=1, source_target_pairs={{0,16},{16,0},{32,48},{48,32},{64,80},{80,64},{96,112},{112,96},{1... | collective-permute-start | bytes 98312 | tf_op jit(solution)/shard_map/ppermute | solution.py:482
  11.7 14.6 %copy-start.11 = (bf16[16,5120]{1,0:T(8,128)(2,1)}, bf16[16,5120]{1,0:T(8,128)(2,1)S(1)}, u32[]{:S(2)}) copy-start(bf16[16,5120]{1,0:T(8,128)(2,1)S(1)} %collective-permute-done.hx_ref.hb_ref.hc_ref) | copy-start | bytes 491524
  14.1 0.6 copy-start.12
  14.1 0.7 copy-start.9
  14.1 1.4 %copy-start.4 = (bf16[256,4096]{1,0:T(8,128)(2,1)}, bf16[256,4096]{1,0:T(8,128)(2,1)S(1)}, u32[]{:S(2)}) copy-start(bf16[256,4096]{1,0:T(8,128)(2,1)S(1)} %collective-permute-done.1.tx_ref.xr_ref) | copy-start | bytes 6291460
  26.3 8.8 %copy-start.8 = (bf16[1,256,512]{2,1,0:T(8,128)(2,1)S(1)}, bf16[1,256,512]{2,1,0:T(8,128)(2,1)}, u32[]{:S(2)}) copy-start(bf16[1,256,512]{2,1,0:T(8,128)(2,1)} %param.14) | copy-start | bytes 786436
  26.4 38.2 %all-to-all-start = ((bf16[8,272,256]{2,1,0:T(8,128)(2,1)}), bf16[8,272,256]{2,1,0:T(8,128)(2,1)S(1)}, u32[]{:S(2)}, u32[]{:S(2)}) async-start(bf16[8,272,256]{2,1,0:T(8,128)(2,1)} %get-tuple-element.15), calls=%async_computation | async-start | bytes 2228224 | tf_op jit(solution)/shard_map/all_to_all | solution.py:493
  35.2 1.6 %collective-permute-start.3 = (bf16[256,512]{1,0:T(8,128)(2,1)S(1)}, bf16[256,512]{1,0:T(8,128)(2,1)S(1)}, u32[]{:S(2)}, u32[]{:S(2)}) collective-permute-start(bf16[256,512]{1,0:T(8,128)(2,1)S(1)} %bitcast.43), channel_id=1, source_target_pairs={{0,16},{16,0},{32,48},{48,32},{64,80},{80,64},{96,112},{112,96},{1... | collective-permute-start | bytes 786440 | tf_op jit(solution)/shard_map/ppermute | solution.py:483
  36.8 0.7 copy-start.14
  64.6 1.0 copy-start.1
  69.1 4.1 %copy-start.7 = (f32[256,256]{1,0:T(8,128)S(1)}, f32[256,256]{1,0:T(8,128)}, u32[]{:S(2)}) copy-start(f32[256,256]{1,0:T(8,128)} %get-tuple-element.19) | copy-start | bytes 786436
  69.1 32.9 %all-to-all-start.1 = ((bf16[8,256,256]{2,1,0:T(8,128)(2,1)}), bf16[8,256,256]{2,1,0:T(8,128)(2,1)S(1)}, u32[]{:S(2)}, u32[]{:S(2)}) async-start(bf16[8,256,256]{2,1,0:T(8,128)(2,1)} %get-tuple-element.16), calls=%async_computation.1 | async-start | bytes 2097152 | tf_op jit(solution)/shard_map/all_to_all | solution.py:499
  73.7 4.8 %collective-permute-start.6 = (f32[2,64,256]{2,1,0:T(8,128)S(1)}, f32[2,64,256]{2,1,0:T(8,128)S(1)}, u32[]{:S(2)}, u32[]{:S(2)}) collective-permute-start(f32[2,64,256]{2,1,0:T(8,128)S(1)} %get-tuple-element.30), channel_id=1, source_target_pairs={{0,1},{1,0},{2,3},{3,2},{4,5},{5,4},{6,7},{7,6},{8,9},{9,8},{10,11... | collective-permute-start | bytes 393224 | tf_op jit(solution)/shard_map/ppermute | solution.py:509
  75.0 8.5 %collective-permute-start.7 = (f32[2,64,256]{2,1,0:T(8,128)S(1)}, f32[2,64,256]{2,1,0:T(8,128)S(1)}, u32[]{:S(2)}, u32[]{:S(2)}) collective-permute-start(f32[2,64,256]{2,1,0:T(8,128)S(1)} %get-tuple-element.29), channel_id=1, source_target_pairs={{0,2},{1,3},{2,0},{3,1},{4,6},{5,7},{6,4},{7,5},{8,10},{9,11},{10,... | collective-permute-start | bytes 393224 | tf_op jit(solution)/shard_map/ppermute | solution.py:509
  77.5 8.5 %collective-permute-start.8 = (f32[2,64,256]{2,1,0:T(8,128)S(1)}, f32[2,64,256]{2,1,0:T(8,128)S(1)}, u32[]{:S(2)}, u32[]{:S(2)}) collective-permute-start(f32[2,64,256]{2,1,0:T(8,128)S(1)} %get-tuple-element.28), channel_id=1, source_target_pairs={{0,3},{1,2},{2,1},{3,0},{4,7},{5,6},{6,5},{7,4},{8,11},{9,10},{10,... | collective-permute-start | bytes 393224 | tf_op jit(solution)/shard_map/ppermute | solution.py:509
  86.0 16.0 %copy-start.3 = (f32[4,2,64,256]{3,2,1,0:T(8,128)}, f32[4,2,64,256]{3,2,1,0:T(8,128)S(1)}, u32[]{:S(2)}) copy-start(f32[4,2,64,256]{3,2,1,0:T(8,128)S(1)} %bitcast_dynamic-update-slice_fusion._) | copy-start | bytes 1572868
  102.0 1.0 copy-start.2
  105.7 3.0 %collective-permute-start.9 = (bf16[8,256,256]{2,1,0:T(8,128)(2,1)}, bf16[8,256,256]{2,1,0:T(8,128)(2,1)S(1)}, u32[]{:S(2)}, u32[]{:S(2)}) collective-permute-start(bf16[8,256,256]{2,1,0:T(8,128)(2,1)} %get-tuple-element.21), channel_id=1, source_target_pairs={{0,16},{16,0},{32,48},{48,32},{64,80},{80,64},{96,112},{112,96},{1... | collective-permute-start | bytes 3145736 | tf_op jit(solution)/shard_map/ppermute | solution.py:513
  108.7 1.0 copy-start.5

commit v2 on v1

v2 whole, which is shorter than its diff:
```python
import functools

import jax
import jax.numpy as jnp
from jax import lax
from jax.experimental import pallas as pl
from jax.experimental.pallas import tpu as pltpu
from jax.sharding import PartitionSpec as P

HEAD_DIM = 64
STATE = 256
BLOCK = 256
HB = 4
WIDE = HB * HEAD_DIM
LOG2E = 1.4426950408889634
VMEM = 40 * 1024 * 1024
SMALL = 12 * 1024 * 1024
IN_VMEM = pl.BlockSpec(memory_space=pltpu.VMEM)
IN_HBM = pl.BlockSpec(memory_space=pl.ANY)


def hbm(value):
    return pltpu.with_memory_space_constraint(value, pltpu.HBM)


def vmem(value):
    return pltpu.with_memory_space_constraint(value, pltpu.VMEM)

epsilon = 1e-05
F32 = jnp.float32
BF16 = jnp.bfloat16
HIGHEST = lax.Precision.HIGHEST


def split3(value):
    high = value.astype(BF16)
    rest = value - high.astype(F32)
    middle = rest.astype(BF16)
    low = (rest - middle.astype(F32)).astype(BF16)
    return high, middle, low


def softplus(value):
    return jnp.maximum(value, 0.0) + jnp.log1p(jnp.exp(-jnp.abs(value)))


def silu_of_twice(half):
    return half + half * jnp.tanh(half)


def spread(rows, width, first_head, heads):
    row = lax.broadcasted_iota(jnp.int32, (rows, width), 0)
    channel = lax.broadcasted_iota(jnp.int32, (rows, width), 1)
    head = row % heads
    return (head == first_head + channel // HEAD_DIM).astype(BF16)


def conv(pad_ref, prior, rows, taps):
    count = rows.shape[0]
    pad_ref[0:8, :] = prior
    pad_ref[8 : 8 + count, :] = rows
    taps = taps.astype(F32) * 0.5
    running = taps[0:1] * pad_ref[5 : 5 + count, :]
    for j in range(1, 4):
        running = running + taps[j : j + 1] * pad_ref[5 + j : 5 + j + count, :]
    return silu_of_twice(running).astype(BF16)


def edge_sums(prior, rows, taps):
    both = jnp.concatenate([prior, rows], axis=0)
    taps = taps.astype(F32) * 0.5
    running = taps[0:1] * both[5:13]
    for j in range(1, 4):
        running = running + taps[j : j + 1] * both[5 + j : 13 + j]
    return running


def steps_of(step, bias, fading):
    size = softplus(step.astype(F32) + bias)
    decay = -size * jnp.exp(fading)
    count = step.shape[0]
    row = lax.broadcasted_iota(jnp.int32, (count, count), 0)
    col = lax.broadcasted_iota(jnp.int32, (count, count), 1)
    lower = (row >= col).astype(BF16)
    pieces = jnp.concatenate(split3(decay), axis=1)
    sums = jnp.dot(lower, pieces, preferred_element_type=F32)
    heads = step.shape[1]
    cumulative = sums[:, :heads] + sums[:, heads : 2 * heads] + sums[:, 2 * heads :]
    return size, cumulative


def lanes(block, width=WIDE):
    return pl.ds(pl.multiple_of(block * width, width), width)


def weights_of(step, bias, fading):
    size, cumulative = steps_of(step, bias, fading)
    last = cumulative[-1:]
    high, middle, _ = split3(size * jnp.exp(last - cumulative))
    return jnp.concatenate([high, middle], axis=1), last


def whole(value):
    return pl.BlockSpec(value.shape, lambda *_: (0,) * value.ndim)


def own_kernel(
    core_ref, x_ref, b_ref, ct_ref, step_ref, kx_ref, kb_ref, bias_ref, fading_ref,
    u_ref, first_weight_ref, closing_ref, tail_ref, pad, weight,
):
    n = pl.program_id(0)
    core = core_ref[0]
    heads = step_ref.shape[1]
    per_group = u_ref.shape[0] // 2
    end = slice(BLOCK - 16, BLOCK)
    x_width, b_width = x_ref.shape[1], b_ref.shape[1]
    tail_ref[:, lanes(n, x_width)] = x_ref[end, :]
    tail_ref[:, lanes(2 * x_width // b_width + n, b_width)] = b_ref[end, :]
    tail_ref[:, 2 * (x_width + b_width) :] = ct_ref[...]

    @pl.when(n == 0)
    def _():
        value, last = weights_of(step_ref[...], bias_ref[...], fading_ref[...])
        first_weight_ref[...] = value[0:16]
        closing_ref[...] = jnp.broadcast_to(last, (8, heads))
        row = lax.broadcasted_iota(jnp.int32, value.shape, 0)
        weight[...] = jnp.where(row < 8, 0.0, value.astype(F32)).astype(BF16)

    none = jnp.zeros((8, STATE), F32)
    b_t = conv(pad.at[0], none, b_ref[...].astype(F32), kb_ref[...]).astype(F32).T.astype(BF16)
    for j in range(per_group):
        block = 2 * j + core
        at = lanes(block)
        x_conv = conv(pad.at[j % 2], none, x_ref[:, at].astype(F32), kx_ref[:, at]).astype(F32)
        select = spread(2 * heads, WIDE, (2 * per_group * n + block) * HB, heads)
        inputs = x_conv * jnp.dot(weight[...], select, preferred_element_type=F32)
        u_ref[n * per_group + j] = jnp.dot(b_t, inputs.astype(BF16), preferred_element_type=F32)


def own_updates(core, x, b, c, step, kernel_x, kernel_b, bias, fading):
    heads = step.shape[1]
    groups = b.shape[1] // STATE
    width = x.shape[1] // groups
    blocks = x.shape[1] // WIDE // 2
    one = lambda n, c: (0, n)
    return pl.pallas_call(
        own_kernel,
        grid_spec=pltpu.PrefetchScalarGridSpec(
            num_scalar_prefetch=1,
            grid=(groups,),
            in_specs=[
                pl.BlockSpec((BLOCK, width), one),
                pl.BlockSpec((BLOCK, STATE), one),
                pl.BlockSpec((16, c.shape[1]), lambda n, s: (BLOCK // 16 - 1, 0)),
                whole(step),
                pl.BlockSpec((4, width), one),
                pl.BlockSpec((4, STATE), one),
                whole(bias),
                whole(fading),
            ],
            out_specs=[IN_VMEM, IN_VMEM, IN_VMEM, IN_VMEM],
            scratch_shapes=[
                pltpu.VMEM((2, BLOCK + 8, WIDE), F32),
                pltpu.VMEM((BLOCK, 2 * heads), BF16),
            ],
        ),
        out_shape=[
            pltpu.VMEM((blocks, STATE, WIDE), F32),
            pltpu.VMEM((16, 2 * heads), BF16),
            pltpu.VMEM((8, heads), F32),
            pltpu.VMEM((16, x.shape[1] + b.shape[1] + c.shape[1]), BF16),
        ],
        compiler_params=pltpu.CompilerParams(vmem_limit_bytes=VMEM),
        cost_estimate=pl.CostEstimate(flops=300_000_000, bytes_accessed=10_000_000, transcendentals=600_000),
        name="own_updates",
    )(core, hbm(x), hbm(b), hbm(c), hbm(step), hbm(kernel_x), hbm(kernel_b), hbm(bias), hbm(fading))


def chip_kernel(
    core_ref, u_own_ref, first_weight_ref, closing_ref, xh_ref, xt_ref, bh_ref, bt_ref, xr_ref, br_ref,
    sr_ref, kx_ref, kb_ref, bias_ref, fading_ref,
    u_ref, first_ref, decay_ref, edge_ref, pad, small, extra, weight, weight_first, values,
):
    n = pl.program_id(0)
    core = core_ref[0]
    even = core == 0
    heads = sr_ref.shape[1]
    per_group = u_ref.shape[0]
    head8 = slice(0, 8)
    tail8 = slice(8, 16)

    @pl.when(n == 0)
    def _():
        value, last = weights_of(sr_ref[...], bias_ref[...], fading_ref[...])
        row = lax.broadcasted_iota(jnp.int32, value.shape, 0)
        weight[...] = jnp.where((row < 3) & jnp.logical_not(even), 0.0, value.astype(F32)).astype(BF16)
        mine = first_weight_ref[...].astype(F32)
        row = lax.broadcasted_iota(jnp.int32, mine.shape, 0)
        dropped = (row >= 8) | ((row < 3) & even)
        weight_first[...] = jnp.where(dropped, 0.0, mine).astype(BF16)
        edge = jnp.where(even, mine, value[0:16].astype(F32))
        edge = edge[:, :heads] + edge[:, heads:]
        own = jnp.exp(closing_ref[0:1, :])
        other = jnp.exp(last)
        values[0:1, :] = own
        values[1:2, :] = other
        values[2:3, :] = jnp.exp(closing_ref[0:1, :] + last)
        values[3:6, :] = edge[0:3] * jnp.where(even, other, own)
        values[6:9, :] = edge[0:3]
        values[9:16, :] = jnp.zeros((7, heads), F32)

    def edges(own_head, own_end, recv_head, recv_end, taps):
        none = jnp.zeros(own_head.shape, F32)
        first = edge_sums(none, jnp.where(even, own_head, recv_head), taps)
        last = edge_sums(jnp.where(even, recv_end, own_end), none, taps)
        return jnp.where(even, none, recv_end), jnp.where(even, own_end, none), first, last

    def rows_of(ref, rows, at):
        return ref[rows, at].astype(F32)

    end = slice(BLOCK - 16, BLOCK)
    at = lanes(n, STATE)
    everything = slice(None)
    prior_own, prior_recv, b_first, b_last = edges(
        rows_of(bh_ref, slice(0, 16), everything)[head8],
        rows_of(bt_ref, slice(0, 16), everything)[tail8],
        rows_of(br_ref, slice(0, 16), at)[head8],
        rows_of(br_ref, end, at)[tail8],
        kb_ref[...],
    )
    b_own = conv(small.at[0], prior_own, bh_ref[...].astype(F32), kb_ref[...])
    b_recv = conv(pad.at[0], prior_recv, br_ref[:, at].astype(F32), kb_ref[...])
    b_own = b_own.astype(F32).T.astype(BF16)
    b_recv = b_recv.astype(F32).T.astype(BF16)
    pieces = jnp.concatenate(split3(values[...]), axis=1)
    for j in range(per_group):
        block = 2 * j + core
        head = (2 * per_group * n + block) * HB
        here = lanes(block)
        at = lanes(2 * per_group * n + block)
        taps = kx_ref[:, here]
        select = spread(2 * heads, WIDE, head, heads)
        prior_own, prior_recv, x_first, x_last = edges(
            rows_of(xh_ref, slice(0, 16), here)[head8],
            rows_of(xt_ref, slice(0, 16), here)[tail8],
            rows_of(xr_ref, slice(0, 16), at)[head8],
            rows_of(xr_ref, end, at)[tail8],
            taps,
        )
        x_own = conv(small.at[j % 2], prior_own, xh_ref[:, here].astype(F32), taps).astype(F32)
        x_own = x_own * jnp.dot(weight_first[...], select, preferred_element_type=F32)
        x_conv = conv(pad.at[j % 2], prior_recv, xr_ref[:, at].astype(F32), taps).astype(F32)
        inputs = x_conv * jnp.dot(weight[...], select, preferred_element_type=F32)
        u_recv = jnp.dot(b_recv, inputs.astype(BF16), preferred_element_type=F32)
        u_own = u_own_ref[n * per_group + j] + jnp.dot(
            b_own, x_own.astype(BF16), preferred_element_type=F32
        )
        wide = jnp.dot(pieces, spread(3 * heads, WIDE, head, heads), preferred_element_type=F32)
        own_factor = jnp.where(even, wide[1:2], 1.0)
        recv_factor = jnp.where(even, 1.0, wide[0:1])
        u_ref[j, 0:STATE, :] = (u_own * own_factor + u_recv * recv_factor).astype(BF16)
        first_ref[j] = jnp.where(even, u_own, u_recv).astype(BF16)
        decay_ref[j] = jnp.broadcast_to(jnp.where(even, wide[0:1], wide[1:2]), (8, WIDE))
        high, middle, low = split3(wide[2:3])
        place = lax.broadcasted_iota(jnp.int32, (1, WIDE), 1) % HEAD_DIM // 8
        packed = jnp.zeros((1, WIDE), F32)
        for q, value in enumerate((high, middle, low, wide[3:4], wide[4:5], wide[5:6])):
            packed = jnp.where(place == q, value.astype(F32), packed)
        extra[0:1, :] = packed
        extra[1:4, :] = x_first[0:3]
        extra[4:7, :] = x_last[0:3]
        extra[7:10, :] = b_first[0:3]
        extra[10:13, :] = b_last[0:3]
        extra[13:16, :] = jnp.zeros((3, WIDE), F32)
        u_ref[j, STATE : STATE + 16, :] = extra[...].astype(BF16)
        edge_ref[j, 0:3, :] = x_first[0:3]
        edge_ref[j, 3:6, :] = b_first[0:3]
        edge_ref[j, 6:9, :] = wide[6:9]
        edge_ref[j, 9:16, :] = jnp.zeros((7, WIDE), F32)


def chip_updates(core, own, x, b, x_recv, b_recv, step_recv, kernel_x, kernel_b, bias, fading):
    u_own, first_weight, closing = own
    heads = step_recv.shape[1]
    groups = b.shape[1] // STATE
    width = x.shape[1] // groups
    blocks = x.shape[1] // WIDE // 2
    per_group = blocks // groups
    end = BLOCK // 16 - 1
    one = lambda n, c: (0, n)
    tail = lambda n, c: (end, n)
    out = lambda n, c: (n, 0, 0)
    return pl.pallas_call(
        chip_kernel,
        grid_spec=pltpu.PrefetchScalarGridSpec(
            num_scalar_prefetch=1,
            grid=(groups,),
            in_specs=[
                IN_VMEM,
                IN_VMEM,
                IN_VMEM,
                pl.BlockSpec((16, width), one),
                pl.BlockSpec((16, width), tail),
                pl.BlockSpec((16, STATE), one),
                pl.BlockSpec((16, STATE), tail),
                IN_VMEM,
                IN_VMEM,
                IN_VMEM,
                pl.BlockSpec((4, width), one),
                pl.BlockSpec((4, STATE), one),
                whole(bias),
                whole(fading),
            ],
            out_specs=[
                pl.BlockSpec((per_group, STATE + 16, WIDE), out),
                pl.BlockSpec((per_group, STATE, WIDE), out),
                pl.BlockSpec((per_group, 8, WIDE), out),
                pl.BlockSpec((per_group, 16, WIDE), out),
            ],
            scratch_shapes=[
                pltpu.VMEM((2, BLOCK + 8, WIDE), F32),
                pltpu.VMEM((2, 24, WIDE), F32),
                pltpu.VMEM((16, WIDE), F32),
                pltpu.VMEM((BLOCK, 2 * heads), BF16),
                pltpu.VMEM((16, 2 * heads), BF16),
                pltpu.VMEM((16, heads), F32),
            ],
        ),
        out_shape=[
            pltpu.HBM((blocks, STATE + 16, WIDE), BF16),
            pltpu.HBM((blocks, STATE, WIDE), BF16),
            pltpu.HBM((blocks, 8, WIDE), F32),
            pltpu.HBM((blocks, 16, WIDE), F32),
        ],
        compiler_params=pltpu.CompilerParams(vmem_limit_bytes=VMEM),
        cost_estimate=pl.CostEstimate(flops=300_000_000, bytes_accessed=10_000_000, transcendentals=600_000),
        name="chip_updates",
    )(
        core, vmem(u_own), vmem(first_weight), vmem(closing), hbm(x), hbm(x), hbm(b), hbm(b), vmem(x_recv),
        vmem(b_recv), vmem(step_recv), hbm(kernel_x), hbm(kernel_b), hbm(bias), hbm(fading),
    )


def edge_kernel(core_ref, first_ref, edge_ref, he_ref, ho_ref, kx_ref, kb_ref, out_ref):
    n = pl.program_id(0)
    core = core_ref[0]
    even = core == 0
    per_group = first_ref.shape[0]
    blocks = 2 * per_group * pl.num_programs(0)
    none = jnp.zeros((8, WIDE), F32)
    row = lax.broadcasted_iota(jnp.int32, (16, WIDE), 0)

    def from_halo(at, taps):
        halo = jnp.where(even, he_ref[:, at].astype(F32), ho_ref[:, at].astype(F32))[8:]
        return edge_sums(halo, none, taps)[0:3]

    b_sums = from_halo(lanes(blocks + n, STATE), kb_ref[...])
    for j in range(per_group):
        block = 2 * j + core
        x_sums = from_halo(lanes(2 * per_group * n + block), kx_ref[:, lanes(block)])
        rows = edge_ref[j]
        x_conv = silu_of_twice(rows[0:3] + x_sums).astype(BF16).astype(F32)
        b_conv = silu_of_twice(rows[3:6] + b_sums)
        inputs = x_conv * rows[6:9]
        pad = jnp.zeros((13, WIDE), F32)
        inputs = jnp.concatenate([inputs, pad], axis=0).astype(BF16)
        b_conv = jnp.concatenate([b_conv, pad], axis=0).astype(BF16)
        term = lax.dot_general(b_conv, inputs, (((0,), (0,)), ((), ())), preferred_element_type=F32)
        out_ref[j] = (first_ref[j].astype(F32) + term).astype(BF16)


def whole_first(core, first, edge, halo_even, halo_odd, kernel_x, kernel_b):
    groups = kernel_b.shape[1] // STATE
    per_group = first.shape[0] // groups
    width = kernel_x.shape[1] // groups
    out = lambda n, c: (n, 0, 0)
    one = lambda n, c: (0, n)
    return pl.pallas_call(
        edge_kernel,
        grid_spec=pltpu.PrefetchScalarGridSpec(
            num_scalar_prefetch=1,
            grid=(groups,),
            in_specs=[
                pl.BlockSpec((per_group, STATE, WIDE), out),
                pl.BlockSpec((per_group, 16, WIDE), out),
                IN_VMEM,
                IN_VMEM,
                pl.BlockSpec((4, width), one),
                pl.BlockSpec((4, STATE), one),
            ],
            out_specs=pl.BlockSpec((per_group, STATE, WIDE), out),
        ),
        out_shape=pltpu.HBM(first.shape, BF16),
        compiler_params=pltpu.CompilerParams(vmem_limit_bytes=SMALL),
        cost_estimate=pl.CostEstimate(flops=30_000_000, bytes_accessed=3_000_000, transcendentals=10_000),
        name="whole_first",
    )(core, hbm(first), hbm(edge), vmem(halo_even), vmem(halo_odd), hbm(kernel_x), hbm(kernel_b))


def within_kernel(
    core_ref, x_ref, gate_ref, b_ref, c_ref, step_ref, halo_ref, tx_ref, tb_ref, tc_ref,
    kx_ref, kb_ref, kc_ref, bias_ref, fading_ref, a_ref, g_ref, cc_ref, pad, pieces, cum_t, scores, cross, x_step,
):
    k = pl.program_id(0)
    even = core_ref[0] == 0
    heads = step_ref.shape[1]
    half = BLOCK // 2
    steps = pl.num_programs(0)
    blocks = x_ref.shape[1] // WIDE
    group = k // (steps // 2)
    end = slice(BLOCK - 16, BLOCK)

    def prior(halo_at, tail_ref, at):
        halo = halo_ref[:, lanes(halo_at)].astype(F32)
        return jnp.where(even, halo, tail_ref[end, lanes(at)].astype(F32))[8:]

    @pl.when(k == 0)
    def _():
        size, cumulative = steps_of(step_ref[...], bias_ref[...], fading_ref[...])
        cumulative = cumulative * LOG2E
        pieces[0] = jnp.concatenate(split3(cumulative), axis=1)
        pieces[1] = jnp.concatenate(split3(size), axis=1)
        turned = cumulative.T
        for n in range(heads // HB):
            cum_t[n, 0:HB, :] = turned[n * HB : (n + 1) * HB]

    @pl.when(k % (steps // 2) == 0)
    def _():
        in_halo = steps * blocks + group
        b_conv = conv(pad.at[0], prior(in_halo, tb_ref, group), b_ref[...].astype(F32), kb_ref[...])
        c_conv = conv(pad.at[1], prior(in_halo + 2, tc_ref, group), c_ref[...].astype(F32), kc_ref[...])
        cc_ref[...] = c_conv
        products = lax.dot_general(
            c_conv, b_conv, (((1,), (1,)), ((), ())), preferred_element_type=F32
        )
        row = lax.broadcasted_iota(jnp.int32, (half, half), 0)
        col = lax.broadcasted_iota(jnp.int32, (half, half), 1)
        for a in range(2):
            at = slice(a * half, (a + 1) * half)
            scores[at, :] = jnp.where(row >= col, products[at, at], 0.0)
        cross[...] = products[half:, :half].astype(BF16)

    for m in range(blocks):
        block = k * blocks + m
        here = slice(m * WIDE, (m + 1) * WIDE)
        select = spread(3 * heads, WIDE, block * HB, heads)
        cum_wide = jnp.dot(pieces[0], select, preferred_element_type=F32)
        step_wide = jnp.dot(pieces[1], select, preferred_element_type=F32)
        rows = x_ref[:, here].astype(F32)
        x_conv = conv(pad.at[m % 2], prior(block, tx_ref, block), rows, kx_ref[:, here]).astype(F32)
        stepped = x_conv * step_wide
        x_step[m % 2] = stepped.astype(BF16)
        lines = cum_t[block]
        middle = cum_wide[half - 1 : half]
        scaled = (stepped[:half] * jnp.exp2(middle - cum_wide[:half])).astype(BF16)
        late = jnp.dot(cross[...], scaled, preferred_element_type=F32)
        late = late * jnp.exp2(cum_wide[half:] - middle)
        gate = silu_of_twice(gate_ref[:, here].astype(F32) * 0.5)
        g_ref[:, here] = (jnp.exp2(cum_wide) * gate).astype(BF16)
        for a in range(2):
            at = slice(a * half, (a + 1) * half)
            parts = []
            for j in range(HB):
                column = cum_wide[at, j * HEAD_DIM : j * HEAD_DIM + 1]
                line = lines[j : j + 1, at]
                weights = scores[at, :] * jnp.exp2(jnp.minimum(column - line, 0.0))
                parts.append(
                    jnp.dot(
                        weights.astype(BF16),
                        x_step[m % 2, at, j * HEAD_DIM : (j + 1) * HEAD_DIM],
                        preferred_element_type=F32,
                    )
                )
            inside = jnp.concatenate(parts, axis=1)
            if a == 1:
                inside = inside + late
            a_ref[at, here] = (inside * gate[at]).astype(BF16)


def within_block(core, x, gate, b, c, step, halo, x_recv, b_recv, c_recv, kernel_x, kernel_b, kernel_c, bias, fading):
    heads = step.shape[1]
    width = 4 * WIDE
    steps = x.shape[1] // width
    per_group = steps // (b.shape[1] // STATE)
    full = lambda k, s: (0, 0)
    group = lambda k, s: (0, k // per_group)
    one = lambda k, s: (0, k)
    return pl.pallas_call(
        within_kernel,
        grid_spec=pltpu.PrefetchScalarGridSpec(
            num_scalar_prefetch=1,
            grid=(steps,),
            in_specs=[
                pl.BlockSpec((BLOCK, width), one),
                pl.BlockSpec((BLOCK, width), one),
                pl.BlockSpec((BLOCK, STATE), group),
                pl.BlockSpec((BLOCK, STATE), group),
                pl.BlockSpec((BLOCK, heads), full),
                IN_VMEM,
                IN_VMEM,
                IN_VMEM,
                IN_VMEM,
                pl.BlockSpec((4, width), one),
                pl.BlockSpec((4, STATE), group),
                pl.BlockSpec((4, STATE), group),
                pl.BlockSpec((1, heads), full),
                pl.BlockSpec((1, heads), full),
            ],
            out_specs=[
                pl.BlockSpec((BLOCK, width), one),
                pl.BlockSpec((BLOCK, width), one),
                pl.BlockSpec((BLOCK, STATE), group),
            ],
            scratch_shapes=[
                pltpu.VMEM((2, BLOCK + 8, WIDE), F32),
                pltpu.VMEM((2, BLOCK, 3 * heads), BF16),
                pltpu.VMEM((heads // HB, 8, BLOCK), F32),
                pltpu.VMEM((BLOCK, BLOCK // 2), F32),
                pltpu.VMEM((BLOCK // 2, BLOCK // 2), BF16),
                pltpu.VMEM((2, BLOCK, WIDE), BF16),
            ],
        ),
        out_shape=[
            jax.ShapeDtypeStruct(x.shape, BF16),
            jax.ShapeDtypeStruct(x.shape, BF16),
            jax.ShapeDtypeStruct(c.shape, BF16),
        ],
        compiler_params=pltpu.CompilerParams(vmem_limit_bytes=VMEM),
        cost_estimate=pl.CostEstimate(flops=8_000_000_000, bytes_accessed=12_000_000, transcendentals=6_000_000),
        name="within_block",
    )(
        core, hbm(x), hbm(gate), hbm(b), hbm(c), hbm(step), vmem(halo), vmem(x_recv), vmem(b_recv),
        vmem(c_recv), hbm(kernel_x), hbm(kernel_b), hbm(kernel_c), hbm(bias), hbm(fading),
    )


def scan_kernel(gathered_ref, _, starts_ref, final_ref, decays, inputs, b_rows):
    chips, part, _ = starts_ref.shape
    r = pl.program_id(0)

    @pl.when(r == 0)
    def _():
        extra = [gathered_ref[n, STATE : STATE + 16, :].astype(F32) for n in range(chips)]
        packed = jnp.concatenate([value[0:1] for value in extra], axis=0).astype(BF16)
        row = lax.broadcasted_iota(jnp.int32, (WIDE, WIDE), 0)
        col = lax.broadcasted_iota(jnp.int32, (WIDE, WIDE), 1)
        wide = [
            jnp.dot(packed, (row == col // HEAD_DIM * HEAD_DIM + 8 * q).astype(BF16), preferred_element_type=F32)
            for q in range(6)
        ]
        decays[...] = wide[0] + wide[1] + wide[2]
        pad = jnp.zeros((13, WIDE), F32)
        for n in range(chips):
            x_sums, b_sums = extra[n][1:4], extra[n][7:10]
            if n:
                x_sums = x_sums + extra[n - 1][4:7]
                b_sums = b_sums + extra[n - 1][10:13]
            x_conv = silu_of_twice(x_sums).astype(BF16).astype(F32)
            weight = jnp.concatenate([wide[3 + t][n : n + 1] for t in range(3)], axis=0)
            inputs[n] = jnp.concatenate([x_conv * weight, pad], axis=0).astype(BF16)
            b_rows[n] = jnp.concatenate([silu_of_twice(b_sums), pad], axis=0).astype(BF16)

    rows = pl.ds(pl.multiple_of(r * part, part), part)
    state = jnp.zeros((part, WIDE), F32)
    for n in range(chips):
        starts_ref[n] = state.astype(BF16)
        term = lax.dot_general(
            b_rows[n, :, rows], inputs[n], (((0,), (0,)), ((), ())), preferred_element_type=F32
        )
        state = state * decays[n : n + 1, :] + (gathered_ref[n, rows, :].astype(F32) + term)
    final_ref[rows, :] = state


def scan_states(gathered, after):
    chips = gathered.shape[0]
    part = STATE // 2
    return pl.pallas_call(
        scan_kernel,
        grid=(2,),
        in_specs=[IN_VMEM, IN_HBM],
        out_specs=[pl.BlockSpec((chips, part, WIDE), lambda r: (0, r, 0)), IN_VMEM],
        out_shape=[
            pltpu.HBM((chips, STATE, WIDE), BF16),
            pltpu.VMEM((STATE, WIDE), F32),
        ],
        scratch_shapes=[
            pltpu.VMEM((chips, WIDE), F32),
            pltpu.VMEM((chips, 16, WIDE), BF16),
            pltpu.VMEM((chips, 16, STATE), BF16),
        ],
        compiler_params=pltpu.CompilerParams(vmem_limit_bytes=SMALL),
        cost_estimate=pl.CostEstimate(flops=20_000_000, bytes_accessed=2_500_000, transcendentals=0),
        name="scan_states",
    )(vmem(gathered), hbm(after))


def start_kernel(core_ref, start_ref, first_ref, decay_ref, _, keep_ref, send_ref):
    even = core_ref[0] == 0
    for j in range(first_ref.shape[0]):
        n = pl.program_id(0) * first_ref.shape[0] + j
        start = start_ref[n].astype(F32)
        later = start * decay_ref[j, 0:1, :] + first_ref[j].astype(F32)
        keep_ref[n] = jnp.where(even, start, later).astype(BF16)
        send_ref[n] = jnp.where(even, later, start).astype(BF16)


def block_starts(core, chip_start, first_update, first_decay, after):
    shape = pltpu.VMEM(chip_start.shape, BF16)
    return pl.pallas_call(
        start_kernel,
        grid=(chip_start.shape[0] // 2,),
        in_specs=[
            pl.BlockSpec(memory_space=pltpu.SMEM),
            IN_VMEM,
            pl.BlockSpec((2, STATE, WIDE), lambda i: (i, 0, 0)),
            pl.BlockSpec((2, 8, WIDE), lambda i: (i, 0, 0)),
            IN_HBM,
        ],
        out_specs=[IN_VMEM, IN_VMEM],
        out_shape=[shape, shape],
        compiler_params=pltpu.CompilerParams(vmem_limit_bytes=SMALL),
        cost_estimate=pl.CostEstimate(flops=2_000_000, bytes_accessed=4_500_000, transcendentals=0),
        name="block_starts",
    )(core, vmem(chip_start), hbm(first_update), hbm(first_decay), hbm(after))


def finish_kernel(core_ref, a_ref, g_ref, cc_ref, keep_ref, recv_ref, gain_ref, out_ref, y_ref):
    core = core_ref[0]
    rows, width = out_ref.shape
    n, r = pl.program_id(0), pl.program_id(1)
    at_rows = pl.ds(pl.multiple_of(r * rows, rows), rows)
    per_group = keep_ref.shape[0] // pl.num_programs(0)
    total = jnp.zeros((rows, 1), F32)
    c_conv = cc_ref[at_rows, pl.ds(pl.multiple_of(n * STATE, STATE), STATE)]
    for j in range(per_group):
        for state_ref, parity in ((keep_ref, core), (recv_ref, 1 - core)):
            block = 2 * j + parity
            at = pl.ds(pl.multiple_of(n * width + block * WIDE, WIDE), WIDE)
            carried = jnp.dot(c_conv, state_ref[n * per_group + j], preferred_element_type=F32)
            y = a_ref[at_rows, at].astype(F32) + carried * g_ref[at_rows, at].astype(F32)
            y_ref[:, pl.ds(pl.multiple_of(block * WIDE, WIDE), WIDE)] = y
            total = total + jnp.sum(y * y, axis=1, keepdims=True)
    inverse = 1.0 / jnp.sqrt(total / width + epsilon)
    out_ref[...] = (y_ref[...] * inverse * gain_ref[...]).astype(BF16)


def finish(core, a, g, cc, keep, recv, gain):
    tokens, channels = a.shape
    groups = cc.shape[1] // STATE
    width = channels // groups
    rows = tokens // 2
    return pl.pallas_call(
        finish_kernel,
        grid=(groups, 2),
        in_specs=[
            pl.BlockSpec(memory_space=pltpu.SMEM),
            IN_VMEM,
            IN_VMEM,
            IN_VMEM,
            IN_VMEM,
            IN_VMEM,
            pl.BlockSpec((1, width), lambda n, r: (0, n)),
        ],
        out_specs=pl.BlockSpec((rows, width), lambda n, r: (r, n)),
        scratch_shapes=[pltpu.VMEM((rows, width), F32)],
        out_shape=jax.ShapeDtypeStruct((tokens, channels), BF16),
        compiler_params=pltpu.CompilerParams(vmem_limit_bytes=SMALL),
        cost_estimate=pl.CostEstimate(flops=600_000_000, bytes_accessed=9_000_000, transcendentals=1000),
        name="finish",
    )(core, vmem(a), vmem(g), vmem(cc), vmem(keep), vmem(recv), gain)


def slots_kernel(owners_ref, rank_ref, state_ref, o0, o1, o2, o3):
    outs = (o0, o1, o2, o3)
    for out in outs:
        out[...] = jnp.zeros(out.shape, F32)
    for j in range(HB):
        owner = owners_ref[j]
        slot = jnp.int32(0)
        for i in range(j):
            slot = slot + (owners_ref[i] == owner).astype(jnp.int32)
        piece = state_ref[:, j * HEAD_DIM : (j + 1) * HEAD_DIM].T
        for d, out in enumerate(outs):
            for r in range(out.shape[0]):

                @pl.when((owner == rank_ref[0] ^ d) & (slot == r))
                def _(out=out, r=r, piece=piece):
                    out[r] = piece


def final_slots(owners, rank, state, dests, capacity):
    one = pltpu.VMEM((capacity, HEAD_DIM, STATE), F32)
    smem = pl.BlockSpec(memory_space=pltpu.SMEM)
    return pl.pallas_call(
        slots_kernel,
        in_specs=[smem, smem, IN_VMEM],
        out_specs=[IN_VMEM] * dests,
        out_shape=[one] * dests,
        compiler_params=pltpu.CompilerParams(vmem_limit_bytes=SMALL),
        name="final_slots",
    )(owners, rank, vmem(state))


def local(
    x_input, b_input, output_projection_input, step_input, gate_input, kernel_x, kernel_b, kernel_c,
    step_bias, fading_logarithm, norm_gain, owner_map,
):
    ctx_count = lax.axis_size("ctx")
    ctx_rank = lax.axis_index("ctx")
    dec_count = lax.axis_size("dec")
    dec_rank = lax.axis_index("dec")
    core = ctx_rank % 2
    core_arg = core.astype(jnp.int32).reshape(1)
    x = x_input[0]
    b = b_input[0]
    c = output_projection_input[0]
    step = step_input[0]
    bias = step_bias.reshape(1, -1)
    fading = fading_logarithm.reshape(1, -1)

    swap = [(i, i ^ 1) for i in range(ctx_count)]
    x_recv, b_recv, step_recv = (
        lax.ppermute(x, "ctx", swap),
        lax.ppermute(b, "ctx", swap),
        lax.ppermute(step, "ctx", swap),
    )
    *own, tail = own_updates(core_arg, x, b, c, step, kernel_x, kernel_b, bias, fading)
    tail, step_recv = lax.optimization_barrier((tail, step_recv))
    from_even = lax.ppermute(tail, "ctx", [(i, i + 1) for i in range(1, ctx_count - 1, 2)])
    updates, first_update, first_decay, edge = chip_updates(
        core_arg, own, x, b, x_recv, b_recv, step_recv, kernel_x, kernel_b, bias, fading
    )
    c_recv = lax.ppermute(c, "ctx", swap)
    from_odd = lax.ppermute(from_even, "ctx", swap)
    updates, from_even = lax.optimization_barrier((updates, from_even))
    same_core = [[2 * i + j for i in range(ctx_count // 2)] for j in range(2)]
    gathered = lax.all_to_all(updates, "ctx", 0, 0, axis_index_groups=same_core, tiled=True)
    a, g, cc = within_block(
        core_arg, x, gate_input[0], b, c, step, from_even, x_recv, b_recv, c_recv,
        kernel_x, kernel_b, kernel_c, bias, fading,
    )
    first_update = whole_first(core_arg, first_update, edge, from_even, from_odd, kernel_x, kernel_b)
    starts, state = scan_states(gathered, cc)
    chip_start = lax.all_to_all(starts, "ctx", 0, 0, axis_index_groups=same_core, tiled=True)

    owners = lax.dynamic_slice_in_dim(owner_map[0, :, 0], ctx_rank * HB, HB)
    outgoing = final_slots(owners, dec_rank.astype(jnp.int32).reshape(1), state, dec_count, 2)
    arrived = jnp.zeros((dec_count,) + outgoing[0].shape, F32)
    for d in range(dec_count):
        piece = outgoing[d]
        if d:
            piece = lax.ppermute(piece, "dec", [(i, i ^ d) for i in range(dec_count)])
        arrived = lax.dynamic_update_index_in_dim(arrived, piece, dec_rank ^ d, 0)

    keep, send = block_starts(core_arg, chip_start, first_update, first_decay, arrived)
    recv = lax.ppermute(send, "ctx", swap)
    mixer_rows = finish(core_arg, a, g, cc, keep, recv, norm_gain.reshape(1, -1))
    return (mixer_rows[None], arrived[None, :, None])


def solution(mesh):
    return jax.shard_map(
        local,
        mesh=mesh,
        in_specs=(
            P("dec", "ctx", "tp"),
            P("dec", "ctx", "tp"),
            P("dec", "ctx", "tp"),
            P("dec", "ctx", "tp"),
            P("dec", "ctx", "tp"),
            P(None, "tp"),
            P(None, "tp"),
            P(None, "tp"),
            P("tp"),
            P("tp"),
            P("tp"),
            P("dec", "tp", None),
        ),
        out_specs=(P("dec", "ctx", "tp"), P("dec", None, ("tp", "ctx"), None, None, None)),
        check_vma=False,
    )
```

time: 117 us -> 102 us (0.87)
  waiting for transfers between devices: 38.9 us -> 29.8 us
  Pallas kernels: 42.9 us -> 38.4 us
  local copies, waits for them, and re-layouts: 5.52 us -> 10 us
  starting transfers between devices: 26.3 us -> 22.1 us
  other arithmetic: 1.35 us -> 0 us
    all_to_all x1, waiting for transfers between devices: 16 us -> 9.32 us  [local(): lax.all_to_all(starts, 'ctx', 0, 0, axis_index_groups=same_core, tiled=True)]
    pallas_call x1, Pallas kernels: 18.2 us -> 14.2 us  [within_block(): pl.pallas_call(within_kernel, grid_spec=pltpu.PrefetchScalarGridSpec(num_...]
    ppermute x2, starting transfers between devices: 3.64 us -> 0.57 us  [the longest x1 0.48 us: local(): from_odd = lax.ppermute(from_even, 'ctx', swap)]
    ppermute x3, waiting for transfers between devices: 8.32 us -> 5.5 us  [local(): piece = lax.ppermute(piece, 'dec', [(i, i ^ d) for i in range(dec_count)])]
    dynamic_update_slice x3 -> x4, local copies, waits for them, and re-layouts: 0.04 us -> 2.66 us  [local(): arrived = lax.dynamic_update_index_in_dim(arrived, piece, dec_rank ^ d, 0)]
    all_to_all x1, starting transfers between devices: 8.8 us -> 7.43 us  [local(): lax.all_to_all(updates, 'ctx', 0, 0, axis_index_groups=same_core, tiled=T...]
    unnamed x31 -> x27, local copies, waits for them, and re-layouts: 5.19 us -> 6.46 us
    pallas_call x5 -> x7, Pallas kernels: 24.7 us -> 24.3 us  [the longest x1 7.65 us: chip_updates(): pl.pallas_call(chip_kernel, grid_spec=pltpu.PrefetchScalarGridSpec(num_sc...]
  transfers between devices with their start and end apart: 12 -> 12, of which waited for: 8 -> 7; matrix products, arithmetic and copies ran while one was open for 2% -> 4% of each run, Pallas kernels for 17% -> 30%
where the time goes in v2:
time: 102 us; the launch traced here: 101 us
  Pallas kernels  38.4 us (38%)
  waiting for transfers between devices  29.8 us (29%)
  starting transfers between devices  22.1 us (22%)
  local copies, waits for them, and re-layouts  10 us (10%)
    pallas_call x1, Pallas kernels, within_block(): pl.pallas_call(within_kernel, grid_spec=pltpu.PrefetchScalarGridSpec(num_...  14.2 us
    all_to_all x1, waiting for transfers between devices, local(): lax.all_to_all(updates, 'ctx', 0, 0, axis_index_groups=same_core, tiled=T...  9.89 us
    all_to_all x1, waiting for transfers between devices, local(): lax.all_to_all(starts, 'ctx', 0, 0, axis_index_groups=same_core, tiled=True)  9.32 us
    pallas_call x1, Pallas kernels, chip_updates(): pl.pallas_call(chip_kernel, grid_spec=pltpu.PrefetchScalarGridSpec(num_sc...  7.65 us
    all_to_all x1, starting transfers between devices, local(): lax.all_to_all(updates, 'ctx', 0, 0, axis_index_groups=same_core, tiled=T...  7.43 us
    unnamed x27, local copies, waits for them, and re-layouts  6.46 us
    ppermute x3, waiting for transfers between devices, local(): piece = lax.ppermute(piece, 'dec', [(i, i ^ d) for i in range(dec_count)])  5.5 us
    pallas_call x1, Pallas kernels, own_updates(): pl.pallas_call(own_kernel, grid_spec=pltpu.PrefetchScalarGridSpec(num_sca...  4.77 us
  transfers between devices with their start and end apart: 12, of which 7 were waited for; matrix products, arithmetic and copies ran while one was open for 4% of the time, Pallas kernels for 30%

profile of v2, /device:TPU:1, one launch (start us, length us, event | category | flops | bytes accessed | tf_op | source)
XLA Modules:
  0.0 101.2 jit_solution(14309276498262592997)
XLA Ops:
  0.6 0.0 copy-start
  0.6 3.3 %collective-permute-start = (bf16[256,4096]{1,0:T(8,128)(2,1)}, bf16[256,4096]{1,0:T(8,128)(2,1)S(1)}, u32[]{:S(2)}, u32[]{:S(2)}) collective-permute-start(bf16[256,4096]{1,0:T(8,128)(2,1)} %bitcast.25), channel_id=1, source_target_pairs={{0,16},{16,0},{32,48},{48,32},{64,80},{80,64},{96,112},{112,96},{1... | collective-permute-start | bytes 6291464 | tf_op jit(solution)/shard_map/ppermute | solution.py:723
  4.0 0.1 collective-permute-start.1
  4.1 0.9 copy.14
  4.9 0.0 copy-start.11
  5.0 0.5 collective-permute-start.2
  5.5 0.1 copy-done.11
  5.6 4.8 %own_updates.1 = (f32[8,256,256]{2,1,0:T(8,128)S(1)}, bf16[16,128]{1,0:T(8,128)(2,1)S(1)}, f32[8,64]{1,0:T(8,128)S(1)}, bf16[16,5120]{1,0:T(8,128)(2,1)S(1)}) custom-call(s32[1]{0:T(128)} %bitcast.core_ref, bf16[256,4096]{1,0:T(8,128)(2,1)} %bitcast.26, bf16[256,512]{1,0:T(8,128)(2,1)} %bitcast.31, bf16[256,512]{1,0:T(8,128)(2,1)} %bitcast.39, ...), custom_call_target="tpu_custom_call" | custom-call | flops 300000000 | bytes 10000000 | tf_op jit(solution)/shard_map/own_updates/pallas_call | solution.py:146
  10.4 0.0 collective-permute-done.2.sr_ref
  10.4 2.1 %collective-permute-start.3 = (bf16[16,5120]{1,0:T(8,128)(2,1)S(1)}, bf16[16,5120]{1,0:T(8,128)(2,1)S(1)}, u32[]{:S(2)}, u32[]{:S(2)}) collective-permute-start(bf16[16,5120]{1,0:T(8,128)(2,1)S(1)} %get-tuple-element.31), channel_id=1, source_target_pairs={{16,32},{48,64},{80,96},{112,128},{144,160},{176,192},{208,224},{1... | collective-permute-start | bytes 491528 | tf_op jit(solution)/shard_map/ppermute | solution.py:729
  12.5 0.0 collective-permute-done.1.br_ref.tb_ref
  12.5 0.0 collective-permute-done.xr_ref.tx_ref
  12.5 0.0 copy-start.3
  12.5 7.7 %chip_updates.1 = (bf16[8,272,256]{2,1,0:T(8,128)(2,1)}, bf16[8,256,256]{2,1,0:T(8,128)(2,1)}, f32[8,8,256]{2,1,0:T(8,128)}, f32[8,16,256]{2,1,0:T(8,128)}) custom-call(s32[1]{0:T(128)} %bitcast.core_ref, f32[8,256,256]{2,1,0:T(8,128)S(1)} %get-tuple-element.25.u_own_ref, bf16[16,128]{1,0:T(8,128)(2,1)S(1)} %get-tuple-element.26.first_weight_ref, ...), custom_call_target="tpu_custom_call" | custom-call | flops 300000000 | bytes 10000000 | tf_op jit(solution)/shard_map/chip_updates/pallas_call | solution.py:293
  20.2 0.0 copy-done.3
  20.2 0.0 copy-start.12
  20.2 0.0 collective-permute-done.3.halo_ref.he_ref
  20.2 0.0 copy-start.7
  20.2 7.4 %all-to-all-start = ((bf16[8,272,256]{2,1,0:T(8,128)(2,1)}), bf16[8,272,256]{2,1,0:T(8,128)(2,1)S(1)}, u32[]{:S(2)}, u32[]{:S(2)}) async-start(bf16[8,272,256]{2,1,0:T(8,128)(2,1)} %get-tuple-element.36), calls=%async_computation | async-start | bytes 2228224 | tf_op jit(solution)/shard_map/all_to_all | solution.py:737
  27.6 0.0 copy-done.12
  27.6 0.1 collective-permute-start.4
  27.7 1.5 %collective-permute-done.4.tc_ref = bf16[256,512]{1,0:T(8,128)(2,1)S(1)} collective-permute-done((bf16[256,512]{1,0:T(8,128)(2,1)S(1)}, bf16[256,512]{1,0:T(8,128)(2,1)S(1)}, u32[]{:S(2)}, u32[]{:S(2)}) %collective-permute-start.4) | collective-permute-done | bytes 262176 | tf_op jit(solution)/shard_map/ppermute | solution.py:733
  29.3 0.0 copy-done.7
  29.3 0.0 copy-start.4
  29.3 1.6 %copy-done.4 = bf16[256,4096]{1,0:T(8,128)(2,1)S(1)} copy-done((bf16[256,4096]{1,0:T(8,128)(2,1)S(1)}, bf16[256,4096]{1,0:T(8,128)(2,1)}, u32[]{:S(2)}) %copy-start.4) | copy-done | bytes 2097176
  30.9 0.0 copy-start.8
  30.9 0.9 copy-done.8
  31.8 14.2 %within_block.1 = (bf16[256,4096]{1,0:T(8,128)(2,1)S(1)}, bf16[256,4096]{1,0:T(8,128)(2,1)S(1)}, bf16[256,512]{1,0:T(8,128)(2,1)S(1)}) custom-call(s32[1]{0:T(128)} %bitcast.core_ref, bf16[256,4096]{1,0:T(8,128)(2,1)} %bitcast.29, bf16[256,4096]{1,0:T(8,128)(2,1)} %bitcast.48, bf16[256,512]{1,0:T(8,128)(2,1)} %bitcast.34, bf16[256,512]{1,0:T(8,128)(2,1)} %bitcast.40, ...), custom_call_target="tpu_custom_call" | custom-call | flops 8000000000 | bytes 12000000 | tf_op jit(solution)/shard_map/within_block/pallas_call | solution.py:488
  45.9 0.0 copy-start.1
  46.0 1.3 %copy-done.1 = bf16[256,4096]{1,0:T(8,128)(2,1)} copy-done((bf16[256,4096]{1,0:T(8,128)(2,1)}, bf16[256,4096]{1,0:T(8,128)(2,1)S(1)}, u32[]{:S(2)}) %copy-start.1) | copy-done | bytes 2097176
  47.3 0.0 copy-start.5
  47.3 0.7 copy-done.5
  48.0 9.9 %all-to-all-done.gathered_ref = bf16[8,272,256]{2,1,0:T(8,128)(2,1)S(1)} async-done(((bf16[8,272,256]{2,1,0:T(8,128)(2,1)}), bf16[8,272,256]{2,1,0:T(8,128)(2,1)S(1)}, u32[]{:S(2)}, u32[]{:S(2)}) %all-to-all-start) | async-done | bytes 1114144 | tf_op jit(solution)/shard_map/all_to_all | solution.py:737
  57.8 1.8 %scan_states.1 = (bf16[8,256,256]{2,1,0:T(8,128)(2,1)}, f32[256,256]{1,0:T(8,128)S(1)}) custom-call(bf16[8,272,256]{2,1,0:T(8,128)(2,1)S(1)} %all-to-all-done.gathered_ref, bf16[256,512]{1,0:T(8,128)(2,1)} %copy-done.5), custom_call_target="tpu_custom_call" | custom-call | flops 20000000 | bytes 2500000 | tf_op jit(solution)/shard_map/scan_states/pallas_call | solution.py:577
  59.6 3.6 %all-to-all-start.1 = ((bf16[8,256,256]{2,1,0:T(8,128)(2,1)}), bf16[8,256,256]{2,1,0:T(8,128)(2,1)S(1)}, u32[]{:S(2)}, u32[]{:S(2)}) async-start(bf16[8,256,256]{2,1,0:T(8,128)(2,1)} %get-tuple-element.37), calls=%async_computation.1 | async-start | bytes 2097152 | tf_op jit(solution)/shard_map/all_to_all | solution.py:744
  63.2 0.5 collective-permute-start.5
  63.7 0.0 copy-done
  63.7 0.1 fusion.owners_ref
  63.7 1.3 %collective-permute-done.5.ho_ref = bf16[16,5120]{1,0:T(8,128)(2,1)} collective-permute-done((bf16[16,5120]{1,0:T(8,128)(2,1)}, bf16[16,5120]{1,0:T(8,128)(2,1)}, u32[]{:S(2)}, u32[]{:S(2)}) %collective-permute-start.5) | collective-permute-done | bytes 163872 | tf_op jit(solution)/shard_map/ppermute | solution.py:734
  65.0 0.0 copy-start.9
  65.0 0.9 copy-done.9
  66.0 2.9 %whole_first.1.first_ref = bf16[8,256,256]{2,1,0:T(8,128)(2,1)} custom-call(s32[1]{0:T(128)} %bitcast.core_ref, bf16[8,256,256]{2,1,0:T(8,128)(2,1)} %get-tuple-element.38.first_ref, f32[8,16,256]{2,1,0:T(8,128)} %get-tuple-element.39.edge_ref, bf16[16,5120]{1,0:T(8,128)(2,1)S(1)} %copy-done.9, bf16[16,5120]{1,0:T(8,128)(2,1)} %collective-permute-done.5.ho_ref, ...), custom_call_target="tpu_custom_call" | custom-call | flops 30000000 | bytes 3000000 | tf_op jit(solution)/shard_map/whole_first/pallas_call | solution.py:378
  68.8 1.3 %final_slots.1 = (f32[2,64,256]{2,1,0:T(8,128)S(1)}, f32[2,64,256]{2,1,0:T(8,128)S(1)}, f32[2,64,256]{2,1,0:T(8,128)S(1)}, f32[2,64,256]{2,1,0:T(8,128)S(1)}) custom-call(s32[4]{0:T(128)S(1)} %fusion.owners_ref, s32[1]{0:T(128)} %bitcast.9.rank_ref, f32[256,256]{1,0:T(8,128)S(1)} %get-tuple-element.41.state_ref), custom_call_target="tpu_custom_call" | custom-call | tf_op jit(solution)/shard_map/final_slots/pallas_call | solution.py:694
  70.1 1.3 %collective-permute-start.6 = (f32[2,64,256]{2,1,0:T(8,128)S(1)}, f32[2,64,256]{2,1,0:T(8,128)S(1)}, u32[]{:S(2)}, u32[]{:S(2)}) collective-permute-start(f32[2,64,256]{2,1,0:T(8,128)S(1)} %get-tuple-element.43), channel_id=1, source_target_pairs={{0,1},{1,0},{2,3},{3,2},{4,5},{5,4},{6,7},{7,6},{8,9},{9,8},{10,11... | collective-permute-start | bytes 393224 | tf_op jit(solution)/shard_map/ppermute | solution.py:752
  71.4 2.4 %collective-permute-start.7 = (f32[2,64,256]{2,1,0:T(8,128)S(1)}, f32[2,64,256]{2,1,0:T(8,128)S(1)}, u32[]{:S(2)}, u32[]{:S(2)}) collective-permute-start(f32[2,64,256]{2,1,0:T(8,128)S(1)} %get-tuple-element.44), channel_id=1, source_target_pairs={{0,2},{1,3},{2,0},{3,1},{4,6},{5,7},{6,4},{7,5},{8,10},{9,11},{10,... | collective-permute-start | bytes 393224 | tf_op jit(solution)/shard_map/ppermute | solution.py:752
  73.8 0.2 collective-permute-start.8
  74.1 0.0 copy-start.6
  74.1 0.8 broadcast_in_dim.22
  74.9 0.7 bitcast_dynamic-update-slice_fusion.3
  75.6 0.0 collective-permute-done.6
  75.6 0.7 bitcast_dynamic-update-slice_fusion.2
  76.3 3.7 %collective-permute-done.7 = f32[2,64,256]{2,1,0:T(8,128)S(1)} collective-permute-done((f32[2,64,256]{2,1,0:T(8,128)S(1)}, f32[2,64,256]{2,1,0:T(8,128)S(1)}, u32[]{:S(2)}, u32[]{:S(2)}) %collective-permute-start.7) | collective-permute-done | bytes 131104 | tf_op jit(solution)/shard_map/ppermute | solution.py:752
  79.9 0.7 bitcast_dynamic-update-slice_fusion.1
  80.6 1.8 %collective-permute-done.8 = f32[2,64,256]{2,1,0:T(8,128)S(1)} collective-permute-done((f32[2,64,256]{2,1,0:T(8,128)S(1)}, f32[2,64,256]{2,1,0:T(8,128)S(1)}, u32[]{:S(2)}, u32[]{:S(2)}) %collective-permute-start.8) | collective-permute-done | bytes 131104 | tf_op jit(solution)/shard_map/ppermute | solution.py:752
  82.4 0.7 bitcast_dynamic-update-slice_fusion._
  83.1 9.3 %all-to-all-done.1.start_ref = bf16[8,256,256]{2,1,0:T(8,128)(2,1)S(1)} async-done(((bf16[8,256,256]{2,1,0:T(8,128)(2,1)}), bf16[8,256,256]{2,1,0:T(8,128)(2,1)S(1)}, u32[]{:S(2)}, u32[]{:S(2)}) %all-to-all-start.1) | async-done | bytes 1048608 | tf_op jit(solution)/shard_map/all_to_all | solution.py:744
  92.4 0.0 copy-start.2
  92.4 2.5 %block_starts.1 = (bf16[8,256,256]{2,1,0:T(8,128)(2,1)S(1)}, bf16[8,256,256]{2,1,0:T(8,128)(2,1)S(1)}) custom-call(s32[1]{0:T(128)} %bitcast.core_ref, bf16[8,256,256]{2,1,0:T(8,128)(2,1)S(1)} %all-to-all-done.1.start_ref, bf16[8,256,256]{2,1,0:T(8,128)(2,1)} %whole_first.1.first_ref, f32[8,8,256]{2,1,0:T(8,128)} %get-tuple-element.40.decay_ref, ...), custom_call_target="tpu_custom_call" | custom-call | flops 2000000 | bytes 4500000 | tf_op jit(solution)/shard_map/block_starts/pallas_call | solution.py:609
  94.9 0.6 collective-permute-start.9
  95.5 2.3 %collective-permute-done.9.recv_ref = bf16[8,256,256]{2,1,0:T(8,128)(2,1)S(1)} collective-permute-done((bf16[8,256,256]{2,1,0:T(8,128)(2,1)S(1)}, bf16[8,256,256]{2,1,0:T(8,128)(2,1)S(1)}, u32[]{:S(2)}, u32[]{:S(2)}) %collective-permute-start.9) | collective-permute-done | bytes 1048608 | tf_op jit(solution)/shard_map/ppermute | solution.py:756
  97.8 0.0 copy-done.6
  97.8 0.0 copy-done.10
  97.8 0.0 copy-done.2
  97.8 3.4 %finish.1 = bf16[256,4096]{1,0:T(8,128)(2,1)} custom-call(s32[1]{0:T(128)} %bitcast.core_ref, bf16[256,4096]{1,0:T(8,128)(2,1)S(1)} %get-tuple-element.33.a_ref, bf16[256,4096]{1,0:T(8,128)(2,1)S(1)} %copy-done.2, bf16[256,512]{1,0:T(8,128)(2,1)S(1)} %copy-done.6, bf16[8,256,256]{2,1,0:T(8,128)(2,1)S(1)} %get-tuple-element.46.keep_ref, ...), custom_call_target="tpu_custom_call" | custom-call | flops 600000000 | bytes 9000000 | tf_op jit(solution)/shard_map/finish/pallas_call | solution.py:652
  (1 shorter events, 0.0 us)
Async XLA Ops:
  0.6 63.0 %copy-start = (s32[1,64,1]{1,2,0:T(1,128)S(1)}, s32[1,64,1]{1,2,0:T(1,128)}, u32[]{:S(2)}) copy-start(s32[1,64,1]{1,2,0:T(1,128)} %param.23) | copy-start | bytes 772
  0.6 11.8 %collective-permute-start = (bf16[256,4096]{1,0:T(8,128)(2,1)}, bf16[256,4096]{1,0:T(8,128)(2,1)S(1)}, u32[]{:S(2)}, u32[]{:S(2)}) collective-permute-start(bf16[256,4096]{1,0:T(8,128)(2,1)} %bitcast.25), channel_id=1, source_target_pairs={{0,16},{16,0},{32,48},{48,32},{64,80},{80,64},{96,112},{112,96},{1... | collective-permute-start | bytes 6291464 | tf_op jit(solution)/shard_map/ppermute | solution.py:723
  4.0 8.5 %collective-permute-start.1 = (bf16[256,512]{1,0:T(8,128)(2,1)}, bf16[256,512]{1,0:T(8,128)(2,1)S(1)}, u32[]{:S(2)}, u32[]{:S(2)}) collective-permute-start(bf16[256,512]{1,0:T(8,128)(2,1)} %bitcast.30), channel_id=1, source_target_pairs={{0,16},{16,0},{32,48},{48,32},{64,80},{80,64},{96,112},{112,96},{1... | collective-permute-start | bytes 786440 | tf_op jit(solution)/shard_map/ppermute | solution.py:724
  4.9 0.6 copy-start.11
  5.0 5.4 %collective-permute-start.2 = (bf16[256,64]{1,0:T(8,128)(2,1)S(1)}, bf16[256,64]{1,0:T(8,128)(2,1)S(1)}, u32[]{:S(2)}, u32[]{:S(2)}) collective-permute-start(bf16[256,64]{1,0:T(8,128)(2,1)S(1)} %bitcast.36), channel_id=1, source_target_pairs={{0,16},{16,0},{32,48},{48,32},{64,80},{80,64},{96,112},{112,96},{1... | collective-permute-start | bytes 98312 | tf_op jit(solution)/shard_map/ppermute | solution.py:725
  10.4 9.8 %collective-permute-start.3 = (bf16[16,5120]{1,0:T(8,128)(2,1)S(1)}, bf16[16,5120]{1,0:T(8,128)(2,1)S(1)}, u32[]{:S(2)}, u32[]{:S(2)}) collective-permute-start(bf16[16,5120]{1,0:T(8,128)(2,1)S(1)} %get-tuple-element.31), channel_id=1, source_target_pairs={{16,32},{48,64},{80,96},{112,128},{144,160},{176,192},{208,224},{1... | collective-permute-start | bytes 491528 | tf_op jit(solution)/shard_map/ppermute | solution.py:729
  12.5 7.7 %copy-start.3 = (bf16[256,4096]{1,0:T(8,128)(2,1)}, bf16[256,4096]{1,0:T(8,128)(2,1)S(1)}, u32[]{:S(2)}) copy-start(bf16[256,4096]{1,0:T(8,128)(2,1)S(1)} %collective-permute-done.xr_ref.tx_ref) | copy-start | bytes 6291460
  20.2 7.5 %copy-start.12 = (bf16[1,256,512]{2,1,0:T(8,128)(2,1)S(1)}, bf16[1,256,512]{2,1,0:T(8,128)(2,1)}, u32[]{:S(2)}) copy-start(bf16[1,256,512]{2,1,0:T(8,128)(2,1)} %param.14) | copy-start | bytes 786436
  20.2 9.1 %copy-start.7 = (bf16[16,5120]{1,0:T(8,128)(2,1)}, bf16[16,5120]{1,0:T(8,128)(2,1)S(1)}, u32[]{:S(2)}) copy-start(bf16[16,5120]{1,0:T(8,128)(2,1)S(1)} %collective-permute-done.3.halo_ref.he_ref) | copy-start | bytes 491524
  20.2 37.6 %all-to-all-start = ((bf16[8,272,256]{2,1,0:T(8,128)(2,1)}), bf16[8,272,256]{2,1,0:T(8,128)(2,1)S(1)}, u32[]{:S(2)}, u32[]{:S(2)}) async-start(bf16[8,272,256]{2,1,0:T(8,128)(2,1)} %get-tuple-element.36), calls=%async_computation | async-start | bytes 2228224 | tf_op jit(solution)/shard_map/all_to_all | solution.py:737
  27.6 1.6 %collective-permute-start.4 = (bf16[256,512]{1,0:T(8,128)(2,1)S(1)}, bf16[256,512]{1,0:T(8,128)(2,1)S(1)}, u32[]{:S(2)}, u32[]{:S(2)}) collective-permute-start(bf16[256,512]{1,0:T(8,128)(2,1)S(1)} %bitcast.41), channel_id=1, source_target_pairs={{0,16},{16,0},{32,48},{48,32},{64,80},{80,64},{96,112},{112,96},{1... | collective-permute-start | bytes 786440 | tf_op jit(solution)/shard_map/ppermute | solution.py:733
  29.3 1.6 %copy-start.4 = (bf16[256,4096]{1,0:T(8,128)(2,1)S(1)}, bf16[256,4096]{1,0:T(8,128)(2,1)}, u32[]{:S(2)}) copy-start(bf16[256,4096]{1,0:T(8,128)(2,1)} %copy-done.3) | copy-start | bytes 6291460
  30.9 0.9 copy-start.8
  45.9 1.3 %copy-start.1 = (bf16[256,4096]{1,0:T(8,128)(2,1)}, bf16[256,4096]{1,0:T(8,128)(2,1)S(1)}, u32[]{:S(2)}) copy-start(bf16[256,4096]{1,0:T(8,128)(2,1)S(1)} %get-tuple-element.34.g_ref) | copy-start | bytes 6291460
  47.3 0.7 copy-start.5
  59.6 32.8 %all-to-all-start.1 = ((bf16[8,256,256]{2,1,0:T(8,128)(2,1)}), bf16[8,256,256]{2,1,0:T(8,128)(2,1)S(1)}, u32[]{:S(2)}, u32[]{:S(2)}) async-start(bf16[8,256,256]{2,1,0:T(8,128)(2,1)} %get-tuple-element.37), calls=%async_computation.1 | async-start | bytes 2097152 | tf_op jit(solution)/shard_map/all_to_all | solution.py:744
  63.2 1.9 %collective-permute-start.5 = (bf16[16,5120]{1,0:T(8,128)(2,1)}, bf16[16,5120]{1,0:T(8,128)(2,1)}, u32[]{:S(2)}, u32[]{:S(2)}) collective-permute-start(bf16[16,5120]{1,0:T(8,128)(2,1)} %copy-done.7), channel_id=1, source_target_pairs={{0,16},{16,0},{32,48},{48,32},{64,80},{80,64},{96,112},{112,96},{1... | collective-permute-start | bytes 491528 | tf_op jit(solution)/shard_map/ppermute | solution.py:734
  65.0 0.9 copy-start.9
  70.1 5.5 %collective-permute-start.6 = (f32[2,64,256]{2,1,0:T(8,128)S(1)}, f32[2,64,256]{2,1,0:T(8,128)S(1)}, u32[]{:S(2)}, u32[]{:S(2)}) collective-permute-start(f32[2,64,256]{2,1,0:T(8,128)S(1)} %get-tuple-element.43), channel_id=1, source_target_pairs={{0,1},{1,0},{2,3},{3,2},{4,5},{5,4},{6,7},{7,6},{8,9},{9,8},{10,11... | collective-permute-start | bytes 393224 | tf_op jit(solution)/shard_map/ppermute | solution.py:752
  71.4 8.5 %collective-permute-start.7 = (f32[2,64,256]{2,1,0:T(8,128)S(1)}, f32[2,64,256]{2,1,0:T(8,128)S(1)}, u32[]{:S(2)}, u32[]{:S(2)}) collective-permute-start(f32[2,64,256]{2,1,0:T(8,128)S(1)} %get-tuple-element.44), channel_id=1, source_target_pairs={{0,2},{1,3},{2,0},{3,1},{4,6},{5,7},{6,4},{7,5},{8,10},{9,11},{10,... | collective-permute-start | bytes 393224 | tf_op jit(solution)/shard_map/ppermute | solution.py:752
  73.8 8.6 %collective-permute-start.8 = (f32[2,64,256]{2,1,0:T(8,128)S(1)}, f32[2,64,256]{2,1,0:T(8,128)S(1)}, u32[]{:S(2)}, u32[]{:S(2)}) collective-permute-start(f32[2,64,256]{2,1,0:T(8,128)S(1)} %get-tuple-element.45), channel_id=1, source_target_pairs={{0,3},{1,2},{2,1},{3,0},{4,7},{5,6},{6,5},{7,4},{8,11},{9,10},{10,... | collective-permute-start | bytes 393224 | tf_op jit(solution)/shard_map/ppermute | solution.py:752
  74.1 23.7 %copy-start.6 = (bf16[256,512]{1,0:T(8,128)(2,1)S(1)}, bf16[256,512]{1,0:T(8,128)(2,1)}, u32[]{:S(2)}) copy-start(bf16[256,512]{1,0:T(8,128)(2,1)} %copy-done.5) | copy-start | bytes 786436
  74.1 23.7 %copy-start.10 = (f32[4096]{0:T(1024)S(1)}, f32[4096]{0:T(1024)}, u32[]{:S(2)}) copy-start(f32[4096]{0:T(1024)} %param.22) | copy-start | bytes 49156
  92.4 5.4 %copy-start.2 = (bf16[256,4096]{1,0:T(8,128)(2,1)S(1)}, bf16[256,4096]{1,0:T(8,128)(2,1)}, u32[]{:S(2)}) copy-start(bf16[256,4096]{1,0:T(8,128)(2,1)} %copy-done.1) | copy-start | bytes 6291460
  94.9 2.9 %collective-permute-start.9 = (bf16[8,256,256]{2,1,0:T(8,128)(2,1)S(1)}, bf16[8,256,256]{2,1,0:T(8,128)(2,1)S(1)}, u32[]{:S(2)}, u32[]{:S(2)}) collective-permute-start(bf16[8,256,256]{2,1,0:T(8,128)(2,1)S(1)} %get-tuple-element.47), channel_id=1, source_target_pairs={{0,16},{16,0},{32,48},{48,32},{64,80},{80,64},{96,112},{112,96},{1... | collective-permute-start | bytes 3145736 | tf_op jit(solution)/shard_map/ppermute | solution.py:756

commit v3 on v2

--- a/solution.py
+++ b/solution.py
@@ -76,7 +76,8 @@
 
 
 def steps_of(step, bias, fading):
-    size = softplus(step.astype(F32) + bias)
+    step = step.astype(F32).T
+    size = softplus(step + bias)
     decay = -size * jnp.exp(fading)
     count = step.shape[0]
     row = lax.broadcasted_iota(jnp.int32, (count, count), 0)
@@ -110,7 +111,7 @@
 ):
     n = pl.program_id(0)
     core = core_ref[0]
-    heads = step_ref.shape[1]
+    heads = step_ref.shape[0]
     per_group = u_ref.shape[0] // 2
     end = slice(BLOCK - 16, BLOCK)
     x_width, b_width = x_ref.shape[1], b_ref.shape[1]
@@ -138,7 +139,7 @@
 
 
 def own_updates(core, x, b, c, step, kernel_x, kernel_b, bias, fading):
-    heads = step.shape[1]
+    heads = step.shape[0]
     groups = b.shape[1] // STATE
     width = x.shape[1] // groups
     blocks = x.shape[1] // WIDE // 2
@@ -184,7 +185,7 @@
     n = pl.program_id(0)
     core = core_ref[0]
     even = core == 0
-    heads = sr_ref.shape[1]
+    heads = sr_ref.shape[0]
     per_group = u_ref.shape[0]
     head8 = slice(0, 8)
     tail8 = slice(8, 16)
@@ -281,7 +282,7 @@
 
 def chip_updates(core, own, x, b, x_recv, b_recv, step_recv, kernel_x, kernel_b, bias, fading):
     u_own, first_weight, closing = own
-    heads = step_recv.shape[1]
+    heads = step_recv.shape[0]
     groups = b.shape[1] // STATE
     width = x.shape[1] // groups
     blocks = x.shape[1] // WIDE // 2
@@ -403,7 +404,7 @@
 ):
     k = pl.program_id(0)
     even = core_ref[0] == 0
-    heads = step_ref.shape[1]
+    heads = step_ref.shape[0]
     half = BLOCK // 2
     steps = pl.num_programs(0)
     blocks = x_ref.shape[1] // WIDE
@@ -478,7 +479,7 @@
 
 
 def within_block(core, x, gate, b, c, step, halo, x_recv, b_recv, c_recv, kernel_x, kernel_b, kernel_c, bias, fading):
-    heads = step.shape[1]
+    heads = step.shape[0]
     width = 4 * WIDE
     steps = x.shape[1] // width
     per_group = steps // (b.shape[1] // STATE)
@@ -495,7 +496,7 @@
                 pl.BlockSpec((BLOCK, width), one),
                 pl.BlockSpec((BLOCK, STATE), group),
                 pl.BlockSpec((BLOCK, STATE), group),
-                pl.BlockSpec((BLOCK, heads), full),
+                whole(step),
                 IN_VMEM,
                 IN_VMEM,
                 IN_VMEM,
@@ -608,12 +609,12 @@
     shape = pltpu.VMEM(chip_start.shape, BF16)
     return pl.pallas_call(
         start_kernel,
-        grid=(chip_start.shape[0] // 2,),
+        grid=(chip_start.shape[0] // 4,),
         in_specs=[
             pl.BlockSpec(memory_space=pltpu.SMEM),
             IN_VMEM,
-            pl.BlockSpec((2, STATE, WIDE), lambda i: (i, 0, 0)),
-            pl.BlockSpec((2, 8, WIDE), lambda i: (i, 0, 0)),
+            pl.BlockSpec((4, STATE, WIDE), lambda i: (i, 0, 0)),
+            pl.BlockSpec((4, 8, WIDE), lambda i: (i, 0, 0)),
             IN_HBM,
         ],
         out_specs=[IN_VMEM, IN_VMEM],
@@ -624,50 +625,82 @@
     )(core, vmem(chip_start), hbm(first_update), hbm(first_decay), hbm(after))
 
 
-def finish_kernel(core_ref, a_ref, g_ref, cc_ref, keep_ref, recv_ref, gain_ref, out_ref, y_ref):
+def carried_rows(n, block, rows, c_conv, state, a_ref, g_ref, width):
+    at = pl.ds(pl.multiple_of(n * width + block * WIDE, WIDE), WIDE)
+    carried = jnp.dot(c_conv, state, preferred_element_type=F32)
+    return a_ref[rows, at].astype(F32) + carried * g_ref[rows, at].astype(F32)
+
+
+def near_kernel(core_ref, a_ref, g_ref, cc_ref, keep_ref, y_ref, sum_ref):
+    n = pl.program_id(0)
+    groups = pl.num_programs(0)
+    per_group = keep_ref.shape[0] // groups
+    width = a_ref.shape[1] // groups
+    everything = slice(None)
+    c_conv = cc_ref[:, lanes(n, STATE)]
+    total = jnp.zeros((BLOCK, 1), F32)
+    for j in range(per_group):
+        at = n * per_group + j
+        block = 2 * j + core_ref[0]
+        y = carried_rows(n, block, everything, c_conv, keep_ref[at], a_ref, g_ref, width)
+        y_ref[:, lanes(at)] = y
+        total = total + jnp.sum(y * y, axis=1, keepdims=True)
+    sum_ref[n] = jnp.broadcast_to(total, sum_ref.shape[1:])
+
+
+def near_rows(core, a, g, cc, keep):
+    tokens, channels = a.shape
+    groups = cc.shape[1] // STATE
+    smem = pl.BlockSpec(memory_space=pltpu.SMEM)
+    return pl.pallas_call(
+        near_kernel,
+        grid=(groups,),
+        in_specs=[smem, IN_VMEM, IN_VMEM, IN_VMEM, IN_VMEM],
+        out_specs=[IN_VMEM, IN_VMEM],
+        out_shape=[pltpu.VMEM((tokens, channels // 2), F32), pltpu.VMEM((groups, tokens, 128), F32)],
+        compiler_params=pltpu.CompilerParams(vmem_limit_bytes=SMALL),
+        cost_estimate=pl.CostEstimate(flops=300_000_000, bytes_accessed=5_000_000, transcendentals=1000),
+        name="near_rows",
+    )(core, vmem(a), vmem(g), vmem(cc), vmem(keep))
+
+
+def finish_kernel(core_ref, a_ref, g_ref, cc_ref, near_ref, sum_ref, recv_ref, gain_ref, out_ref, y_ref):
     core = core_ref[0]
     rows, width = out_ref.shape
     n, r = pl.program_id(0), pl.program_id(1)
     at_rows = pl.ds(pl.multiple_of(r * rows, rows), rows)
-    per_group = keep_ref.shape[0] // pl.num_programs(0)
-    total = jnp.zeros((rows, 1), F32)
-    c_conv = cc_ref[at_rows, pl.ds(pl.multiple_of(n * STATE, STATE), STATE)]
+    per_group = recv_ref.shape[0] // pl.num_programs(0)
+    total = sum_ref[n, at_rows, 0:1]
+    c_conv = cc_ref[at_rows, lanes(n, STATE)]
     for j in range(per_group):
-        for state_ref, parity in ((keep_ref, core), (recv_ref, 1 - core)):
-            block = 2 * j + parity
-            at = pl.ds(pl.multiple_of(n * width + block * WIDE, WIDE), WIDE)
-            carried = jnp.dot(c_conv, state_ref[n * per_group + j], preferred_element_type=F32)
-            y = a_ref[at_rows, at].astype(F32) + carried * g_ref[at_rows, at].astype(F32)
-            y_ref[:, pl.ds(pl.multiple_of(block * WIDE, WIDE), WIDE)] = y
-            total = total + jnp.sum(y * y, axis=1, keepdims=True)
+        block = 2 * j + 1 - core
+        y = carried_rows(n, block, at_rows, c_conv, recv_ref[n * per_group + j], a_ref, g_ref, width)
+        y_ref[:, j * WIDE : (j + 1) * WIDE] = y
+        total = total + jnp.sum(y * y, axis=1, keepdims=True)
     inverse = 1.0 / jnp.sqrt(total / width + epsilon)
-    out_ref[...] = (y_ref[...] * inverse * gain_ref[...]).astype(BF16)
-
-
-def finish(core, a, g, cc, keep, recv, gain):
+    for j in range(per_group):
+        near = near_ref[at_rows, lanes(n * per_group + j)]
+        for y, block in ((near, 2 * j + core), (y_ref[:, j * WIDE : (j + 1) * WIDE], 2 * j + 1 - core)):
+            out_ref[:, lanes(block)] = (y * inverse * gain_ref[:, lanes(block)]).astype(BF16)
+
+
+def finish(core, a, g, cc, near, sums, recv, gain):
     tokens, channels = a.shape
     groups = cc.shape[1] // STATE
     width = channels // groups
-    rows = tokens // 2
+    rows = tokens
+    smem = pl.BlockSpec(memory_space=pltpu.SMEM)
     return pl.pallas_call(
         finish_kernel,
-        grid=(groups, 2),
-        in_specs=[
-            pl.BlockSpec(memory_space=pltpu.SMEM),
-            IN_VMEM,
-            IN_VMEM,
-            IN_VMEM,
-            IN_VMEM,
-            IN_VMEM,
-            pl.BlockSpec((1, width), lambda n, r: (0, n)),
-        ],
+        grid=(groups, 1),
+        in_specs=[smem] + [IN_VMEM] * 6 + [pl.BlockSpec((1, width), lambda n, r: (0, n))],
         out_specs=pl.BlockSpec((rows, width), lambda n, r: (r, n)),
-        scratch_shapes=[pltpu.VMEM((rows, width), F32)],
+        scratch_shapes=[pltpu.VMEM((rows, width // 2), F32)],
         out_shape=jax.ShapeDtypeStruct((tokens, channels), BF16),
         compiler_params=pltpu.CompilerParams(vmem_limit_bytes=SMALL),
-        cost_estimate=pl.CostEstimate(flops=600_000_000, bytes_accessed=9_000_000, transcendentals=1000),
+        cost_estimate=pl.CostEstimate(flops=300_000_000, bytes_accessed=9_000_000, transcendentals=1000),
         name="finish",
-    )(core, vmem(a), vmem(g), vmem(cc), vmem(keep), vmem(recv), gain)
+    )(core, vmem(a), vmem(g), vmem(cc), vmem(near), vmem(sums), vmem(recv), gain)
 
 
 def slots_kernel(owners_ref, rank_ref, state_ref, o0, o1, o2, o3):
@@ -714,7 +747,7 @@
     x = x_input[0]
     b = b_input[0]
     c = output_projection_input[0]
-    step = step_input[0]
+    step = step_input[0].T
     bias = step_bias.reshape(1, -1)
     fading = fading_logarithm.reshape(1, -1)
 
@@ -754,7 +787,9 @@
 
     keep, send = block_starts(core_arg, chip_start, first_update, first_decay, arrived)
     recv = lax.ppermute(send, "ctx", swap)
-    mixer_rows = finish(core_arg, a, g, cc, keep, recv, norm_gain.reshape(1, -1))
+    near, sums = near_rows(core_arg, a, g, cc, keep)
+    recv, near, sums = lax.optimization_barrier((recv, near, sums))
+    mixer_rows = finish(core_arg, a, g, cc, near, sums, recv, norm_gain.reshape(1, -1))
     return (mixer_rows[None], arrived[None, :, None])
 
 

time: 102 us -> 99.3 us (0.974)
    pallas_call x2 -> x3, Pallas kernels: 5.89 us -> 5.24 us  [the longest x1 2.58 us: finish(): pl.pallas_call(finish_kernel, grid=(groups, 1), in_specs=[smem] + [IN_VME...]
    unnamed x27 -> x24, local copies, waits for them, and re-layouts: 6.46 us -> 6.1 us
  transfers between devices with their start and end apart: 12 -> 12, of which waited for: 7 -> 7; matrix products, arithmetic and copies ran while one was open for 4% -> 4% of each run, Pallas kernels for 30% -> 32%
where the time goes in v3:
time: 99.3 us; the launch traced here: 98.8 us
  Pallas kernels  37.9 us (38%)
  waiting for transfers between devices  28.9 us (29%)
  starting transfers between devices  21.6 us (22%)
  local copies, waits for them, and re-layouts  9.67 us (10%)
    pallas_call x1, Pallas kernels, within_block(): pl.pallas_call(within_kernel, grid_spec=pltpu.PrefetchScalarGridSpec(num_...  14.1 us
    all_to_all x1, waiting for transfers between devices, local(): lax.all_to_all(updates, 'ctx', 0, 0, axis_index_groups=same_core, tiled=T...  9.9 us
    all_to_all x1, waiting for transfers between devices, local(): lax.all_to_all(starts, 'ctx', 0, 0, axis_index_groups=same_core, tiled=True)  9.3 us
    pallas_call x1, Pallas kernels, chip_updates(): pl.pallas_call(chip_kernel, grid_spec=pltpu.PrefetchScalarGridSpec(num_sc...  7.72 us
    all_to_all x1, starting transfers between devices, local(): lax.all_to_all(updates, 'ctx', 0, 0, axis_index_groups=same_core, tiled=T...  7.29 us
    unnamed x24, local copies, waits for them, and re-layouts  6.1 us
    ppermute x3, waiting for transfers between devices, local(): piece = lax.ppermute(piece, 'dec', [(i, i ^ d) for i in range(dec_count)])  5.53 us
    pallas_call x1, Pallas kernels, own_updates(): pl.pallas_call(own_kernel, grid_spec=pltpu.PrefetchScalarGridSpec(num_sca...  4.84 us
  transfers between devices with their start and end apart: 12, of which 7 were waited for; matrix products, arithmetic and copies ran while one was open for 4% of the time, Pallas kernels for 32%

profile of v3, /device:TPU:1, one launch (start us, length us, event | category | flops | bytes accessed | tf_op | source)
XLA Modules:
  0.0 98.8 jit_solution(5437945612285289522)
XLA Ops:
  0.6 0.0 copy-start
  0.6 3.3 %collective-permute-start = (bf16[256,4096]{1,0:T(8,128)(2,1)}, bf16[256,4096]{1,0:T(8,128)(2,1)S(1)}, u32[]{:S(2)}, u32[]{:S(2)}) collective-permute-start(bf16[256,4096]{1,0:T(8,128)(2,1)} %bitcast.27), channel_id=1, source_target_pairs={{0,16},{16,0},{32,48},{48,32},{64,80},{80,64},{96,112},{112,96},{1... | collective-permute-start | bytes 6291464 | tf_op jit(solution)/shard_map/ppermute | solution.py:756
  4.0 0.1 collective-permute-start.1
  4.1 0.4 collective-permute-start.2
  4.5 4.8 %own_updates.1 = (f32[8,256,256]{2,1,0:T(8,128)S(1)}, bf16[16,128]{1,0:T(8,128)(2,1)S(1)}, f32[8,64]{1,0:T(8,128)S(1)}, bf16[16,5120]{1,0:T(8,128)(2,1)S(1)}) custom-call(s32[1]{0:T(128)} %bitcast.core_ref, bf16[256,4096]{1,0:T(8,128)(2,1)} %bitcast.28, bf16[256,512]{1,0:T(8,128)(2,1)} %bitcast.33, bf16[256,512]{1,0:T(8,128)(2,1)} %bitcast.38, ...), custom_call_target="tpu_custom_call" | custom-call | flops 300000000 | bytes 10000000 | tf_op jit(solution)/shard_map/own_updates/pallas_call | solution.py:147
  9.3 0.0 collective-permute-done.2.sr_ref
  9.3 1.8 %collective-permute-start.3 = (bf16[16,5120]{1,0:T(8,128)(2,1)S(1)}, bf16[16,5120]{1,0:T(8,128)(2,1)S(1)}, u32[]{:S(2)}, u32[]{:S(2)}) collective-permute-start(bf16[16,5120]{1,0:T(8,128)(2,1)S(1)} %get-tuple-element.36), channel_id=1, source_target_pairs={{16,32},{48,64},{80,96},{112,128},{144,160},{176,192},{208,224},{1... | collective-permute-start | bytes 491528 | tf_op jit(solution)/shard_map/ppermute | solution.py:762
  11.1 0.0 collective-permute-done.1.br_ref.tb_ref
  11.2 0.0 collective-permute-done.xr_ref.tx_ref
  11.2 0.0 copy-start.5
  11.2 7.7 %chip_updates.1 = (bf16[8,272,256]{2,1,0:T(8,128)(2,1)}, bf16[8,256,256]{2,1,0:T(8,128)(2,1)}, f32[8,8,256]{2,1,0:T(8,128)}, f32[8,16,256]{2,1,0:T(8,128)}) custom-call(s32[1]{0:T(128)} %bitcast.core_ref, f32[8,256,256]{2,1,0:T(8,128)S(1)} %get-tuple-element.30.u_own_ref, bf16[16,128]{1,0:T(8,128)(2,1)S(1)} %get-tuple-element.31.first_weight_ref, ...), custom_call_target="tpu_custom_call" | custom-call | flops 300000000 | bytes 10000000 | tf_op jit(solution)/shard_map/chip_updates/pallas_call | solution.py:294
  18.9 0.0 copy-done.5
  18.9 0.0 collective-permute-done.3.halo_ref.he_ref
  18.9 0.0 copy-start.7
  18.9 0.0 copy-start.11
  18.9 0.6 copy-done.7
  19.6 7.3 %all-to-all-start = ((bf16[8,272,256]{2,1,0:T(8,128)(2,1)}), bf16[8,272,256]{2,1,0:T(8,128)(2,1)S(1)}, u32[]{:S(2)}, u32[]{:S(2)}) async-start(bf16[8,272,256]{2,1,0:T(8,128)(2,1)} %get-tuple-element.41), calls=%async_computation | async-start | bytes 2228224 | tf_op jit(solution)/shard_map/all_to_all | solution.py:770
  26.9 0.0 copy-done.11
  26.9 0.1 collective-permute-start.4
  27.0 1.5 %collective-permute-done.4.tc_ref = bf16[256,512]{1,0:T(8,128)(2,1)S(1)} collective-permute-done((bf16[256,512]{1,0:T(8,128)(2,1)S(1)}, bf16[256,512]{1,0:T(8,128)(2,1)S(1)}, u32[]{:S(2)}, u32[]{:S(2)}) %collective-permute-start.4) | collective-permute-done | bytes 262176 | tf_op jit(solution)/shard_map/ppermute | solution.py:766
  28.5 0.0 copy-start.6
  28.5 1.6 %copy-done.6 = bf16[256,4096]{1,0:T(8,128)(2,1)S(1)} copy-done((bf16[256,4096]{1,0:T(8,128)(2,1)S(1)}, bf16[256,4096]{1,0:T(8,128)(2,1)}, u32[]{:S(2)}) %copy-start.6) | copy-done | bytes 2097176
  30.1 0.0 copy-start.8
  30.1 0.9 copy-done.8
  31.0 14.1 %within_block.1 = (bf16[256,4096]{1,0:T(8,128)(2,1)S(1)}, bf16[256,4096]{1,0:T(8,128)(2,1)S(1)}, bf16[256,512]{1,0:T(8,128)(2,1)S(1)}) custom-call(s32[1]{0:T(128)} %bitcast.core_ref, bf16[256,4096]{1,0:T(8,128)(2,1)} %bitcast.31, bf16[256,4096]{1,0:T(8,128)(2,1)} %bitcast.50, bf16[256,512]{1,0:T(8,128)(2,1)} %bitcast.36, bf16[256,512]{1,0:T(8,128)(2,1)} %bitcast.39, ...), custom_call_target="tpu_custom_call" | custom-call | flops 8000000000 | bytes 12000000 | tf_op jit(solution)/shard_map/within_block/pallas_call | solution.py:489
  45.2 0.0 copy-start.1
  45.2 1.3 %copy-done.1 = bf16[256,4096]{1,0:T(8,128)(2,1)} copy-done((bf16[256,4096]{1,0:T(8,128)(2,1)}, bf16[256,4096]{1,0:T(8,128)(2,1)S(1)}, u32[]{:S(2)}) %copy-start.1) | copy-done | bytes 2097176
  46.5 0.0 copy-start.3
  46.5 0.7 copy-done.3
  47.2 9.9 %all-to-all-done.gathered_ref = bf16[8,272,256]{2,1,0:T(8,128)(2,1)S(1)} async-done(((bf16[8,272,256]{2,1,0:T(8,128)(2,1)}), bf16[8,272,256]{2,1,0:T(8,128)(2,1)S(1)}, u32[]{:S(2)}, u32[]{:S(2)}) %all-to-all-start) | async-done | bytes 1114144 | tf_op jit(solution)/shard_map/all_to_all | solution.py:770
  57.1 1.8 %scan_states.1 = (bf16[8,256,256]{2,1,0:T(8,128)(2,1)}, f32[256,256]{1,0:T(8,128)S(1)}) custom-call(bf16[8,272,256]{2,1,0:T(8,128)(2,1)S(1)} %all-to-all-done.gathered_ref, bf16[256,512]{1,0:T(8,128)(2,1)} %copy-done.3), custom_call_target="tpu_custom_call" | custom-call | flops 20000000 | bytes 2500000 | tf_op jit(solution)/shard_map/scan_states/pallas_call | solution.py:578
  58.9 3.6 %all-to-all-start.1 = ((bf16[8,256,256]{2,1,0:T(8,128)(2,1)}), bf16[8,256,256]{2,1,0:T(8,128)(2,1)S(1)}, u32[]{:S(2)}, u32[]{:S(2)}) async-start(bf16[8,256,256]{2,1,0:T(8,128)(2,1)} %get-tuple-element.42), calls=%async_computation.1 | async-start | bytes 2097152 | tf_op jit(solution)/shard_map/all_to_all | solution.py:777
  62.4 0.5 collective-permute-start.5
  62.9 0.0 copy-done
  62.9 0.1 fusion.owners_ref
  63.0 1.3 %collective-permute-done.5.ho_ref = bf16[16,5120]{1,0:T(8,128)(2,1)} collective-permute-done((bf16[16,5120]{1,0:T(8,128)(2,1)}, bf16[16,5120]{1,0:T(8,128)(2,1)}, u32[]{:S(2)}, u32[]{:S(2)}) %collective-permute-start.5) | collective-permute-done | bytes 163872 | tf_op jit(solution)/shard_map/ppermute | solution.py:767
  64.3 0.0 copy-start.9
  64.3 0.9 copy-done.9
  65.2 2.9 %whole_first.1.first_ref = bf16[8,256,256]{2,1,0:T(8,128)(2,1)} custom-call(s32[1]{0:T(128)} %bitcast.core_ref, bf16[8,256,256]{2,1,0:T(8,128)(2,1)} %get-tuple-element.43.first_ref, f32[8,16,256]{2,1,0:T(8,128)} %get-tuple-element.44.edge_ref, bf16[16,5120]{1,0:T(8,128)(2,1)S(1)} %copy-done.9, bf16[16,5120]{1,0:T(8,128)(2,1)} %collective-permute-done.5.ho_ref, ...), custom_call_target="tpu_custom_call" | custom-call | flops 30000000 | bytes 3000000 | tf_op jit(solution)/shard_map/whole_first/pallas_call | solution.py:379
  68.1 1.3 %final_slots.1 = (f32[2,64,256]{2,1,0:T(8,128)S(1)}, f32[2,64,256]{2,1,0:T(8,128)S(1)}, f32[2,64,256]{2,1,0:T(8,128)S(1)}, f32[2,64,256]{2,1,0:T(8,128)S(1)}) custom-call(s32[4]{0:T(128)S(1)} %fusion.owners_ref, s32[1]{0:T(128)} %bitcast.11.rank_ref, f32[256,256]{1,0:T(8,128)S(1)} %get-tuple-element.46.state_ref), custom_call_target="tpu_custom_call" | custom-call | tf_op jit(solution)/shard_map/final_slots/pallas_call | solution.py:727
  69.3 1.3 %collective-permute-start.6 = (f32[2,64,256]{2,1,0:T(8,128)S(1)}, f32[2,64,256]{2,1,0:T(8,128)S(1)}, u32[]{:S(2)}, u32[]{:S(2)}) collective-permute-start(f32[2,64,256]{2,1,0:T(8,128)S(1)} %get-tuple-element.48), channel_id=1, source_target_pairs={{0,1},{1,0},{2,3},{3,2},{4,5},{5,4},{6,7},{7,6},{8,9},{9,8},{10,11... | collective-permute-start | bytes 393224 | tf_op jit(solution)/shard_map/ppermute | solution.py:785
  70.6 2.4 %collective-permute-start.7 = (f32[2,64,256]{2,1,0:T(8,128)S(1)}, f32[2,64,256]{2,1,0:T(8,128)S(1)}, u32[]{:S(2)}, u32[]{:S(2)}) collective-permute-start(f32[2,64,256]{2,1,0:T(8,128)S(1)} %get-tuple-element.49), channel_id=1, source_target_pairs={{0,2},{1,3},{2,0},{3,1},{4,6},{5,7},{6,4},{7,5},{8,10},{9,11},{10,... | collective-permute-start | bytes 393224 | tf_op jit(solution)/shard_map/ppermute | solution.py:785
  73.1 0.2 collective-permute-start.8
  73.3 0.0 copy-start.4
  73.3 0.8 broadcast_in_dim.22
  74.1 0.7 bitcast_dynamic-update-slice_fusion.3
  74.8 0.0 collective-permute-done.6
  74.8 0.7 bitcast_dynamic-update-slice_fusion.2
  75.5 3.7 %collective-permute-done.7 = f32[2,64,256]{2,1,0:T(8,128)S(1)} collective-permute-done((f32[2,64,256]{2,1,0:T(8,128)S(1)}, f32[2,64,256]{2,1,0:T(8,128)S(1)}, u32[]{:S(2)}, u32[]{:S(2)}) %collective-permute-start.7) | collective-permute-done | bytes 131104 | tf_op jit(solution)/shard_map/ppermute | solution.py:785
  79.2 0.7 bitcast_dynamic-update-slice_fusion.1
  79.8 1.8 %collective-permute-done.8 = f32[2,64,256]{2,1,0:T(8,128)S(1)} collective-permute-done((f32[2,64,256]{2,1,0:T(8,128)S(1)}, f32[2,64,256]{2,1,0:T(8,128)S(1)}, u32[]{:S(2)}, u32[]{:S(2)}) %collective-permute-start.8) | collective-permute-done | bytes 131104 | tf_op jit(solution)/shard_map/ppermute | solution.py:785
  81.7 0.7 bitcast_dynamic-update-slice_fusion._
  82.3 9.3 %all-to-all-done.1.start_ref = bf16[8,256,256]{2,1,0:T(8,128)(2,1)S(1)} async-done(((bf16[8,256,256]{2,1,0:T(8,128)(2,1)}), bf16[8,256,256]{2,1,0:T(8,128)(2,1)S(1)}, u32[]{:S(2)}, u32[]{:S(2)}) %all-to-all-start.1) | async-done | bytes 1048608 | tf_op jit(solution)/shard_map/all_to_all | solution.py:777
  91.6 0.0 copy-start.2
  91.6 1.7 %block_starts.1 = (bf16[8,256,256]{2,1,0:T(8,128)(2,1)S(1)}, bf16[8,256,256]{2,1,0:T(8,128)(2,1)S(1)}) custom-call(s32[1]{0:T(128)} %bitcast.core_ref, bf16[8,256,256]{2,1,0:T(8,128)(2,1)S(1)} %all-to-all-done.1.start_ref, bf16[8,256,256]{2,1,0:T(8,128)(2,1)} %whole_first.1.first_ref, f32[8,8,256]{2,1,0:T(8,128)} %get-tuple-element.45.decay_ref, ...), custom_call_target="tpu_custom_call" | custom-call | flops 2000000 | bytes 4500000 | tf_op jit(solution)/shard_map/block_starts/pallas_call | solution.py:610
  93.4 0.6 collective-permute-start.9
  93.9 0.0 copy-done.4
  93.9 0.0 copy-done.2
  93.9 0.0 copy-start.10
  93.9 0.9 near_rows.1
  94.9 1.3 %collective-permute-done.9.recv_ref = bf16[8,256,256]{2,1,0:T(8,128)(2,1)S(1)} collective-permute-done((bf16[8,256,256]{2,1,0:T(8,128)(2,1)S(1)}, bf16[8,256,256]{2,1,0:T(8,128)(2,1)S(1)}, u32[]{:S(2)}, u32[]{:S(2)}) %collective-permute-start.9) | collective-permute-done | bytes 1048608 | tf_op jit(solution)/shard_map/ppermute | solution.py:789
  96.2 0.0 copy-done.10
  96.2 2.6 %finish.1 = bf16[256,4096]{1,0:T(8,128)(2,1)} custom-call(s32[1]{0:T(128)} %bitcast.core_ref, bf16[256,4096]{1,0:T(8,128)(2,1)S(1)} %get-tuple-element.38.a_ref, bf16[256,4096]{1,0:T(8,128)(2,1)S(1)} %copy-done.2, bf16[256,512]{1,0:T(8,128)(2,1)S(1)} %copy-done.4, f32[256,2048]{1,0:T(8,128)S(1)} %get-tuple-element.55.near_ref, ...), custom_call_target="tpu_custom_call" | custom-call | flops 300000000 | bytes 9000000 | tf_op jit(solution)/shard_map/finish/pallas_call | solution.py:693
Async XLA Ops:
  0.6 62.3 %copy-start = (s32[1,64,1]{1,2,0:T(1,128)S(1)}, s32[1,64,1]{1,2,0:T(1,128)}, u32[]{:S(2)}) copy-start(s32[1,64,1]{1,2,0:T(1,128)} %param.23) | copy-start | bytes 772
  0.6 10.5 %collective-permute-start = (bf16[256,4096]{1,0:T(8,128)(2,1)}, bf16[256,4096]{1,0:T(8,128)(2,1)S(1)}, u32[]{:S(2)}, u32[]{:S(2)}) collective-permute-start(bf16[256,4096]{1,0:T(8,128)(2,1)} %bitcast.27), channel_id=1, source_target_pairs={{0,16},{16,0},{32,48},{48,32},{64,80},{80,64},{96,112},{112,96},{1... | collective-permute-start | bytes 6291464 | tf_op jit(solution)/shard_map/ppermute | solution.py:756
  4.0 7.2 %collective-permute-start.1 = (bf16[256,512]{1,0:T(8,128)(2,1)}, bf16[256,512]{1,0:T(8,128)(2,1)S(1)}, u32[]{:S(2)}, u32[]{:S(2)}) collective-permute-start(bf16[256,512]{1,0:T(8,128)(2,1)} %bitcast.32), channel_id=1, source_target_pairs={{0,16},{16,0},{32,48},{48,32},{64,80},{80,64},{96,112},{112,96},{1... | collective-permute-start | bytes 786440 | tf_op jit(solution)/shard_map/ppermute | solution.py:757
  4.1 5.3 %collective-permute-start.2 = (bf16[64,256]{1,0:T(8,128)(2,1)}, bf16[64,256]{1,0:T(8,128)(2,1)S(1)}, u32[]{:S(2)}, u32[]{:S(2)}) collective-permute-start(bf16[64,256]{1,0:T(8,128)(2,1)} %bitcast.41), channel_id=1, source_target_pairs={{0,16},{16,0},{32,48},{48,32},{64,80},{80,64},{96,112},{112,96},{1... | collective-permute-start | bytes 98312 | tf_op jit(solution)/shard_map/ppermute | solution.py:758
  9.3 9.6 %collective-permute-start.3 = (bf16[16,5120]{1,0:T(8,128)(2,1)S(1)}, bf16[16,5120]{1,0:T(8,128)(2,1)S(1)}, u32[]{:S(2)}, u32[]{:S(2)}) collective-permute-start(bf16[16,5120]{1,0:T(8,128)(2,1)S(1)} %get-tuple-element.36), channel_id=1, source_target_pairs={{16,32},{48,64},{80,96},{112,128},{144,160},{176,192},{208,224},{1... | collective-permute-start | bytes 491528 | tf_op jit(solution)/shard_map/ppermute | solution.py:762
  11.2 7.7 %copy-start.5 = (bf16[256,4096]{1,0:T(8,128)(2,1)}, bf16[256,4096]{1,0:T(8,128)(2,1)S(1)}, u32[]{:S(2)}) copy-start(bf16[256,4096]{1,0:T(8,128)(2,1)S(1)} %collective-permute-done.xr_ref.tx_ref) | copy-start | bytes 6291460
  18.9 0.7 copy-start.7
  18.9 7.9 %copy-start.11 = (bf16[1,256,512]{2,1,0:T(8,128)(2,1)S(1)}, bf16[1,256,512]{2,1,0:T(8,128)(2,1)}, u32[]{:S(2)}) copy-start(bf16[1,256,512]{2,1,0:T(8,128)(2,1)} %param.14) | copy-start | bytes 786436
  19.6 37.5 %all-to-all-start = ((bf16[8,272,256]{2,1,0:T(8,128)(2,1)}), bf16[8,272,256]{2,1,0:T(8,128)(2,1)S(1)}, u32[]{:S(2)}, u32[]{:S(2)}) async-start(bf16[8,272,256]{2,1,0:T(8,128)(2,1)} %get-tuple-element.41), calls=%async_computation | async-start | bytes 2228224 | tf_op jit(solution)/shard_map/all_to_all | solution.py:770
  26.9 1.6 %collective-permute-start.4 = (bf16[256,512]{1,0:T(8,128)(2,1)S(1)}, bf16[256,512]{1,0:T(8,128)(2,1)S(1)}, u32[]{:S(2)}, u32[]{:S(2)}) collective-permute-start(bf16[256,512]{1,0:T(8,128)(2,1)S(1)} %bitcast.40), channel_id=1, source_target_pairs={{0,16},{16,0},{32,48},{48,32},{64,80},{80,64},{96,112},{112,96},{1... | collective-permute-start | bytes 786440 | tf_op jit(solution)/shard_map/ppermute | solution.py:766
  28.5 1.6 %copy-start.6 = (bf16[256,4096]{1,0:T(8,128)(2,1)S(1)}, bf16[256,4096]{1,0:T(8,128)(2,1)}, u32[]{:S(2)}) copy-start(bf16[256,4096]{1,0:T(8,128)(2,1)} %copy-done.5) | copy-start | bytes 6291460
  30.1 0.9 copy-start.8
  45.2 1.3 %copy-start.1 = (bf16[256,4096]{1,0:T(8,128)(2,1)}, bf16[256,4096]{1,0:T(8,128)(2,1)S(1)}, u32[]{:S(2)}) copy-start(bf16[256,4096]{1,0:T(8,128)(2,1)S(1)} %get-tuple-element.39.g_ref) | copy-start | bytes 6291460
  46.5 0.7 copy-start.3
  58.9 32.8 %all-to-all-start.1 = ((bf16[8,256,256]{2,1,0:T(8,128)(2,1)}), bf16[8,256,256]{2,1,0:T(8,128)(2,1)S(1)}, u32[]{:S(2)}, u32[]{:S(2)}) async-start(bf16[8,256,256]{2,1,0:T(8,128)(2,1)} %get-tuple-element.42), calls=%async_computation.1 | async-start | bytes 2097152 | tf_op jit(solution)/shard_map/all_to_all | solution.py:777
  62.4 1.9 %collective-permute-start.5 = (bf16[16,5120]{1,0:T(8,128)(2,1)}, bf16[16,5120]{1,0:T(8,128)(2,1)}, u32[]{:S(2)}, u32[]{:S(2)}) collective-permute-start(bf16[16,5120]{1,0:T(8,128)(2,1)} %copy-done.7), channel_id=1, source_target_pairs={{0,16},{16,0},{32,48},{48,32},{64,80},{80,64},{96,112},{112,96},{1... | collective-permute-start | bytes 491528 | tf_op jit(solution)/shard_map/ppermute | solution.py:767
  64.3 0.9 copy-start.9
  69.3 5.5 %collective-permute-start.6 = (f32[2,64,256]{2,1,0:T(8,128)S(1)}, f32[2,64,256]{2,1,0:T(8,128)S(1)}, u32[]{:S(2)}, u32[]{:S(2)}) collective-permute-start(f32[2,64,256]{2,1,0:T(8,128)S(1)} %get-tuple-element.48), channel_id=1, source_target_pairs={{0,1},{1,0},{2,3},{3,2},{4,5},{5,4},{6,7},{7,6},{8,9},{9,8},{10,11... | collective-permute-start | bytes 393224 | tf_op jit(solution)/shard_map/ppermute | solution.py:785
  70.6 8.5 %collective-permute-start.7 = (f32[2,64,256]{2,1,0:T(8,128)S(1)}, f32[2,64,256]{2,1,0:T(8,128)S(1)}, u32[]{:S(2)}, u32[]{:S(2)}) collective-permute-start(f32[2,64,256]{2,1,0:T(8,128)S(1)} %get-tuple-element.49), channel_id=1, source_target_pairs={{0,2},{1,3},{2,0},{3,1},{4,6},{5,7},{6,4},{7,5},{8,10},{9,11},{10,... | collective-permute-start | bytes 393224 | tf_op jit(solution)/shard_map/ppermute | solution.py:785
  73.1 8.6 %collective-permute-start.8 = (f32[2,64,256]{2,1,0:T(8,128)S(1)}, f32[2,64,256]{2,1,0:T(8,128)S(1)}, u32[]{:S(2)}, u32[]{:S(2)}) collective-permute-start(f32[2,64,256]{2,1,0:T(8,128)S(1)} %get-tuple-element.50), channel_id=1, source_target_pairs={{0,3},{1,2},{2,1},{3,0},{4,7},{5,6},{6,5},{7,4},{8,11},{9,10},{10,... | collective-permute-start | bytes 393224 | tf_op jit(solution)/shard_map/ppermute | solution.py:785
  73.3 20.6 %copy-start.4 = (bf16[256,512]{1,0:T(8,128)(2,1)S(1)}, bf16[256,512]{1,0:T(8,128)(2,1)}, u32[]{:S(2)}) copy-start(bf16[256,512]{1,0:T(8,128)(2,1)} %copy-done.3) | copy-start | bytes 786436
  91.6 2.3 %copy-start.2 = (bf16[256,4096]{1,0:T(8,128)(2,1)S(1)}, bf16[256,4096]{1,0:T(8,128)(2,1)}, u32[]{:S(2)}) copy-start(bf16[256,4096]{1,0:T(8,128)(2,1)} %copy-done.1) | copy-start | bytes 6291460
  93.4 2.9 %collective-permute-start.9 = (bf16[8,256,256]{2,1,0:T(8,128)(2,1)S(1)}, bf16[8,256,256]{2,1,0:T(8,128)(2,1)S(1)}, u32[]{:S(2)}, u32[]{:S(2)}) collective-permute-start(bf16[8,256,256]{2,1,0:T(8,128)(2,1)S(1)} %get-tuple-element.51), channel_id=1, source_target_pairs={{0,16},{16,0},{32,48},{48,32},{64,80},{80,64},{96,112},{112,96},{1... | collective-permute-start | bytes 3145736 | tf_op jit(solution)/shard_map/ppermute | solution.py:789
  93.9 2.3 %copy-start.10 = (f32[4096]{0:T(1024)S(1)}, f32[4096]{0:T(1024)}, u32[]{:S(2)}) copy-start(f32[4096]{0:T(1024)} %param.22) | copy-start | bytes 49156

commit v4 on v3

--- a/solution.py
+++ b/solution.py
@@ -384,8 +384,8 @@
             in_specs=[
                 pl.BlockSpec((per_group, STATE, WIDE), out),
                 pl.BlockSpec((per_group, 16, WIDE), out),
-                IN_VMEM,
-                IN_VMEM,
+                whole(halo_even),
+                whole(halo_odd),
                 pl.BlockSpec((4, width), one),
                 pl.BlockSpec((4, STATE), one),
             ],
@@ -395,7 +395,7 @@
         compiler_params=pltpu.CompilerParams(vmem_limit_bytes=SMALL),
         cost_estimate=pl.CostEstimate(flops=30_000_000, bytes_accessed=3_000_000, transcendentals=10_000),
         name="whole_first",
-    )(core, hbm(first), hbm(edge), vmem(halo_even), vmem(halo_odd), hbm(kernel_x), hbm(kernel_b))
+    )(core, hbm(first), hbm(edge), hbm(halo_even), hbm(halo_odd), hbm(kernel_x), hbm(kernel_b))
 
 
 def within_kernel(
@@ -409,11 +409,10 @@
     steps = pl.num_programs(0)
     blocks = x_ref.shape[1] // WIDE
     group = k // (steps // 2)
-    end = slice(BLOCK - 16, BLOCK)
 
     def prior(halo_at, tail_ref, at):
         halo = halo_ref[:, lanes(halo_at)].astype(F32)
-        return jnp.where(even, halo, tail_ref[end, lanes(at)].astype(F32))[8:]
+        return jnp.where(even, halo, tail_ref[:, lanes(at)].astype(F32))[8:]
 
     @pl.when(k == 0)
     def _():
@@ -484,6 +483,7 @@
     steps = x.shape[1] // width
     per_group = steps // (b.shape[1] // STATE)
     full = lambda k, s: (0, 0)
+    end = BLOCK // 16 - 1
     group = lambda k, s: (0, k // per_group)
     one = lambda k, s: (0, k)
     return pl.pallas_call(
@@ -497,10 +497,8 @@
                 pl.BlockSpec((BLOCK, STATE), group),
                 pl.BlockSpec((BLOCK, STATE), group),
                 whole(step),
-                IN_VMEM,
-                IN_VMEM,
-                IN_VMEM,
-                IN_VMEM,
+                whole(halo),
+                *[pl.BlockSpec((16, v.shape[1]), lambda k, s: (end, 0)) for v in (x_recv, b_recv, c_recv)],
                 pl.BlockSpec((4, width), one),
                 pl.BlockSpec((4, STATE), group),
                 pl.BlockSpec((4, STATE), group),
@@ -530,8 +528,8 @@
         cost_estimate=pl.CostEstimate(flops=8_000_000_000, bytes_accessed=12_000_000, transcendentals=6_000_000),
         name="within_block",
     )(
-        core, hbm(x), hbm(gate), hbm(b), hbm(c), hbm(step), vmem(halo), vmem(x_recv), vmem(b_recv),
-        vmem(c_recv), hbm(kernel_x), hbm(kernel_b), hbm(kernel_c), hbm(bias), hbm(fading),
+        core, hbm(x), hbm(gate), hbm(b), hbm(c), hbm(step), hbm(halo), hbm(x_recv), hbm(b_recv),
+        hbm(c_recv), hbm(kernel_x), hbm(kernel_b), hbm(kernel_c), hbm(bias), hbm(fading),
     )
 
 

time: 99.3 us -> 98.6 us (level)
  local copies, waits for them, and re-layouts: 9.67 us -> 6.29 us
  waiting for transfers between devices: 28.9 us -> 30.7 us
    unnamed x24 -> x20, local copies, waits for them, and re-layouts: 6.1 us -> 2.73 us
  transfers between devices with their start and end apart: 12 -> 12, of which waited for: 7 -> 7; matrix products, arithmetic and copies ran while one was open for 4% -> 4% of each run, Pallas kernels for 32% -> 33%
where the time goes in v4:
time: 98.6 us; the launch traced here: 98.2 us
  Pallas kernels  38 us (39%)
  waiting for transfers between devices  30.7 us (31%)
  starting transfers between devices  22.4 us (23%)
  local copies, waits for them, and re-layouts  6.29 us (6%)
    pallas_call x1, Pallas kernels, within_block(): pl.pallas_call(within_kernel, grid_spec=pltpu.PrefetchScalarGridSpec(num_...  14.4 us
    all_to_all x1, waiting for transfers between devices, local(): lax.all_to_all(updates, 'ctx', 0, 0, axis_index_groups=same_core, tiled=T...  10.7 us
    all_to_all x1, waiting for transfers between devices, local(): lax.all_to_all(starts, 'ctx', 0, 0, axis_index_groups=same_core, tiled=True)  10.3 us
    pallas_call x1, Pallas kernels, chip_updates(): pl.pallas_call(chip_kernel, grid_spec=pltpu.PrefetchScalarGridSpec(num_sc...  7.68 us
    all_to_all x1, starting transfers between devices, local(): lax.all_to_all(updates, 'ctx', 0, 0, axis_index_groups=same_core, tiled=T...  7.43 us
    ppermute x3, waiting for transfers between devices, local(): piece = lax.ppermute(piece, 'dec', [(i, i ^ d) for i in range(dec_count)])  5.56 us
    pallas_call x1, Pallas kernels, own_updates(): pl.pallas_call(own_kernel, grid_spec=pltpu.PrefetchScalarGridSpec(num_sca...  4.84 us
    ppermute x3, starting transfers between devices, local(): piece = lax.ppermute(piece, 'dec', [(i, i ^ d) for i in range(dec_count)])  3.95 us
  transfers between devices with their start and end apart: 12, of which 7 were waited for; matrix products, arithmetic and copies ran while one was open for 4% of the time, Pallas kernels for 33%

profile of v4, /device:TPU:1, one launch (start us, length us, event | category | flops | bytes accessed | tf_op | source)
XLA Modules:
  0.0 98.2 jit_solution(5701986033001562035)
XLA Ops:
  0.6 0.0 copy-start
  0.6 3.3 %collective-permute-start = (bf16[256,4096]{1,0:T(8,128)(2,1)}, bf16[256,4096]{1,0:T(8,128)(2,1)S(1)}, u32[]{:S(2)}, u32[]{:S(2)}) collective-permute-start(bf16[256,4096]{1,0:T(8,128)(2,1)} %bitcast.27), channel_id=1, source_target_pairs={{0,16},{16,0},{32,48},{48,32},{64,80},{80,64},{96,112},{112,96},{1... | collective-permute-start | bytes 6291464 | tf_op jit(solution)/shard_map/ppermute | solution.py:754
  4.0 0.1 collective-permute-start.1
  4.1 0.4 collective-permute-start.2
  4.5 4.8 %own_updates.1 = (f32[8,256,256]{2,1,0:T(8,128)S(1)}, bf16[16,128]{1,0:T(8,128)(2,1)S(1)}, f32[8,64]{1,0:T(8,128)S(1)}, bf16[16,5120]{1,0:T(8,128)(2,1)S(1)}) custom-call(s32[1]{0:T(128)} %bitcast.core_ref, bf16[256,4096]{1,0:T(8,128)(2,1)} %bitcast.28, bf16[256,512]{1,0:T(8,128)(2,1)} %bitcast.33, bf16[256,512]{1,0:T(8,128)(2,1)} %bitcast.38, ...), custom_call_target="tpu_custom_call" | custom-call | flops 300000000 | bytes 10000000 | tf_op jit(solution)/shard_map/own_updates/pallas_call | solution.py:147
  9.3 0.0 collective-permute-done.2.sr_ref
  9.3 2.5 %collective-permute-start.3 = (bf16[16,5120]{1,0:T(8,128)(2,1)S(1)}, bf16[16,5120]{1,0:T(8,128)(2,1)}, u32[]{:S(2)}, u32[]{:S(2)}) collective-permute-start(bf16[16,5120]{1,0:T(8,128)(2,1)S(1)} %get-tuple-element.36), channel_id=1, source_target_pairs={{16,32},{48,64},{80,96},{112,128},{144,160},{176,192},{208,224},{1... | collective-permute-start | bytes 491528 | tf_op jit(solution)/shard_map/ppermute | solution.py:760
  11.8 0.0 collective-permute-done.1.br_ref.tb_ref
  11.8 0.0 copy-start.6
  11.8 0.0 collective-permute-done.xr_ref.tx_ref
  11.8 0.0 copy-start.5
  11.8 7.7 %chip_updates.1 = (bf16[8,272,256]{2,1,0:T(8,128)(2,1)}, bf16[8,256,256]{2,1,0:T(8,128)(2,1)}, f32[8,8,256]{2,1,0:T(8,128)}, f32[8,16,256]{2,1,0:T(8,128)}) custom-call(s32[1]{0:T(128)} %bitcast.core_ref, f32[8,256,256]{2,1,0:T(8,128)S(1)} %get-tuple-element.30.u_own_ref, bf16[16,128]{1,0:T(8,128)(2,1)S(1)} %get-tuple-element.31.first_weight_ref, ...), custom_call_target="tpu_custom_call" | custom-call | flops 300000000 | bytes 10000000 | tf_op jit(solution)/shard_map/chip_updates/pallas_call | solution.py:294
  19.5 0.0 copy-done.6
  19.5 0.0 copy-done.5
  19.5 0.0 collective-permute-done.3.halo_ref.he_ref
  19.5 0.0 copy-start.8
  19.5 7.4 %all-to-all-start = ((bf16[8,272,256]{2,1,0:T(8,128)(2,1)}), bf16[8,272,256]{2,1,0:T(8,128)(2,1)S(1)}, u32[]{:S(2)}, u32[]{:S(2)}) async-start(bf16[8,272,256]{2,1,0:T(8,128)(2,1)} %get-tuple-element.41), calls=%async_computation | async-start | bytes 2228224 | tf_op jit(solution)/shard_map/all_to_all | solution.py:768
  27.0 0.0 copy-done.8
  27.0 0.1 collective-permute-start.4
  27.1 1.5 %collective-permute-done.4.tc_ref = bf16[256,512]{1,0:T(8,128)(2,1)S(1)} collective-permute-done((bf16[256,512]{1,0:T(8,128)(2,1)S(1)}, bf16[256,512]{1,0:T(8,128)(2,1)S(1)}, u32[]{:S(2)}, u32[]{:S(2)}) %collective-permute-start.4) | collective-permute-done | bytes 262176 | tf_op jit(solution)/shard_map/ppermute | solution.py:764
  28.6 0.0 copy-start.9
  28.6 0.7 copy-done.9
  29.3 14.4 %within_block.1 = (bf16[256,4096]{1,0:T(8,128)(2,1)S(1)}, bf16[256,4096]{1,0:T(8,128)(2,1)S(1)}, bf16[256,512]{1,0:T(8,128)(2,1)S(1)}) custom-call(s32[1]{0:T(128)} %bitcast.core_ref, bf16[256,4096]{1,0:T(8,128)(2,1)} %bitcast.31, bf16[256,4096]{1,0:T(8,128)(2,1)} %bitcast.50, bf16[256,512]{1,0:T(8,128)(2,1)} %bitcast.36, bf16[256,512]{1,0:T(8,128)(2,1)} %bitcast.39, ...), custom_call_target="tpu_custom_call" | custom-call | flops 8000000000 | bytes 12000000 | tf_op jit(solution)/shard_map/within_block/pallas_call | solution.py:489
  43.7 0.0 copy-start.1
  43.7 1.3 %copy-done.1 = bf16[256,4096]{1,0:T(8,128)(2,1)} copy-done((bf16[256,4096]{1,0:T(8,128)(2,1)}, bf16[256,4096]{1,0:T(8,128)(2,1)S(1)}, u32[]{:S(2)}) %copy-start.1) | copy-done | bytes 2097176
  45.0 0.0 copy-start.3
  45.0 0.7 copy-done.3
  45.7 10.7 %all-to-all-done.gathered_ref = bf16[8,272,256]{2,1,0:T(8,128)(2,1)S(1)} async-done(((bf16[8,272,256]{2,1,0:T(8,128)(2,1)}), bf16[8,272,256]{2,1,0:T(8,128)(2,1)S(1)}, u32[]{:S(2)}, u32[]{:S(2)}) %all-to-all-start) | async-done | bytes 1114144 | tf_op jit(solution)/shard_map/all_to_all | solution.py:768
  56.4 1.8 %scan_states.1 = (bf16[8,256,256]{2,1,0:T(8,128)(2,1)}, f32[256,256]{1,0:T(8,128)S(1)}) custom-call(bf16[8,272,256]{2,1,0:T(8,128)(2,1)S(1)} %all-to-all-done.gathered_ref, bf16[256,512]{1,0:T(8,128)(2,1)} %copy-done.3), custom_call_target="tpu_custom_call" | custom-call | flops 20000000 | bytes 2500000 | tf_op jit(solution)/shard_map/scan_states/pallas_call | solution.py:576
  58.2 3.6 %all-to-all-start.1 = ((bf16[8,256,256]{2,1,0:T(8,128)(2,1)}), bf16[8,256,256]{2,1,0:T(8,128)(2,1)S(1)}, u32[]{:S(2)}, u32[]{:S(2)}) async-start(bf16[8,256,256]{2,1,0:T(8,128)(2,1)} %get-tuple-element.42), calls=%async_computation.1 | async-start | bytes 2097152 | tf_op jit(solution)/shard_map/all_to_all | solution.py:775
  61.8 0.5 collective-permute-start.5
  62.3 0.0 copy-done
  62.3 0.1 fusion.owners_ref
  62.3 1.3 %collective-permute-done.5.ho_ref = bf16[16,5120]{1,0:T(8,128)(2,1)} collective-permute-done((bf16[16,5120]{1,0:T(8,128)(2,1)}, bf16[16,5120]{1,0:T(8,128)(2,1)}, u32[]{:S(2)}, u32[]{:S(2)}) %collective-permute-start.5) | collective-permute-done | bytes 163872 | tf_op jit(solution)/shard_map/ppermute | solution.py:765
  63.6 2.8 %whole_first.1.first_ref = bf16[8,256,256]{2,1,0:T(8,128)(2,1)} custom-call(s32[1]{0:T(128)} %bitcast.core_ref, bf16[8,256,256]{2,1,0:T(8,128)(2,1)} %get-tuple-element.43.first_ref, f32[8,16,256]{2,1,0:T(8,128)} %get-tuple-element.44.edge_ref, bf16[16,5120]{1,0:T(8,128)(2,1)} %collective-permute-done.3.halo_ref.he_ref, ...), custom_call_target="tpu_custom_call" | custom-call | flops 30000000 | bytes 3000000 | tf_op jit(solution)/shard_map/whole_first/pallas_call | solution.py:379
  66.4 1.3 %final_slots.1 = (f32[2,64,256]{2,1,0:T(8,128)S(1)}, f32[2,64,256]{2,1,0:T(8,128)S(1)}, f32[2,64,256]{2,1,0:T(8,128)S(1)}, f32[2,64,256]{2,1,0:T(8,128)S(1)}) custom-call(s32[4]{0:T(128)S(1)} %fusion.owners_ref, s32[1]{0:T(128)} %bitcast.11.rank_ref, f32[256,256]{1,0:T(8,128)S(1)} %get-tuple-element.46.state_ref), custom_call_target="tpu_custom_call" | custom-call | tf_op jit(solution)/shard_map/final_slots/pallas_call | solution.py:725
  67.7 1.3 %collective-permute-start.6 = (f32[2,64,256]{2,1,0:T(8,128)S(1)}, f32[2,64,256]{2,1,0:T(8,128)S(1)}, u32[]{:S(2)}, u32[]{:S(2)}) collective-permute-start(f32[2,64,256]{2,1,0:T(8,128)S(1)} %get-tuple-element.48), channel_id=1, source_target_pairs={{0,1},{1,0},{2,3},{3,2},{4,5},{5,4},{6,7},{7,6},{8,9},{9,8},{10,11... | collective-permute-start | bytes 393224 | tf_op jit(solution)/shard_map/ppermute | solution.py:783
  69.0 2.5 %collective-permute-start.7 = (f32[2,64,256]{2,1,0:T(8,128)S(1)}, f32[2,64,256]{2,1,0:T(8,128)S(1)}, u32[]{:S(2)}, u32[]{:S(2)}) collective-permute-start(f32[2,64,256]{2,1,0:T(8,128)S(1)} %get-tuple-element.49), channel_id=1, source_target_pairs={{0,2},{1,3},{2,0},{3,1},{4,6},{5,7},{6,4},{7,5},{8,10},{9,11},{10,... | collective-permute-start | bytes 393224 | tf_op jit(solution)/shard_map/ppermute | solution.py:783
  71.5 0.2 collective-permute-start.8
  71.7 0.0 copy-start.4
  71.7 0.8 broadcast_in_dim.22
  72.5 0.7 bitcast_dynamic-update-slice_fusion.3
  73.2 0.0 collective-permute-done.6
  73.2 0.7 bitcast_dynamic-update-slice_fusion.2
  73.8 3.7 %collective-permute-done.7 = f32[2,64,256]{2,1,0:T(8,128)S(1)} collective-permute-done((f32[2,64,256]{2,1,0:T(8,128)S(1)}, f32[2,64,256]{2,1,0:T(8,128)S(1)}, u32[]{:S(2)}, u32[]{:S(2)}) %collective-permute-start.7) | collective-permute-done | bytes 131104 | tf_op jit(solution)/shard_map/ppermute | solution.py:783
  77.6 0.7 bitcast_dynamic-update-slice_fusion.1
  78.2 1.8 %collective-permute-done.8 = f32[2,64,256]{2,1,0:T(8,128)S(1)} collective-permute-done((f32[2,64,256]{2,1,0:T(8,128)S(1)}, f32[2,64,256]{2,1,0:T(8,128)S(1)}, u32[]{:S(2)}, u32[]{:S(2)}) %collective-permute-start.8) | collective-permute-done | bytes 131104 | tf_op jit(solution)/shard_map/ppermute | solution.py:783
  80.0 0.7 bitcast_dynamic-update-slice_fusion._
  80.7 10.3 %all-to-all-done.1.start_ref = bf16[8,256,256]{2,1,0:T(8,128)(2,1)S(1)} async-done(((bf16[8,256,256]{2,1,0:T(8,128)(2,1)}), bf16[8,256,256]{2,1,0:T(8,128)(2,1)S(1)}, u32[]{:S(2)}, u32[]{:S(2)}) %all-to-all-start.1) | async-done | bytes 1048608 | tf_op jit(solution)/shard_map/all_to_all | solution.py:775
  91.0 0.0 copy-start.2
  91.0 1.7 %block_starts.1 = (bf16[8,256,256]{2,1,0:T(8,128)(2,1)S(1)}, bf16[8,256,256]{2,1,0:T(8,128)(2,1)S(1)}) custom-call(s32[1]{0:T(128)} %bitcast.core_ref, bf16[8,256,256]{2,1,0:T(8,128)(2,1)S(1)} %all-to-all-done.1.start_ref, bf16[8,256,256]{2,1,0:T(8,128)(2,1)} %whole_first.1.first_ref, f32[8,8,256]{2,1,0:T(8,128)} %get-tuple-element.45.decay_ref, ...), custom_call_target="tpu_custom_call" | custom-call | flops 2000000 | bytes 4500000 | tf_op jit(solution)/shard_map/block_starts/pallas_call | solution.py:608
  92.7 0.6 collective-permute-start.9
  93.3 0.0 copy-done.4
  93.3 0.0 copy-done.2
  93.3 0.0 copy-start.7
  93.3 0.9 near_rows.1
  94.3 1.3 %collective-permute-done.9.recv_ref = bf16[8,256,256]{2,1,0:T(8,128)(2,1)S(1)} collective-permute-done((bf16[8,256,256]{2,1,0:T(8,128)(2,1)S(1)}, bf16[8,256,256]{2,1,0:T(8,128)(2,1)S(1)}, u32[]{:S(2)}, u32[]{:S(2)}) %collective-permute-start.9) | collective-permute-done | bytes 1048608 | tf_op jit(solution)/shard_map/ppermute | solution.py:787
  95.6 0.0 copy-done.7
  95.6 2.6 %finish.1 = bf16[256,4096]{1,0:T(8,128)(2,1)} custom-call(s32[1]{0:T(128)} %bitcast.core_ref, bf16[256,4096]{1,0:T(8,128)(2,1)S(1)} %get-tuple-element.38.a_ref, bf16[256,4096]{1,0:T(8,128)(2,1)S(1)} %copy-done.2, bf16[256,512]{1,0:T(8,128)(2,1)S(1)} %copy-done.4, f32[256,2048]{1,0:T(8,128)S(1)} %get-tuple-element.55.near_ref, ...), custom_call_target="tpu_custom_call" | custom-call | flops 300000000 | bytes 9000000 | tf_op jit(solution)/shard_map/finish/pallas_call | solution.py:691
Async XLA Ops:
  0.6 61.6 %copy-start = (s32[1,64,1]{1,2,0:T(1,128)S(1)}, s32[1,64,1]{1,2,0:T(1,128)}, u32[]{:S(2)}) copy-start(s32[1,64,1]{1,2,0:T(1,128)} %param.23) | copy-start | bytes 772
  0.6 11.2 %collective-permute-start = (bf16[256,4096]{1,0:T(8,128)(2,1)}, bf16[256,4096]{1,0:T(8,128)(2,1)S(1)}, u32[]{:S(2)}, u32[]{:S(2)}) collective-permute-start(bf16[256,4096]{1,0:T(8,128)(2,1)} %bitcast.27), channel_id=1, source_target_pairs={{0,16},{16,0},{32,48},{48,32},{64,80},{80,64},{96,112},{112,96},{1... | collective-permute-start | bytes 6291464 | tf_op jit(solution)/shard_map/ppermute | solution.py:754
  4.0 7.8 %collective-permute-start.1 = (bf16[256,512]{1,0:T(8,128)(2,1)}, bf16[256,512]{1,0:T(8,128)(2,1)S(1)}, u32[]{:S(2)}, u32[]{:S(2)}) collective-permute-start(bf16[256,512]{1,0:T(8,128)(2,1)} %bitcast.32), channel_id=1, source_target_pairs={{0,16},{16,0},{32,48},{48,32},{64,80},{80,64},{96,112},{112,96},{1... | collective-permute-start | bytes 786440 | tf_op jit(solution)/shard_map/ppermute | solution.py:755
  4.1 5.3 %collective-permute-start.2 = (bf16[64,256]{1,0:T(8,128)(2,1)}, bf16[64,256]{1,0:T(8,128)(2,1)S(1)}, u32[]{:S(2)}, u32[]{:S(2)}) collective-permute-start(bf16[64,256]{1,0:T(8,128)(2,1)} %bitcast.41), channel_id=1, source_target_pairs={{0,16},{16,0},{32,48},{48,32},{64,80},{80,64},{96,112},{112,96},{1... | collective-permute-start | bytes 98312 | tf_op jit(solution)/shard_map/ppermute | solution.py:756
  9.3 10.2 %collective-permute-start.3 = (bf16[16,5120]{1,0:T(8,128)(2,1)S(1)}, bf16[16,5120]{1,0:T(8,128)(2,1)}, u32[]{:S(2)}, u32[]{:S(2)}) collective-permute-start(bf16[16,5120]{1,0:T(8,128)(2,1)S(1)} %get-tuple-element.36), channel_id=1, source_target_pairs={{16,32},{48,64},{80,96},{112,128},{144,160},{176,192},{208,224},{1... | collective-permute-start | bytes 491528 | tf_op jit(solution)/shard_map/ppermute | solution.py:760
  11.8 7.7 %copy-start.6 = (bf16[256,512]{1,0:T(8,128)(2,1)}, bf16[256,512]{1,0:T(8,128)(2,1)S(1)}, u32[]{:S(2)}) copy-start(bf16[256,512]{1,0:T(8,128)(2,1)S(1)} %collective-permute-done.1.br_ref.tb_ref) | copy-start | bytes 786436
  11.8 7.7 %copy-start.5 = (bf16[256,4096]{1,0:T(8,128)(2,1)}, bf16[256,4096]{1,0:T(8,128)(2,1)S(1)}, u32[]{:S(2)}) copy-start(bf16[256,4096]{1,0:T(8,128)(2,1)S(1)} %collective-permute-done.xr_ref.tx_ref) | copy-start | bytes 6291460
  19.5 7.4 %copy-start.8 = (bf16[1,256,512]{2,1,0:T(8,128)(2,1)S(1)}, bf16[1,256,512]{2,1,0:T(8,128)(2,1)}, u32[]{:S(2)}) copy-start(bf16[1,256,512]{2,1,0:T(8,128)(2,1)} %param.14) | copy-start | bytes 786436
  19.5 36.9 %all-to-all-start = ((bf16[8,272,256]{2,1,0:T(8,128)(2,1)}), bf16[8,272,256]{2,1,0:T(8,128)(2,1)S(1)}, u32[]{:S(2)}, u32[]{:S(2)}) async-start(bf16[8,272,256]{2,1,0:T(8,128)(2,1)} %get-tuple-element.41), calls=%async_computation | async-start | bytes 2228224 | tf_op jit(solution)/shard_map/all_to_all | solution.py:768
  27.0 1.6 %collective-permute-start.4 = (bf16[256,512]{1,0:T(8,128)(2,1)S(1)}, bf16[256,512]{1,0:T(8,128)(2,1)S(1)}, u32[]{:S(2)}, u32[]{:S(2)}) collective-permute-start(bf16[256,512]{1,0:T(8,128)(2,1)S(1)} %bitcast.40), channel_id=1, source_target_pairs={{0,16},{16,0},{32,48},{48,32},{64,80},{80,64},{96,112},{112,96},{1... | collective-permute-start | bytes 786440 | tf_op jit(solution)/shard_map/ppermute | solution.py:764
  28.6 0.7 copy-start.9
  43.7 1.3 %copy-start.1 = (bf16[256,4096]{1,0:T(8,128)(2,1)}, bf16[256,4096]{1,0:T(8,128)(2,1)S(1)}, u32[]{:S(2)}) copy-start(bf16[256,4096]{1,0:T(8,128)(2,1)S(1)} %get-tuple-element.39.g_ref) | copy-start | bytes 6291460
  45.0 0.7 copy-start.3
  58.2 32.8 %all-to-all-start.1 = ((bf16[8,256,256]{2,1,0:T(8,128)(2,1)}), bf16[8,256,256]{2,1,0:T(8,128)(2,1)S(1)}, u32[]{:S(2)}, u32[]{:S(2)}) async-start(bf16[8,256,256]{2,1,0:T(8,128)(2,1)} %get-tuple-element.42), calls=%async_computation.1 | async-start | bytes 2097152 | tf_op jit(solution)/shard_map/all_to_all | solution.py:775
  61.8 1.9 %collective-permute-start.5 = (bf16[16,5120]{1,0:T(8,128)(2,1)}, bf16[16,5120]{1,0:T(8,128)(2,1)}, u32[]{:S(2)}, u32[]{:S(2)}) collective-permute-start(bf16[16,5120]{1,0:T(8,128)(2,1)} %collective-permute-done.3.halo_ref.he_ref), channel_id=1, source_target_pairs={{0,16},{16,0},{32,48},{48,32},{64,80},{80,64},{96,112},{112,96},{1... | collective-permute-start | bytes 491528 | tf_op jit(solution)/shard_map/ppermute | solution.py:765
  67.7 5.5 %collective-permute-start.6 = (f32[2,64,256]{2,1,0:T(8,128)S(1)}, f32[2,64,256]{2,1,0:T(8,128)S(1)}, u32[]{:S(2)}, u32[]{:S(2)}) collective-permute-start(f32[2,64,256]{2,1,0:T(8,128)S(1)} %get-tuple-element.48), channel_id=1, source_target_pairs={{0,1},{1,0},{2,3},{3,2},{4,5},{5,4},{6,7},{7,6},{8,9},{9,8},{10,11... | collective-permute-start | bytes 393224 | tf_op jit(solution)/shard_map/ppermute | solution.py:783
  69.0 8.6 %collective-permute-start.7 = (f32[2,64,256]{2,1,0:T(8,128)S(1)}, f32[2,64,256]{2,1,0:T(8,128)S(1)}, u32[]{:S(2)}, u32[]{:S(2)}) collective-permute-start(f32[2,64,256]{2,1,0:T(8,128)S(1)} %get-tuple-element.49), channel_id=1, source_target_pairs={{0,2},{1,3},{2,0},{3,1},{4,6},{5,7},{6,4},{7,5},{8,10},{9,11},{10,... | collective-permute-start | bytes 393224 | tf_op jit(solution)/shard_map/ppermute | solution.py:783
  71.5 8.6 %collective-permute-start.8 = (f32[2,64,256]{2,1,0:T(8,128)S(1)}, f32[2,64,256]{2,1,0:T(8,128)S(1)}, u32[]{:S(2)}, u32[]{:S(2)}) collective-permute-start(f32[2,64,256]{2,1,0:T(8,128)S(1)} %get-tuple-element.50), channel_id=1, source_target_pairs={{0,3},{1,2},{2,1},{3,0},{4,7},{5,6},{6,5},{7,4},{8,11},{9,10},{10,... | collective-permute-start | bytes 393224 | tf_op jit(solution)/shard_map/ppermute | solution.py:783
  71.7 21.7 %copy-start.4 = (bf16[256,512]{1,0:T(8,128)(2,1)S(1)}, bf16[256,512]{1,0:T(8,128)(2,1)}, u32[]{:S(2)}) copy-start(bf16[256,512]{1,0:T(8,128)(2,1)} %copy-done.3) | copy-start | bytes 786436
  91.0 2.3 %copy-start.2 = (bf16[256,4096]{1,0:T(8,128)(2,1)S(1)}, bf16[256,4096]{1,0:T(8,128)(2,1)}, u32[]{:S(2)}) copy-start(bf16[256,4096]{1,0:T(8,128)(2,1)} %copy-done.1) | copy-start | bytes 6291460
  92.7 2.9 %collective-permute-start.9 = (bf16[8,256,256]{2,1,0:T(8,128)(2,1)S(1)}, bf16[8,256,256]{2,1,0:T(8,128)(2,1)S(1)}, u32[]{:S(2)}, u32[]{:S(2)}) collective-permute-start(bf16[8,256,256]{2,1,0:T(8,128)(2,1)S(1)} %get-tuple-element.51), channel_id=1, source_target_pairs={{0,16},{16,0},{32,48},{48,32},{64,80},{80,64},{96,112},{112,96},{1... | collective-permute-start | bytes 3145736 | tf_op jit(solution)/shard_map/ppermute | solution.py:787
  93.3 2.3 %copy-start.7 = (f32[4096]{0:T(1024)S(1)}, f32[4096]{0:T(1024)}, u32[]{:S(2)}) copy-start(f32[4096]{0:T(1024)} %param.22) | copy-start | bytes 49156
